TPU v7x, 128 devices: a whole 4x4x4 slice. The times are simulated.
128 devices in a mesh: row: 16 (over y, z), col: 8 (over x, core).
Axes of the slice: x: 4, y: 4, z: 4, core: 2. Of those that a mesh axis runs over, the one named last changes fastest.
Arguments:
- atoms: bfloat16 [16384, 128], P(('row', 'col')), may hold values from -6 to 6
- atom_bias: bfloat16 [4, 16384, 128], P(None, ('row', 'col')), may hold values from -8 to 250
- key_shift: int32 [512], P(('row', 'col')), may hold values from -16 to 16, as said below
- atom_token: int32 [16384], P(('row', 'col')), may hold values from 0 to 2047, as said below
- token_atoms: int32 [2048], P(('row', 'col')), may hold values from 1 to 209, as said below
- token_mask: int32 [2048], P(('row', 'col')), may hold values from 0 to 1, as said below
- pair: bfloat16 [2048, 16, 8, 16, 128], P('row', None, 'col'), may hold values from -45 to 45
- w_atom_qkv: bfloat16 [128, 384], replicated, may hold values from -0.5 to 0.5
- w_atom_out: bfloat16 [128, 128], replicated, may hold values from -0.5 to 0.5
- w_pool: bfloat16 [128, 768], replicated, may hold values from -0.5 to 0.5
- w_token_qkv: bfloat16 [768, 2304], replicated, may hold values from -0.21875 to 0.21875
- w_token_out: bfloat16 [768, 768], replicated, may hold values from -0.21875 to 0.21875
- w_bias: bfloat16 [128, 16], replicated, may hold values from -1 to 1
- w_back: bfloat16 [768, 128], replicated, may hold values from -0.21875 to 0.21875
- cotangent: bfloat16 [16384, 128], P(('row', 'col')), may hold values from -768 to 768
Outputs:
- atom_out: bfloat16 [16384, 128], P(('row', 'col'))
- pair_grad: bfloat16 [2048, 16, 8, 16, 128], P('row', None, 'col')
Inputs may be any that keep to these rules, and one draw needn't show every extreme that they name: `atom_token`: never falling. The atoms of the 16 tokens 16 * e to 16 * e + 15 form one run that begins within 48 atoms of atom 8 * 16 * e and ends within 48 atoms of atom 8 * 16 * (e + 1); every token has at least one atom. In every draw the tokens of the second device run into the atoms of both of its neighbours. `token_atoms`: the number of atoms a with atom_token[a] equal to the token; the most is taken in every draw. `key_shift`: both ends of the range are taken in every draw. `token_mask`: between 128 and 512 tokens are 0, anywhere among the tokens.
All inputs are finite; a program needn't handle non-finite values.
Results may differ from a plain program's by a relative error of at most 0.0187.
Values may be sent and summed in bfloat16 or wider, within the bound.
No kernel may reach another device: no remote copies, remote signals or barrier semaphores. Data moves between devices by JAX's collectives and lax.ppermute only.
A program may use at most 128 MiB of HBM per device.

v0:
```python
import math

import jax
import jax.numpy as jnp
from jax import lax
from jax.sharding import PartitionSpec as P

HA = 4
HT = 16
QB = 32
KW = 128
SHIFT = 16
HALO = 64


norm_epsilon = 1e-05


def extended_2(cells, sides, width):
    for axis, dim in sides:
        count = lax.axis_size(axis)
        ends = count - 1
        head = lax.slice_in_dim(cells, 0, width, axis=dim)
        tail = lax.slice_in_dim(cells, cells.shape[dim] - width, cells.shape[dim], axis=dim)
        cells = jnp.concatenate(
            [
                lax.ppermute(tail, axis, [(i, (i + 1) % count) for i in range(ends)]),
                cells,
                lax.ppermute(head, axis, [((i + 1) % count, i) for i in range(ends)]),
            ],
            axis=dim,
        )
    return cells


def combined_all(value, axis, join):
    pieces = jax.tree.map(lambda part: lax.all_gather(part, axis), value)
    head = jax.tree.map(lambda part: part[0], pieces)
    tail = jax.tree.map(lambda part: part[1:], pieces)
    subtotal, _ = lax.scan(lambda subtotal, section: (join(subtotal, section), None), head, tail)
    return subtotal


def layer_norm(values):
    values = values.astype(jnp.float32)
    centred = values - jnp.mean(values, axis=-1, keepdims=True)
    return centred * lax.rsqrt(jnp.mean(centred * centred, axis=-1, keepdims=True) + norm_epsilon)


def softmax_rows(scores):
    row_max = jnp.max(scores, axis=-1, keepdims=True)
    raised = jnp.exp(scores - row_max)
    return raised / jnp.sum(raised, axis=-1, keepdims=True)


def neighbours(values, rim_width):
    return extended_2(values.astype(jnp.bfloat16), ((("row", "col"), 0),), rim_width).astype(
        values.dtype
    )


def return_sums(partial_value, rim_width):
    outside = jnp.concatenate([partial_value[:rim_width], partial_value[2 * rim_width :]], axis=0)
    arrived = neighbours(outside, rim_width)
    return partial_value[rim_width : 2 * rim_width] + arrived[:rim_width] + arrived[3 * rim_width :]


def combine_parts(earlier, later):
    max_a, sum_a, out_a = earlier
    max_b, sum_b, out_b = later
    joint = jnp.maximum(max_a, max_b)
    scale_a = jnp.exp(max_a - joint)
    scale_b = jnp.exp(max_b - joint)
    merged_out = (
        out_a * jnp.transpose(scale_a)[:, :, None] + out_b * jnp.transpose(scale_b)[:, :, None]
    )
    return (joint, scale_a * sum_a + scale_b * sum_b, merged_out)


def shards(
    atoms,
    atom_bias,
    key_shift,
    atom_token,
    token_atoms,
    token_mask,
    pair,
    w_atom_qkv,
    w_atom_out,
    w_pool,
    w_token_qkv,
    w_token_out,
    w_bias,
    w_back,
    cotangent,
):
    atom_rows = atoms.shape[0]
    tok_rows = token_atoms.shape[0]
    width_atom = w_atom_qkv.shape[0]
    width_token = w_token_out.shape[0]
    device = lax.axis_index(("row", "col"))
    devices = lax.axis_size(("row", "col"))
    blocks = atom_rows // QB
    head_atom = width_atom // HA
    head_tok = width_token // HT
    normed = layer_norm(atoms).astype(jnp.bfloat16)
    project = jnp.dot(normed, w_atom_qkv, preferred_element_type=jnp.float32).astype(jnp.bfloat16)
    queries = project[:, :width_atom].reshape(blocks, QB, HA, head_atom)
    extended = extended_2(project[:, width_atom:], ((("row", "col"), 0),), HALO)
    starts = jnp.arange(blocks, dtype=jnp.int32) * QB + SHIFT + key_shift
    windows = jax.vmap(lambda window_at: lax.dynamic_slice_in_dim(extended, window_at, KW, 0))(
        starts
    )
    key_rows = windows[..., :width_atom].reshape(blocks, KW, HA, head_atom)
    value_rows = windows[..., width_atom:].reshape(blocks, KW, HA, head_atom)
    positions = (
        device * atom_rows - HALO + starts[:, None] + jnp.arange(KW, dtype=jnp.int32)[None, :]
    )
    inside = (positions >= 0) & (positions < devices * atom_rows)
    scores = jnp.einsum(
        "bqhd,bkhd->hbqk", queries, key_rows, preferred_element_type=jnp.float32
    ) / math.sqrt(head_atom)
    scores = scores + atom_bias.reshape(HA, blocks, QB, KW)
    scores = jnp.where(inside[None, :, None, :], scores, -jnp.inf)
    attend = softmax_rows(scores).astype(jnp.bfloat16)
    mixture = jnp.einsum("hbqk,bkhd->bqhd", attend, value_rows, preferred_element_type=jnp.float32)
    mixture = mixture.reshape(atom_rows, width_atom).astype(jnp.bfloat16)
    hidden = (
        atoms.astype(jnp.float32) + jnp.dot(mixture, w_atom_out, preferred_element_type=jnp.float32)
    ).astype(jnp.bfloat16)
    lifted = jax.nn.relu(jnp.dot(hidden, w_pool, preferred_element_type=jnp.float32))
    local_token = atom_token - (device - 1) * tok_rows
    selector = (jnp.arange(3 * tok_rows, dtype=jnp.int32)[:, None] == local_token[None, :]).astype(
        jnp.float32
    )
    partial_value = jnp.dot(
        selector, lifted, precision=lax.Precision.HIGHEST, preferred_element_type=jnp.float32
    )
    pooled = return_sums(partial_value, tok_rows) / token_atoms.astype(jnp.float32)[:, None]
    normed_tok = layer_norm(pooled).astype(jnp.bfloat16)
    row_index = lax.axis_index("row")
    col_index = lax.axis_index("col")
    live_own = token_mask.astype(jnp.bfloat16)
    everything, live_all = (
        lax.all_gather(normed_tok, ("row", "col"), axis=0, tiled=True),
        lax.all_gather(live_own, ("row", "col"), axis=0, tiled=True),
    )
    row_tokens = lax.axis_size("col") * tok_rows
    query_in = lax.dynamic_slice_in_dim(everything, row_index * row_tokens, row_tokens, 0)
    key_in = lax.dynamic_index_in_dim(
        everything.reshape(lax.axis_size("row"), lax.axis_size("col"), tok_rows, width_token),
        col_index,
        1,
        keepdims=False,
    )
    key_in = key_in.reshape(-1, width_token)
    live_keys = lax.dynamic_index_in_dim(
        live_all.reshape(lax.axis_size("row"), lax.axis_size("col"), tok_rows),
        col_index,
        1,
        keepdims=False,
    ).reshape(-1)
    queries_tok = jnp.dot(
        query_in, w_token_qkv[:, :width_token], preferred_element_type=jnp.float32
    ).astype(jnp.bfloat16)
    key_value = jnp.dot(
        key_in, w_token_qkv[:, width_token:], preferred_element_type=jnp.float32
    ).astype(jnp.bfloat16)
    tile = pair.reshape(pair.shape[0], -1, pair.shape[-1])
    pair_bias = jnp.einsum("ijc,ch->hij", tile, w_bias, preferred_element_type=jnp.float32)
    query_heads = queries_tok.reshape(-1, HT, head_tok)
    kv_heads = key_value.reshape(-1, 2, HT, head_tok)
    scores_tok = jnp.einsum(
        "ihd,jhd->hij", query_heads, kv_heads[:, 0], preferred_element_type=jnp.float32
    ) / math.sqrt(head_tok)
    scores_tok = jnp.where(live_keys[None, None, :] > 0, scores_tok + pair_bias, -jnp.inf)
    local_max = jnp.maximum(jnp.max(scores_tok, axis=-1), -1e30)
    raised = jnp.exp(scores_tok - local_max[:, :, None])
    local_sum = jnp.sum(raised, axis=-1)
    local_out = jnp.einsum(
        "hij,jhd->ihd",
        raised.astype(jnp.bfloat16),
        kv_heads[:, 1],
        preferred_element_type=jnp.float32,
    )
    row_max, row_sum, row_out = combined_all(
        (local_max, local_sum, local_out), "col", combine_parts
    )
    token_mix = (
        (row_out / jnp.transpose(row_sum)[:, :, None]).reshape(-1, width_token).astype(jnp.bfloat16)
    )
    own_rows = lax.dynamic_slice_in_dim(token_mix, col_index * tok_rows, tok_rows, 0)
    updated = (pooled + jnp.dot(own_rows, w_token_out, preferred_element_type=jnp.float32)).astype(
        jnp.bfloat16
    )
    lowered = jnp.dot(updated, w_back, preferred_element_type=jnp.float32)
    beside_all = neighbours(lowered, tok_rows)
    spread_back = jnp.einsum("ta,tc->ac", selector, beside_all, precision=lax.Precision.HIGHEST)
    atom_out = (hidden.astype(jnp.float32) + spread_back).astype(jnp.bfloat16)
    partial_grad = jnp.dot(
        selector,
        cotangent.astype(jnp.float32),
        precision=lax.Precision.HIGHEST,
        preferred_element_type=jnp.float32,
    )
    grad_up = return_sums(partial_grad, tok_rows).astype(jnp.bfloat16)
    grad_mid = lax.dot_general(
        grad_up, w_back, (((1,), (1,)), ((), ())), preferred_element_type=jnp.float32
    ).astype(jnp.bfloat16)
    grad_own = lax.dot_general(
        grad_mid, w_token_out, (((1,), (1,)), ((), ())), preferred_element_type=jnp.float32
    ).astype(jnp.bfloat16)
    grad_tile = lax.all_gather(grad_own, "col", axis=0, tiled=True)
    grad_heads = grad_tile.reshape(-1, HT, head_tok)
    grad_diag = jnp.einsum(
        "ihd,ihd->hi",
        grad_heads,
        token_mix.reshape(-1, HT, head_tok),
        preferred_element_type=jnp.float32,
    )
    grad_prob = jnp.einsum(
        "ihd,jhd->hij", grad_heads, kv_heads[:, 1], preferred_element_type=jnp.float32
    )
    probs_tok = jnp.exp(scores_tok - row_max[:, :, None]) / row_sum[:, :, None]
    grad_score = probs_tok * (grad_prob - grad_diag[:, :, None])
    pair_grad = jnp.einsum(
        "hij,ch->ijc", grad_score, w_bias.astype(jnp.float32), precision=lax.Precision.HIGHEST
    )
    pair_grad = pair_grad.astype(jnp.bfloat16).reshape(pair.shape)
    return (atom_out, pair_grad)


def solution(mesh):
    return jax.shard_map(
        shards,
        mesh=mesh,
        in_specs=(
            P(("row", "col"), None),
            P(None, ("row", "col"), None),
            P(("row", "col")),
            P(("row", "col")),
            P(("row", "col")),
            P(("row", "col")),
            P("row", None, "col", None, None),
            P(),
            P(),
            P(),
            P(),
            P(),
            P(),
            P(),
            P(("row", "col"), None),
        ),
        out_specs=(P(("row", "col"), None), P("row", None, "col", None, None)),
        check_vma=False,
    )
```

profile of v0, /device:TPU:8, one launch (start us, length us, event | category | flops | bytes accessed | tf_op | source)
XLA Modules:
  0.0 250.5 jit_solution(4272096329102207605)
XLA Ops:
  7.2 1.0 convert_reduce_fusion
  8.2 0.9 fusion.37
  9.2 1.1 convolution_convert_fusion.3
  10.3 1.9 collective-permute-start
  12.3 7.9 %collective-permute-start.1 = (bf16[64,256]{1,0:T(8,128)(2,1)S(1)}, bf16[64,256]{1,0:T(8,128)(2,1)S(1)}, u32[]{:S(2)}, u32[]{:S(2)}) collective-permute-start(bf16[64,256]{1,0:T(8,128)(2,1)S(1)} %get-tuple-element.110), channel_id=1, source_target_pairs={{1,0},{2,1},{3,2},{4,3},{5,4},{6,5},{7,6},{8,7},{9,8},{10,9},{11,1... | collective-permute-start | bytes 98312 | tf_op jit(solution)/shard_map/ppermute | solution.py:29
  20.1 0.7 broadcast_add_fusion
  20.9 0.7 broadcast_subtract_fusion
  21.8 5.1 %while.16 = (s32[]{:T(128)}, bf16[256,256]{1,0:T(8,128)(2,1)S(1)}, s32[4,2]{0,1:T(2,128)S(1)}, bf16[4,128,256]{2,1,0:T(8,128)(2,1)S(1)}, s32[]{:T(128)}) while((s32[]{:T(128)}, bf16[256,256]{1,0:T(8,128)(2,1)S(1)}, s32[4,2]{0,1:T(2,128)S(1)}, bf16[4,128,256]{2,1,0:T(8,128)(2,1)S(1)}, s32[]{:T(128)}) %tuple.55), condition=%wide.while_cond, body=%wide.while_body.sunk | while | flops 2 | bytes 131177 | solution.py:111
  21.8 0.5 slice.176
  22.4 0.7 bitcast_dynamic-update-slice_fusion.2
  23.1 0.5 slice.176
  23.6 0.7 bitcast_dynamic-update-slice_fusion.2
  24.4 0.5 slice.176
  24.9 0.7 bitcast_dynamic-update-slice_fusion.2
  25.7 0.5 slice.176
  26.2 0.7 bitcast_dynamic-update-slice_fusion.2
  27.3 0.4 fusion.92
  27.7 0.3 fusion.20
  28.6 0.3 fusion.93
  28.9 1.9 collective-permute-start.2
  30.8 7.9 %collective-permute-start.3 = (bf16[16,768]{1,0:T(8,128)(2,1)S(1)}, bf16[16,768]{1,0:T(8,128)(2,1)S(1)}, u32[]{:S(2)}, u32[]{:S(2)}) collective-permute-start(bf16[16,768]{1,0:T(8,128)(2,1)S(1)} %get-tuple-element.112), channel_id=1, source_target_pairs={{1,0},{2,1},{3,2},{4,3},{5,4},{6,5},{7,6},{8,7},{9,8},{10,9},{11,1... | collective-permute-start | bytes 73736 | tf_op jit(solution)/shard_map/ppermute | solution.py:29
  38.7 1.5 collective-permute-done.3
  40.6 0.7 multiply_convert_fusion
  41.7 67.4 %all-reduce.2 = bf16[16,8,16]{2,1,0:T(8,128)(2,1)S(1)} all-reduce(bf16[16,8,16]{2,1,0:T(8,128)(2,1)S(1)} %reshape.127), channel_id=1, replica_groups=mesh['row'=16,'col'=8] {'row','col'}, use_global_device_ids=true, to_apply=%add.1 | all-reduce | flops 2048 | bytes 8192
  109.1 0.6 gt.16
  109.7 7.0 %fusion.75 = f32[16,128,256]{2,0,1:T(8,128)} fusion(bf16[128,256,128]{2,1,0:T(8,128)(2,1)} %bitcast.99, bf16[128,16]{0,1:T(8,128)(2,1)S(1)} %copy-done.10), kind=kOutput, calls=%fused_computation.102 | convolution fusion | flops 134217728 | bytes 10489856 | tf_op jit(solution)/shard_map/ijc,ch->hij/dot_general | solution.py:170
  116.7 1.7 fusion.14
  118.6 1.0 constant_dynamic-slice_fusion.1
  119.6 2.4 convolution_convert_fusion.1
  122.1 1.2 copy.57
  123.3 3.3 %fusion.95 = (f32[16,128]{1,0:T(8,128)S(1)}, f32[16,128,256]{2,1,0:T(8,128)S(1)}) fusion(f32[16,128,256]{2,0,1:T(8,128)} %fusion.75, bf16[128,16,48]{0,2,1:T(8,128)(2,1)S(1)} %bitcast.103, bf16[256,2,16,48]{0,3,2,1:T(8,128)(2,1)} %bitcast.100, pred[256]{0:T(512)(128)(4,1)} %gt.16), kind=kOutput, calls=%fused_computation.130 | convolution fusion | flops 52426752 | bytes 4792832 | tf_op jit(solution)/shard_map/ihd,jhd->hij/dot_general | solution.py:173
  126.7 0.6 copy-done.7
  127.3 1.3 convolution_bitcast_fusion
  128.6 1.5 fusion.94
  130.1 0.6 fusion.91
  130.7 1.9 collective-permute-start.6
  132.7 7.9 %collective-permute-start.7 = (bf16[16,128]{1,0:T(8,128)(2,1)}, bf16[16,128]{1,0:T(8,128)(2,1)}, u32[]{:S(2)}, u32[]{:S(2)}) collective-permute-start(bf16[16,128]{1,0:T(8,128)(2,1)} %get-tuple-element.114), channel_id=1, source_target_pairs={{1,0},{2,1},{3,2},{4,3},{5,4},{6,5},{7,6},{8,7},{9,8},{10,9},{11,1... | collective-permute-start | bytes 12296 | tf_op jit(solution)/shard_map/ppermute | solution.py:29
  140.5 1.5 collective-permute-done.7
  142.0 1.9 convolution_convert_fusion.4
  143.9 13.1 %all_gather.32 = bf16[128,768]{1,0:T(8,128)(2,1)S(1)} all-gather(bf16[16,768]{1,0:T(8,128)(2,1)} %convolution_convert_fusion.4), channel_id=1, replica_groups=mesh['row'=16,'col'=8] {'col'}, dimensions={0}, use_global_device_ids=true | all-gather | bytes 221184 | tf_op jit(solution)/shard_map/all_gather | solution.py:213
  157.0 0.8 copy.62
  157.8 1.4 fusion.10
  159.2 12.8 %all-gather.1 = f32[128,128]{1,0:T(8,128)S(1)} all-gather(f32[16,128]{1,0:T(8,128)S(1)} %fusion.10), channel_id=3, replica_groups=mesh['row'=16,'col'=8] {'col'}, dimensions={0}, use_global_device_ids=true | all-gather | bytes 73728 | tf_op jit(solution)/shard_map/all_gather | solution.py:37
  172.0 12.9 %all-gather = f32[128,128]{1,0:T(8,128)S(1)} all-gather(f32[16,128]{1,0:T(8,128)S(1)} %copy-done.8), channel_id=2, replica_groups=mesh['row'=16,'col'=8] {'col'}, dimensions={0}, use_global_device_ids=true | all-gather | bytes 73728 | tf_op jit(solution)/shard_map/all_gather | solution.py:37
  185.0 1.0 slice.144
  186.0 0.5 copy.59
  186.5 3.5 %slice.147 = f32[896,16,48]{0,2,1:T(8,128)} slice(f32[1024,16,48]{0,2,1:T(8,128)} %all-gather.8.cloned.1.call-done), slice={[128:1024], [0:16], [0:48]} | slice | bytes 5505024 | tf_op jit(solution)/shard_map/slice | solution.py:39
  190.0 7.2 %copy.71 = f32[896,16,48]{2,1,0:T(8,128)} copy(f32[896,16,48]{0,2,1:T(8,128)} %slice.147) | data formatting | bytes 5505024 | tf_op jit(solution)/shard_map/while | solution.py:40
  197.2 15.1 %while.15 = (s32[]{:T(128)}, f32[16,128]{1,0:T(8,128)S(1)}, f32[16,128]{1,0:T(8,128)S(1)}, f32[128,16,48]{2,1,0:T(8,128)S(1)}, f32[7,16,128]{2,1,0:T(8,128)S(1)}...) while((s32[]{:T(128)}, f32[16,128]{1,0:T(8,128)S(1)}, f32[16,128]{1,0:T(8,128)S(1)}, ...), condition=%wide.region_9.10_spmd, body=%wide.region_8.9_spmd.sunk | while | flops 309250 | bytes 1335401 | solution.py:40
  197.5 1.9 fusion.121
  199.7 1.9 fusion.121
  201.8 1.9 fusion.121
  204.0 1.9 fusion.121
  206.2 1.9 fusion.121
  208.3 1.9 fusion.121
  210.5 1.9 fusion.121
  212.4 1.2 copy.61
  213.6 2.0 fusion.28
  215.5 1.5 fusion.25
  217.0 6.3 %collective-permute-start.5 = (bf16[16,128]{1,0:T(8,128)(2,1)S(1)}, bf16[16,128]{1,0:T(8,128)(2,1)S(1)}, u32[]{:S(2)}, u32[]{:S(2)}) collective-permute-start(bf16[16,128]{1,0:T(8,128)(2,1)S(1)} %fusion.25), channel_id=1, source_target_pairs={{1,0},{2,1},{3,2},{4,3},{5,4},{6,5},{7,6},{8,7},{9,8},{10,9},{11,1... | collective-permute-start | bytes 12296 | tf_op jit(solution)/shard_map/ppermute | solution.py:29
  223.4 1.9 collective-permute-start.4
  225.3 2.2 subtract_multiply_fusion
  227.6 15.2 %convolution_convert_fusion = bf16[128,256,128]{2,1,0:T(8,128)(2,1)} fusion(f32[16,128,256]{2,1,0:T(8,128)S(1)} %subtract_multiply_fusion, bf16[128,16]{0,1:T(8,128)(2,1)S(1)} %copy-done.11), kind=kOutput, calls=%fused_computation.13 | convolution fusion | flops 809500672 | bytes 10489856 | tf_op jit(solution)/shard_map/hij,ch->ijc/dot_general | solution.py:226
  242.8 0.8 fusion.22
  (119 shorter events, 4.3 us)
Async XLA Ops:
  7.2 134.9 %copy-start = (bf16[768,768]{1,0:T(8,128)(2,1)S(1)}, bf16[768,768]{1,0:T(8,128)(2,1)}, u32[]{:S(2)}) copy-start(bf16[768,768]{1,0:T(8,128)(2,1)} %param.28) | copy-start | bytes 3538948
  7.2 20.1 %copy-start.14 = (bf16[4,128,128]{2,1,0:T(8,128)(2,1)S(1)}, bf16[4,128,128]{2,1,0:T(8,128)(2,1)}, u32[]{:S(2)}) copy-start(bf16[4,128,128]{2,1,0:T(8,128)(2,1)} %param.18) | copy-start | bytes 393220
  7.2 109.5 %all-gather.6.cloned.1.call-start = ((), (), s32[]{:S(2)}) async-start(), calls=%async_computation | async-start | bytes 3170304 | tf_op jit(solution)/shard_map/all_gather | solution.py:145
  10.3 11.4 %collective-permute-start = (bf16[64,256]{1,0:T(8,128)(2,1)S(1)}, bf16[64,256]{1,0:T(8,128)(2,1)S(1)}, u32[]{:S(2)}, u32[]{:S(2)}) collective-permute-start(bf16[64,256]{1,0:T(8,128)(2,1)S(1)} %get-tuple-element.109), channel_id=1, source_target_pairs={{0,1},{1,2},{2,3},{3,4},{4,5},{5,6},{6,7},{7,8},{8,9},{9,10},{10,1... | collective-permute-start | bytes 98312 | tf_op jit(solution)/shard_map/ppermute | solution.py:27
  12.3 9.4 %collective-permute-start.1 = (bf16[64,256]{1,0:T(8,128)(2,1)S(1)}, bf16[64,256]{1,0:T(8,128)(2,1)S(1)}, u32[]{:S(2)}, u32[]{:S(2)}) collective-permute-start(bf16[64,256]{1,0:T(8,128)(2,1)S(1)} %get-tuple-element.110), channel_id=1, source_target_pairs={{1,0},{2,1},{3,2},{4,3},{5,4},{6,5},{7,6},{8,7},{9,8},{10,9},{11,1... | collective-permute-start | bytes 98312 | tf_op jit(solution)/shard_map/ppermute | solution.py:29
  21.5 7.1 %copy-start.12 = (s32[128]{0:T(128)}, s32[128]{0:T(128)S(1)}, u32[]{:S(2)}) copy-start(s32[128]{0:T(128)S(1)} %broadcast_subtract_fusion) | copy-start | bytes 1540
  21.7 6.5 %copy-start.5 = (bf16[128,128]{1,0:T(8,128)(2,1)S(1)}, bf16[128,128]{1,0:T(8,128)(2,1)}, u32[]{:S(2)}) copy-start(bf16[128,128]{1,0:T(8,128)(2,1)} %param.17) | copy-start | bytes 98308
  21.7 6.5 %copy-start.9 = (bf16[128,128]{1,0:T(8,128)(2,1)S(1)}, bf16[128,128]{1,0:T(8,128)(2,1)}, u32[]{:S(2)}) copy-start(bf16[128,128]{1,0:T(8,128)(2,1)} %param.25) | copy-start | bytes 98308
  26.9 1.5 copy-start.6
  27.1 11.6 %copy-start.15 = (s32[16]{0:T(128)S(1)}, s32[16]{0:T(128)}, u32[]{:S(2)}) copy-start(s32[16]{0:T(128)} %param.21) | copy-start | bytes 196
  27.3 14.1 %copy-start.16 = (s32[16]{0:T(128)S(1)}, s32[16]{0:T(128)}, u32[]{:S(2)}) copy-start(s32[16]{0:T(128)} %param.22) | copy-start | bytes 196
  27.3 82.4 %copy-start.10 = (bf16[128,16]{0,1:T(8,128)(2,1)S(1)}, bf16[128,16]{0,1:T(8,128)(2,1)}, u32[]{:S(2)}) copy-start(bf16[128,16]{0,1:T(8,128)(2,1)} %param.29) | copy-start | bytes 12292
  28.9 9.8 %collective-permute-start.2 = (bf16[16,768]{1,0:T(8,128)(2,1)S(1)}, bf16[16,768]{1,0:T(8,128)(2,1)S(1)}, u32[]{:S(2)}, u32[]{:S(2)}) collective-permute-start(bf16[16,768]{1,0:T(8,128)(2,1)S(1)} %get-tuple-element.111), channel_id=1, source_target_pairs={{0,1},{1,2},{2,3},{3,4},{4,5},{5,6},{6,7},{7,8},{8,9},{9,10},{10,1... | collective-permute-start | bytes 73736 | tf_op jit(solution)/shard_map/ppermute | solution.py:27
  30.8 9.4 %collective-permute-start.3 = (bf16[16,768]{1,0:T(8,128)(2,1)S(1)}, bf16[16,768]{1,0:T(8,128)(2,1)S(1)}, u32[]{:S(2)}, u32[]{:S(2)}) collective-permute-start(bf16[16,768]{1,0:T(8,128)(2,1)S(1)} %get-tuple-element.112), channel_id=1, source_target_pairs={{1,0},{2,1},{3,2},{4,3},{5,4},{6,5},{7,6},{8,7},{9,8},{10,9},{11,1... | collective-permute-start | bytes 73736 | tf_op jit(solution)/shard_map/ppermute | solution.py:29
  41.3 143.6 %all-gather.8.cloned.1.call-start = ((), (), s32[]{:S(2)}) async-start(), calls=%async_computation.1 | async-start | bytes 3538944 | tf_op jit(solution)/shard_map/all_gather | solution.py:37
  123.3 4.0 %copy-start.3 = (bf16[256,1536]{0,1:T(8,128)(2,1)S(1)}, bf16[256,1536]{0,1:T(8,128)(2,1)}, u32[]{:S(2)}) copy-start(bf16[256,1536]{0,1:T(8,128)(2,1)} %copy.57) | copy-start | bytes 2359300
  126.7 31.2 %copy-start.1 = (f32[16,128,256]{2,1,0:T(8,128)}, f32[16,128,256]{2,1,0:T(8,128)S(1)}, u32[]{:S(2)}) copy-start(f32[16,128,256]{2,1,0:T(8,128)S(1)} %get-tuple-element.124) | copy-start | bytes 6291460
  126.7 15.4 %copy-start.4 = (bf16[768,128]{1,0:T(8,128)(2,1)S(1)}, bf16[768,128]{1,0:T(8,128)(2,1)}, u32[]{:S(2)}) copy-start(bf16[768,128]{1,0:T(8,128)(2,1)} %param.30) | copy-start | bytes 589828
  126.7 0.6 copy-start.7
  130.7 9.8 %collective-permute-start.6 = (bf16[16,128]{1,0:T(8,128)(2,1)}, bf16[16,128]{1,0:T(8,128)(2,1)}, u32[]{:S(2)}, u32[]{:S(2)}) collective-permute-start(bf16[16,128]{1,0:T(8,128)(2,1)} %get-tuple-element.113), channel_id=1, source_target_pairs={{0,1},{1,2},{2,3},{3,4},{4,5},{5,6},{6,7},{7,8},{8,9},{9,10},{10,1... | collective-permute-start | bytes 12296 | tf_op jit(solution)/shard_map/ppermute | solution.py:27
  132.7 9.4 %collective-permute-start.7 = (bf16[16,128]{1,0:T(8,128)(2,1)}, bf16[16,128]{1,0:T(8,128)(2,1)}, u32[]{:S(2)}, u32[]{:S(2)}) collective-permute-start(bf16[16,128]{1,0:T(8,128)(2,1)} %get-tuple-element.114), channel_id=1, source_target_pairs={{1,0},{2,1},{3,2},{4,3},{5,4},{6,5},{7,6},{8,7},{9,8},{10,9},{11,1... | collective-permute-start | bytes 12296 | tf_op jit(solution)/shard_map/ppermute | solution.py:29
  157.8 14.2 %copy-start.8 = (f32[16,128]{1,0:T(8,128)S(1)}, f32[16,128]{1,0:T(8,128)}, u32[]{:S(2)}) copy-start(f32[16,128]{1,0:T(8,128)} %copy-done.7) | copy-start | bytes 24580
  213.6 11.8 %copy-start.2 = (f32[16,128,256]{2,1,0:T(8,128)S(1)}, f32[16,128,256]{2,1,0:T(8,128)}, u32[]{:S(2)}) copy-start(f32[16,128,256]{2,1,0:T(8,128)} %copy-done.1) | copy-start | bytes 6291460
  217.0 25.7 %collective-permute-start.5 = (bf16[16,128]{1,0:T(8,128)(2,1)S(1)}, bf16[16,128]{1,0:T(8,128)(2,1)S(1)}, u32[]{:S(2)}, u32[]{:S(2)}) collective-permute-start(bf16[16,128]{1,0:T(8,128)(2,1)S(1)} %fusion.25), channel_id=1, source_target_pairs={{1,0},{2,1},{3,2},{4,3},{5,4},{6,5},{7,6},{8,7},{9,8},{10,9},{11,1... | collective-permute-start | bytes 12296 | tf_op jit(solution)/shard_map/ppermute | solution.py:29
  223.4 19.4 %collective-permute-start.4 = (bf16[16,128]{1,0:T(8,128)(2,1)S(1)}, bf16[16,128]{1,0:T(8,128)(2,1)S(1)}, u32[]{:S(2)}, u32[]{:S(2)}) collective-permute-start(bf16[16,128]{1,0:T(8,128)(2,1)S(1)} %fusion.25), channel_id=1, source_target_pairs={{0,1},{1,2},{2,3},{3,4},{4,5},{5,6},{6,7},{7,8},{8,9},{9,10},{10,1... | collective-permute-start | bytes 12296 | tf_op jit(solution)/shard_map/ppermute | solution.py:27
  225.3 2.2 copy-start.11
  227.6 15.2 %copy-start.13 = (s32[128]{0:T(128)S(1)}, s32[128]{0:T(128)}, u32[]{:S(2)}) copy-start(s32[128]{0:T(128)} %copy-done.12) | copy-start | bytes 1540
Sparse Core Ops, SparseCore 0:
  41.4 66.2 all-gather.5
  128.8 29.5 all-gather.7
where the time goes:
time: 252 us; the launch traced here: 250 us
  blocking collectives  106 us (42%)
  matrix products  41.3 us (16%)
  starting transfers between devices  37.7 us (15%)
  local copies, waits for them, and re-layouts  26.1 us (10%)
  other arithmetic  21.3 us (8%)
  between operations  14.6 us (6%)
  waiting for transfers between devices  3.04 us (1%)
    unnamed x1, blocking collectives  67.4 us
    ppermute x4, starting transfers between devices, extended_2(): lax.ppermute(head, axis, [((i + 1) % count, i) for i in range(ends)])  29.9 us
    all_gather x2, blocking collectives, combined_all(): pieces = jax.tree.map(lambda part: lax.all_gather(part, axis), value)  25.7 us
    dot_general x1, matrix products, shards(): jnp.einsum('hij,ch->ijc', grad_score, w_bias.astype(jnp.float32), precisi...  15.2 us
    add x7, other arithmetic, combine_parts(): out_a * jnp.transpose(scale_a)[:, :, None]  13.2 us
    all_gather x1, blocking collectives, shards(): grad_tile = lax.all_gather(grad_own, 'col', axis=0, tiled=True)  13.1 us
    while x3, local copies, waits for them, and re-layouts, combined_all(): lax.scan(lambda subtotal, section: (join(subtotal, section), None), head,...  8.9 us
    ppermute x4, starting transfers between devices, extended_2(): lax.ppermute(tail, axis, [(i, (i + 1) % count) for i in range(ends)])  7.67 us
  transfers between devices with their start and end apart: 10, of which 2 were waited for; matrix products, arithmetic and copies ran while one was open for 13% of the time, Pallas kernels for 0%

commit v1 on v0

v1 whole, which is shorter than its diff:
```python
import functools
import math

import jax
import jax.numpy as jnp
from jax import lax
from jax.experimental import pallas as pl
from jax.experimental.pallas import tpu as pltpu
from jax.sharding import PartitionSpec as P

HA = 4
HT = 16
QB = 32
KW = 128
SHIFT = 16
HALF = 64
GROUP = 8
AUX = 16
EPSILON = 1e-05
LOWEST = -1e30
F32 = jnp.float32
BF16 = jnp.bfloat16
NT = (((1,), (1,)), ((), ()))
TN = (((0,), (0,)), ((), ()))

VMEM = pl.BlockSpec(memory_space=pltpu.VMEM)
SMEM = pl.BlockSpec(memory_space=pltpu.SMEM)


def params(mib):
    return pltpu.CompilerParams(vmem_limit_bytes=mib << 20)


def iota(shape, dim):
    return lax.broadcasted_iota(jnp.int32, shape, dim)


def dot(a, b, dims=None):
    if dims is None:
        return jnp.dot(a, b, preferred_element_type=F32)
    return lax.dot_general(a, b, dims, preferred_element_type=F32)


def normal(values):
    centred = values - jnp.mean(values, axis=-1, keepdims=True)
    return centred * lax.rsqrt(jnp.mean(centred * centred, axis=-1, keepdims=True) + EPSILON)


def split(values):
    high = values.astype(BF16)
    return high, (values - high.astype(F32)).astype(BF16)


def grouped_weight(head_rows, member):
    rows = iota(head_rows.shape, 0)
    return jnp.where(rows % GROUP == member, head_rows, 0.0).astype(BF16)


def pair_bias_kernel(pair_ref, head_ref, out_ref):
    head_rows = head_ref[...].astype(F32)
    weights = [
        jnp.concatenate(
            [grouped_weight(head_rows, 2 * p), grouped_weight(head_rows, 2 * p + 1)], axis=1
        )
        for p in range(GROUP // 2)
    ]
    for g in range(pair_ref.shape[0] // GROUP):
        total = None
        for p in range(GROUP // 2):
            row = g * GROUP + 2 * p
            both = jnp.concatenate([pair_ref[row], pair_ref[row + 1]], axis=1)
            part = dot(weights[p], both, NT)
            total = part if total is None else total + part
        out_ref[g] = total.reshape(HT, GROUP, total.shape[-1])


def pack_kernel(flag_ref, atoms_ref, bias_ref, cot_ref, aux_ref, near_ref, far_ref):
    def fill(out_ref, at):
        out_ref[0:128] = atoms_ref[...]
        for h in range(HA):
            out_ref[128 + HALF * h : 128 + HALF * (h + 1)] = bias_ref[h, at : at + HALF]
        out_ref[384:448] = cot_ref[at : at + HALF]
        out_ref[448:464] = aux_ref[...]

    @pl.when(flag_ref[0] == 1)
    def _():
        fill(near_ref, 0)
        fill(far_ref, HALF)

    @pl.when(flag_ref[0] == 0)
    def _():
        fill(near_ref, HALF)
        fill(far_ref, 0)


def atom_kernel(
    flag_ref,
    near_ref,
    far_ref,
    atoms_ref,
    bias_ref,
    cot_ref,
    aux_ref,
    count_ref,
    mask_ref,
    w_qkv_ref,
    w_out_ref,
    w_pool_ref,
    hidden_ref,
    pooled_ref,
    to_row_ref,
    to_col_ref,
    prev_ref,
    next_ref,
):
    @pl.when(flag_ref[0] == 1)
    def _():
        prev_ref[...] = near_ref[...]
        next_ref[...] = far_ref[...]

    @pl.when(flag_ref[0] == 0)
    def _():
        prev_ref[...] = far_ref[...]
        next_ref[...] = near_ref[...]

    first = flag_ref[1] * 128
    extended = jnp.concatenate([prev_ref[0:128], atoms_ref[...], next_ref[0:128]], axis=0)
    wide = extended.astype(F32)
    project = dot(normal(wide).astype(BF16), w_qkv_ref[...]).astype(BF16)
    head_lane = iota((QB, 128), 1) // 32
    head_mask = [jnp.where(head_lane == h, 1.0, 0.0) for h in range(HA)]
    slot = iota((1, KW), 1)
    offset = iota((KW, 160), 1) - iota((KW, 160), 0) - SHIFT
    mixes = []
    for block in (2, 3, 4, 5, 6, 7, 0, 1):
        if block < 2:
            source, local = prev_ref, block
            bias = [
                prev_ref[128 + HALF * h + 32 * local : 160 + HALF * h + 32 * local]
                for h in range(HA)
            ]
            shift = prev_ref[451 + local : 452 + local]
        elif block > 5:
            local = block - 6
            bias = [
                next_ref[128 + HALF * h + 32 * local : 160 + HALF * h + 32 * local]
                for h in range(HA)
            ]
            shift = next_ref[449 + local : 450 + local]
        else:
            local = block - 2
            bias = [bias_ref[h, 32 * local : 32 * local + 32] for h in range(HA)]
            shift = aux_ref[1 + local : 2 + local]
        shift = shift.astype(F32).astype(jnp.int32)
        pick = jnp.where(offset == shift[:, 0:1], 1.0, 0.0).astype(BF16)
        window = dot(pick, project[32 * block : 32 * block + 160, 128:]).astype(BF16)
        query = project[64 + 32 * block : 96 + 32 * block, :128].astype(F32)
        stacked = jnp.concatenate([query * head_mask[h] for h in range(HA)], axis=0).astype(BF16)
        scores = dot(stacked, window[:, :128], NT) * (1.0 / math.sqrt(32))
        scores = scores + jnp.concatenate(bias, axis=0).astype(F32)
        position = slot + (first + 32 * block - 112) + shift
        inside = (position >= 0) & (position < flag_ref[2])
        scores = jnp.where(inside, scores, LOWEST)
        raised = jnp.exp(scores - jnp.max(scores, axis=-1, keepdims=True))
        weight = (raised / jnp.sum(raised, axis=-1, keepdims=True)).astype(BF16)
        mixed = dot(weight, window[:, 128:])
        mix = mixed[0:32] * head_mask[0]
        for h in range(1, HA):
            mix = mix + mixed[32 * h : 32 * h + 32] * head_mask[h]
        mixes.append(mix)
    mixture = jnp.concatenate(mixes, axis=0).astype(BF16)
    base = jnp.concatenate([wide[128:320], wide[64:128]], axis=0)
    hidden = (base + dot(mixture, w_out_ref[...])).astype(BF16)
    hidden_ref[...] = hidden[:128]
    lifted = jnp.maximum(dot(hidden, w_pool_ref[...]), 0.0)
    own_token = aux_ref[0:1].astype(F32) - 17.0
    prev_token = prev_ref[448:449].astype(F32) - 33.0
    next_token = next_ref[448:449].astype(F32) - 1.0
    beside = jnp.where(iota((1, 128), 1) < HALF, next_token, prev_token)
    token = jnp.concatenate([own_token, beside], axis=1)
    select = jnp.where(iota((16, 256), 0).astype(F32) == token, 1.0, 0.0).astype(BF16)
    high, low = split(lifted)
    pooled = (dot(select, high) + dot(select, low)) / count_ref[...].astype(F32)
    pooled_ref[...] = pooled
    normed = normal(pooled).astype(BF16)
    cot = jnp.concatenate([cot_ref[...], next_ref[384:448], prev_ref[384:448]], axis=0)
    grad_up = dot(select, cot).astype(BF16)
    live = jnp.broadcast_to(mask_ref[...].astype(F32), (16, 128)).astype(BF16)
    for r in range(to_row_ref.shape[0]):
        to_row_ref[r, :, :768] = normed
        to_row_ref[r, :, 768:] = live
    for c in range(to_col_ref.shape[0]):
        to_col_ref[c, :, :768] = normed
        to_col_ref[c, :, 768:] = grad_up


def window_of(head):
    block, rest = divmod(head, 8)
    return 384 * block + (0 if rest < 5 else 128)


def token_kernel(
    keys_ref,
    rows_ref,
    bias_ref,
    w_qkv_ref,
    w_out_ref,
    w_back_ref,
    prob_ref,
    grad_ref,
    to_col_ref,
):
    normed = rows_ref[:, :768]
    query = dot(normed, w_qkv_ref[:, :768]).astype(BF16)
    key = dot(keys_ref[:, :768], w_qkv_ref[:, 768:1536]).astype(BF16)
    value = dot(keys_ref[:, :768], w_qkv_ref[:, 1536:]).astype(BF16)
    middle = dot(rows_ref[:, 768:], w_back_ref[...], NT).astype(BF16)
    grad = dot(middle, w_out_ref[...], NT).astype(BF16)
    live = keys_ref[:, 768:].astype(F32).T[0:1]
    closed = jnp.where(live > 0, 0.0, -jnp.inf)
    lane = iota((128, 256), 1)
    stat_lane = iota((128, 128), 1)
    mixed = [jnp.zeros((128, 128), F32) for _ in range(6)]
    tops = jnp.zeros((128, 128), F32)
    sums = jnp.zeros((128, 128), F32)
    diags = jnp.zeros((128, 128), F32)
    for h in range(HT):
        at = window_of(h)
        inside = (lane >= 48 * h - at) & (lane < 48 * (h + 1) - at)
        query_h = jnp.where(inside, query[:, at : at + 256].astype(F32), 0.0).astype(BF16)
        grad_h = jnp.where(inside, grad[:, at : at + 256].astype(F32), 0.0).astype(BF16)
        value_h = value[:, at : at + 256]
        scores = dot(query_h, key[:, at : at + 256], NT) * (1.0 / math.sqrt(48))
        scores = scores + bias_ref[:, h].reshape(128, 256) + closed
        top = jnp.maximum(jnp.max(scores, axis=-1, keepdims=True), LOWEST)
        high = top.astype(BF16).astype(F32)
        top = high + (top - high).astype(BF16).astype(F32)
        raised = jnp.exp(scores - top)
        grads = dot(grad_h, value_h, NT)
        prob_ref[:, h] = raised.reshape(16, GROUP, 256)
        grad_ref[:, h] = grads.reshape(16, GROUP, 256)
        total = jnp.sum(raised, axis=-1, keepdims=True)
        diag = jnp.sum(raised * grads, axis=-1, keepdims=True)
        out = jnp.where(inside, dot(raised.astype(BF16), value_h), 0.0)
        mixed[at // 128] = mixed[at // 128] + out[:, :128]
        mixed[at // 128 + 1] = mixed[at // 128 + 1] + out[:, 128:]
        here = stat_lane == h
        tops = jnp.where(here, top, tops)
        sums = jnp.where(here, total, sums)
        diags = jnp.where(here, diag, diags)
    stats = jnp.zeros((128, 128), F32)
    for k, part in enumerate((tops, sums, diags)):
        high = part.astype(BF16).astype(F32)
        for n, piece in enumerate((high, part - high)):
            turn = 32 * k + 16 * n
            stats = stats + (pltpu.roll(piece, turn, axis=1) if turn else piece)
    stats = stats.astype(BF16)
    blocks = [part.astype(BF16) for part in mixed]
    for c in range(8):
        for k in range(6):
            to_col_ref[c, :, 128 * k : 128 * (k + 1)] = blocks[k][16 * c : 16 * c + 16]
        for k in range(8):
            to_col_ref[c, :, 768 + 128 * k : 896 + 128 * k] = stats[16 * k : 16 * k + 16]


def merge_kernel(
    flag_ref, parts_ref, pooled_ref, w_out_ref, w_back_ref, scale_ref, diag_ref, low_ref, ratio_ref
):
    lane = iota((128, 128), 1)
    tops, sums, diags = [], [], []
    for c in range(8):
        part = jnp.concatenate(
            [parts_ref[c, :, 768 + 128 * k : 896 + 128 * k] for k in range(8)], axis=0
        ).astype(F32)
        part = part + pltpu.roll(part, 112, axis=1)
        tops.append(part)
        sums.append(pltpu.roll(part, 96, axis=1))
        diags.append(pltpu.roll(part, 64, axis=1))
    top = functools.reduce(jnp.maximum, tops)
    ratios = [jnp.where(lane < HT, jnp.exp(part - top), 0.0) for part in tops]
    total = functools.reduce(jnp.add, [r * s for r, s in zip(ratios, sums)])
    diag = functools.reduce(jnp.add, [r * d for r, d in zip(ratios, diags)])
    total = jnp.where(lane < HT, total, 1.0)
    inverse = 1.0 / total
    for c in range(8):
        ratio_ref[c] = ratios[c] * inverse
    col = flag_ref[0]
    scale_ref[...] = ratio_ref[col]
    diag_ref[...] = diag * inverse
    own = pl.ds(pl.multiple_of(col * 16, 16), 16)
    spread = jnp.where(iota((128, 768), 1) // 48 == iota((128, 768), 0), 1.0, 0.0).astype(BF16)
    high, low = split(jnp.concatenate([ratio_ref[c, own] for c in range(8)], axis=0))
    factor = dot(high, spread) + dot(low, spread)
    mixed = None
    for c in range(8):
        part = parts_ref[c, :, :768].astype(F32) * factor[16 * c : 16 * c + 16]
        mixed = part if mixed is None else mixed + part
    updated = (pooled_ref[...] + dot(mixed.astype(BF16), w_out_ref[...])).astype(BF16)
    high, low = split(dot(updated, w_back_ref[...]))
    low_ref[0] = high
    low_ref[1] = low


def pair_grad_kernel(prob_ref, grad_ref, scale_ref, diag_ref, head_ref, out_ref):
    head_rows = head_ref[...].astype(F32)
    weights = jnp.concatenate([grouped_weight(head_rows, i) for i in range(GROUP)], axis=1)
    for g in range(prob_ref.shape[0]):
        scale = scale_ref[g * GROUP : (g + 1) * GROUP]
        diag = diag_ref[g * GROUP : (g + 1) * GROUP]
        rows = []
        for h in range(HT):
            rows.append(
                prob_ref[g, h] * scale[:, h : h + 1] * (grad_ref[g, h] - diag[:, h : h + 1])
            )
        score = jnp.concatenate(rows, axis=0)
        result = dot(score.T.astype(BF16), weights)
        for i in range(GROUP):
            out_ref[g * GROUP + i] = result[:, 128 * i : 128 * (i + 1)].astype(BF16)


def atom_out_kernel(flag_ref, near_ref, far_ref, low_ref, aux_ref, hidden_ref, out_ref):
    odd = flag_ref[0] == 1
    near = near_ref[...].astype(F32)
    far = far_ref[...].astype(F32)
    before = jnp.where(odd, near, far).astype(BF16)
    after = jnp.where(odd, far, near).astype(BF16)
    rows = jnp.concatenate([before, low_ref[0], after, low_ref[1]], axis=0)
    token = aux_ref[0:1].astype(F32) - 1.0
    index = iota((64, 128), 0)
    index = jnp.where(index < 48, index, index - 32).astype(F32)
    select = jnp.where(index == token, 1.0, 0.0).astype(BF16)
    out_ref[...] = (hidden_ref[...].astype(F32) + dot(select, rows, TN)).astype(BF16)


def shards(
    atoms,
    atom_bias,
    key_shift,
    atom_token,
    token_atoms,
    token_mask,
    pair,
    w_atom_qkv,
    w_atom_out,
    w_pool,
    w_token_qkv,
    w_token_out,
    w_bias,
    w_back,
    cotangent,
):
    row_count, col_count = lax.axis_size("row"), lax.axis_size("col")
    devices = row_count * col_count
    device = lax.axis_index(("row", "col"))
    col = lax.axis_index("col")
    core_pairs = [(i, i ^ 1) for i in range(col_count)]
    chip_pairs = [(i, i + 1) for i in range(1, devices - 1, 2)]
    chip_pairs = chip_pairs + [(j, i) for i, j in chip_pairs]

    relative = (atom_token - 16 * device + 17).astype(BF16)
    aux = jnp.concatenate(
        [
            relative[None, :],
            jnp.broadcast_to(key_shift.astype(BF16)[:, None], (4, 128)),
            jnp.zeros((AUX - 5, 128), BF16),
        ],
        axis=0,
    )
    flags = jnp.stack([device % 2, device, jnp.int32(128) * devices]).astype(jnp.int32)
    payload = jax.ShapeDtypeStruct((464, 128), BF16)
    near, far = pl.pallas_call(
        pack_kernel,
        in_specs=[SMEM, VMEM, VMEM, VMEM, VMEM],
        out_specs=[VMEM, VMEM],
        out_shape=[payload, payload],
        name="pack",
        cost_estimate=pl.CostEstimate(flops=0, bytes_accessed=1 << 20, transcendentals=0),
    )(flags, atoms, atom_bias, cotangent, aux)
    near = lax.ppermute(near, "col", core_pairs)
    far = lax.ppermute(far, ("row", "col"), chip_pairs)

    tile = pair.reshape(128, 256, 128)
    head_rows = jnp.repeat(jnp.transpose(w_bias), GROUP, axis=0)
    steps = 8
    bias = pl.pallas_call(
        pair_bias_kernel,
        grid=(steps,),
        in_specs=[
            pl.BlockSpec((128 // steps, 256, 128), lambda i: (i, 0, 0)),
            pl.BlockSpec((128, 128), lambda i: (0, 0)),
        ],
        out_specs=pl.BlockSpec((16 // steps, HT, GROUP, 256), lambda i: (i, 0, 0, 0)),
        out_shape=jax.ShapeDtypeStruct((16, HT, GROUP, 256), F32),
        compiler_params=params(24),
        name="pair_bias",
        cost_estimate=pl.CostEstimate(
            flops=2 * 128 * 256 * 128 * 16 * 8, bytes_accessed=12 << 20, transcendentals=0
        ),
    )(tile, head_rows)

    hidden, pooled, to_row, to_col = pl.pallas_call(
        atom_kernel,
        in_specs=[SMEM] + [VMEM] * 11,
        out_specs=[VMEM] * 4,
        out_shape=[
            jax.ShapeDtypeStruct((128, 128), BF16),
            jax.ShapeDtypeStruct((16, 768), F32),
            jax.ShapeDtypeStruct((row_count, 16, 896), BF16),
            jax.ShapeDtypeStruct((col_count, 16, 896), BF16),
        ],
        scratch_shapes=[pltpu.VMEM((464, 128), BF16), pltpu.VMEM((464, 128), BF16)],
        compiler_params=params(24),
        name="atom_stage",
        cost_estimate=pl.CostEstimate(flops=1 << 28, bytes_accessed=2 << 20, transcendentals=1 << 17),
    )(
        flags,
        near,
        far,
        atoms,
        atom_bias,
        cotangent,
        aux,
        token_atoms[:, None],
        token_mask[:, None],
        w_atom_qkv,
        w_atom_out,
        w_pool,
    )
    rows = lax.all_to_all(to_col, "col", 0, 0).reshape(128, 896)
    keys = lax.all_to_all(to_row, "row", 0, 0).reshape(256, 896)

    table = jax.ShapeDtypeStruct((16, HT, GROUP, 256), F32)
    prob, grad, to_col = pl.pallas_call(
        token_kernel,
        in_specs=[VMEM] * 6,
        out_specs=[VMEM] * 3,
        out_shape=[table, table, jax.ShapeDtypeStruct((col_count, 16, 1792), BF16)],
        compiler_params=params(40),
        name="token_stage",
        cost_estimate=pl.CostEstimate(flops=1 << 31, bytes_accessed=12 << 20, transcendentals=1 << 19),
    )(keys, rows, bias, w_token_qkv, w_token_out, w_back)
    parts = lax.all_to_all(to_col, "col", 0, 0)

    stat = jax.ShapeDtypeStruct((128, 128), F32)
    scale, diag, low = pl.pallas_call(
        merge_kernel,
        in_specs=[SMEM] + [VMEM] * 4,
        out_specs=[VMEM] * 3,
        out_shape=[stat, stat, jax.ShapeDtypeStruct((2, 16, 128), BF16)],
        scratch_shapes=[pltpu.VMEM((8, 128, 128), F32)],
        compiler_params=params(24),
        name="merge",
        cost_estimate=pl.CostEstimate(flops=1 << 26, bytes_accessed=2 << 20, transcendentals=1 << 17),
    )(col[None].astype(jnp.int32), parts, pooled, w_token_out, w_back)
    near = lax.ppermute(low[0], "col", core_pairs)
    far = lax.ppermute(low[0], ("row", "col"), chip_pairs)

    pair_grad = pl.pallas_call(
        pair_grad_kernel,
        grid=(steps,),
        in_specs=[
            pl.BlockSpec((16 // steps, HT, GROUP, 256), lambda i: (i, 0, 0, 0)),
            pl.BlockSpec((16 // steps, HT, GROUP, 256), lambda i: (i, 0, 0, 0)),
            pl.BlockSpec((128 // steps, 128), lambda i: (i, 0)),
            pl.BlockSpec((128 // steps, 128), lambda i: (i, 0)),
            pl.BlockSpec((128, 128), lambda i: (0, 0)),
        ],
        out_specs=pl.BlockSpec((128 // steps, 256, 128), lambda i: (i, 0, 0)),
        out_shape=jax.ShapeDtypeStruct((128, 256, 128), BF16),
        compiler_params=params(32),
        name="pair_grad",
        cost_estimate=pl.CostEstimate(
            flops=2 * 128 * 256 * 128 * 16 * 8, bytes_accessed=14 << 20, transcendentals=0
        ),
    )(prob, grad, scale, diag, head_rows)
    atom_out = pl.pallas_call(
        atom_out_kernel,
        in_specs=[SMEM] + [VMEM] * 5,
        out_specs=VMEM,
        out_shape=jax.ShapeDtypeStruct((128, 128), BF16),
        name="atom_out",
        cost_estimate=pl.CostEstimate(flops=1 << 21, bytes_accessed=1 << 17, transcendentals=0),
    )(flags, near, far, low, aux, hidden)
    return (atom_out, pair_grad.reshape(pair.shape))


def solution(mesh):
    return jax.shard_map(
        shards,
        mesh=mesh,
        in_specs=(
            P(("row", "col"), None),
            P(None, ("row", "col"), None),
            P(("row", "col")),
            P(("row", "col")),
            P(("row", "col")),
            P(("row", "col")),
            P("row", None, "col", None, None),
            P(),
            P(),
            P(),
            P(),
            P(),
            P(),
            P(),
            P(("row", "col"), None),
        ),
        out_specs=(P(("row", "col"), None), P("row", None, "col", None, None)),
        check_vma=False,
    )
```

time: 252 us -> 92.2 us (0.37)
  the two profiles are of different devices: /device:TPU:8 before, /device:TPU:1 now
where the time goes in v1:
time: 92.2 us; the launch traced here: 91.3 us
  blocking collectives  26.6 us (29%)
  Pallas kernels  25.6 us (28%)
  starting transfers between devices  17.5 us (19%)
  local copies, waits for them, and re-layouts  14.9 us (16%)
  waiting for transfers between devices  3.19 us (3%)
  other arithmetic  2.65 us (3%)
    all_to_all x1, blocking collectives, shards(): parts = lax.all_to_all(to_col, 'col', 0, 0)  14.3 us
    unnamed x38, local copies, waits for them, and re-layouts  13.3 us
    all_to_all x1, blocking collectives, shards(): rows = lax.all_to_all(to_col, 'col', 0, 0).reshape(128, 896)  12.3 us
    all_to_all x1, starting transfers between devices, shards(): keys = lax.all_to_all(to_row, 'row', 0, 0).reshape(256, 896)  9.92 us
    pallas_call x1, Pallas kernels, shards(): pl.pallas_call(pair_grad_kernel, grid=(steps,), in_specs=[pl.BlockSpec((1...  6.74 us
    pallas_call x1, Pallas kernels, shards(): pl.pallas_call(token_kernel, in_specs=[VMEM] * 6, out_specs=[VMEM] * 3, o...  5.53 us
    pallas_call x1, Pallas kernels, shards(): pl.pallas_call(atom_kernel, in_specs=[SMEM] + [VMEM] * 11, out_specs=[VME...  5.27 us
    pallas_call x1, Pallas kernels, shards(): pl.pallas_call(pair_bias_kernel, grid=(steps,), in_specs=[pl.BlockSpec((1...  3.85 us
  transfers between devices with their start and end apart: 5, of which 2 were waited for; matrix products, arithmetic and copies ran while one was open for 2% of the time, Pallas kernels for 12%

profile of v1, /device:TPU:1, one launch (start us, length us, event | category | flops | bytes accessed | tf_op | source)
XLA Modules:
  0.0 91.3 jit_solution(2910675006464259750)
XLA Ops:
  0.6 0.0 copy-start
  0.7 0.7 convert_element_type.7
  1.3 0.1 pad.1.clone
  1.4 0.1 pad.2.clone
  1.5 0.7 convert_bitcast_fusion
  2.1 0.7 pad_add_fusion.flag_ref
  2.8 0.7 maximum_maximum_fusion.aux_ref
  3.5 1.6 %pack.1 = (bf16[464,128]{1,0:T(8,128)(2,1)}, bf16[464,128]{1,0:T(8,128)(2,1)}) custom-call(s32[3]{0:T(128)} %pad_add_fusion.flag_ref, bf16[128,128]{1,0:T(8,128)(2,1)} %atoms_ref.3, bf16[4,128,128]{2,1,0:T(8,128)(2,1)} %bias_ref.3, bf16[128,128]{1,0:T(8,128)(2,1)} %cot_ref.3, bf16[16,128]{1,0:T(8,128)(2,1)} %maximum_maximum_fusion.aux_ref), custom_call_target="tpu_custom_call" | custom-call | bytes 1048576 | tf_op jit(solution)/shard_map/pack/pallas_call | solution.py:371
  5.1 1.4 %collective-permute-start = (bf16[464,128]{1,0:T(8,128)(2,1)}, bf16[464,128]{1,0:T(8,128)(2,1)S(1)}, u32[]{:S(2)}, u32[]{:S(2)}) collective-permute-start(bf16[464,128]{1,0:T(8,128)(2,1)} %get-tuple-element.14), channel_id=1, source_target_pairs={{0,1},{1,0},{2,3},{3,2},{4,5},{5,4},{6,7},{7,6},{8,9},{9,8},{10,11... | collective-permute-start | bytes 356360 | tf_op jit(solution)/shard_map/ppermute | solution.py:379
  6.5 3.1 %collective-permute-start.1 = (bf16[464,128]{1,0:T(8,128)(2,1)}, bf16[464,128]{1,0:T(8,128)(2,1)S(1)}, u32[]{:S(2)}, u32[]{:S(2)}) collective-permute-start(bf16[464,128]{1,0:T(8,128)(2,1)} %get-tuple-element.15), channel_id=1, source_target_pairs={{1,2},{3,4},{5,6},{7,8},{9,10},{11,12},{13,14},{15,16},{17,18},{19... | collective-permute-start | bytes 356360 | tf_op jit(solution)/shard_map/ppermute | solution.py:380
  9.6 0.7 copy.17.count_ref
  10.4 0.7 copy.18.mask_ref
  11.1 0.0 collective-permute-done.near_ref
  11.1 1.8 %collective-permute-done.1.far_ref = bf16[464,128]{1,0:T(8,128)(2,1)S(1)} collective-permute-done((bf16[464,128]{1,0:T(8,128)(2,1)}, bf16[464,128]{1,0:T(8,128)(2,1)S(1)}, u32[]{:S(2)}, u32[]{:S(2)}) %collective-permute-start.1) | collective-permute-done | bytes 118816 | tf_op jit(solution)/shard_map/ppermute | solution.py:380
  12.9 0.0 copy-start.4
  12.9 0.9 copy-done.4
  13.8 0.0 copy-start.7
  13.8 0.7 copy-done.7
  14.5 0.0 copy-start.8
  14.5 0.8 copy-done.8
  15.2 0.0 copy-start.9
  15.2 0.8 copy-done.9
  16.0 0.0 copy-start.12
  16.0 0.7 copy-done.12
  16.7 0.0 copy-start.14
  16.7 0.9 %copy-done.14 = bf16[128,768]{1,0:T(8,128)(2,1)S(1)} copy-done((bf16[128,768]{1,0:T(8,128)(2,1)S(1)}, bf16[128,768]{1,0:T(8,128)(2,1)}, u32[]{:S(2)}) %copy-start.14) | copy-done | bytes 196632
  17.6 0.0 copy-start.15
  17.6 0.9 copy-done.15
  18.5 0.0 copy-start.16
  18.5 0.8 copy-done.16
  19.2 5.3 %atom_stage.1 = (bf16[128,128]{1,0:T(8,128)(2,1)S(1)}, f32[16,768]{1,0:T(8,128)S(1)}, bf16[16,16,896]{2,1,0:T(8,128)(2,1)}, bf16[8,16,896]{2,1,0:T(8,128)(2,1)S(1)}) custom-call(s32[3]{0:T(128)S(1)} %copy-done.12, bf16[464,128]{1,0:T(8,128)(2,1)S(1)} %collective-permute-done.near_ref, bf16[464,128]{1,0:T(8,128)(2,1)S(1)} %collective-permute-done.1.far_ref, ...), custom_call_target="tpu_custom_call" | custom-call | flops 268435456 | bytes 2097152 | tf_op jit(solution)/shard_map/atom_stage/pallas_call | solution.py:401
  24.5 0.0 copy-start.5
  24.5 0.0 copy-start.10
  24.5 12.3 %all_to_all.15 = bf16[8,16,896]{2,1,0:T(8,128)(2,1)S(1)} all-to-all(bf16[8,16,896]{2,1,0:T(8,128)(2,1)S(1)} %get-tuple-element.17), channel_id=1, replica_groups=mesh['row'=16,'col'=8] {'col'}, dimensions={0} | all-to-all | bytes 458752 | tf_op jit(solution)/shard_map/all_to_all | solution.py:429
  36.8 0.0 copy-done.5
  36.8 0.0 copy-done.10
  36.8 9.9 %all-to-all-start = ((bf16[16,16,896]{2,1,0:T(8,128)(2,1)}), bf16[16,16,896]{2,1,0:T(8,128)(2,1)}, u32[]{:S(2)}, u32[]{:S(2)}) async-start(bf16[16,16,896]{2,1,0:T(8,128)(2,1)} %get-tuple-element.16), calls=%async_computation | async-start | bytes 917504 | tf_op jit(solution)/shard_map/all_to_all | solution.py:430
  46.8 0.0 copy-done
  46.8 0.0 copy-start.1
  46.8 3.4 %copy-done.1 = bf16[128,16,1,16,128]{4,3,2,1,0:T(8,128)(2,1)S(1)} copy-done((bf16[128,16,1,16,128]{4,3,2,1,0:T(8,128)(2,1)S(1)}, bf16[128,16,1,16,128]{4,3,2,1,0:T(8,128)(2,1)}, u32[]{:S(2)}) %copy-start.1) | copy-done | bytes 8388632
  50.2 0.0 copy-start.2
  50.2 3.8 %pair_bias.1.bias_ref = f32[16,16,8,256]{3,2,1,0:T(8,128)S(1)} custom-call(bf16[128,256,128]{2,1,0:T(8,128)(2,1)S(1)} %bitcast.19, bf16[128,128]{1,0:T(8,128)(2,1)S(1)} %broadcast_bitcast_fusion.head_ref), custom_call_target="tpu_custom_call" | custom-call | flops 1073741824 | bytes 12582912 | tf_op jit(solution)/shard_map/pair_bias/pallas_call | solution.py:385
  54.0 1.4 %all-to-all-done = bf16[16,16,896]{2,1,0:T(8,128)(2,1)} async-done(((bf16[16,16,896]{2,1,0:T(8,128)(2,1)}), bf16[16,16,896]{2,1,0:T(8,128)(2,1)}, u32[]{:S(2)}, u32[]{:S(2)}) %all-to-all-start) | async-done | bytes 458784 | tf_op jit(solution)/shard_map/all_to_all | solution.py:430
  55.4 0.0 copy-done.2
  55.4 0.0 copy-start.3
  55.4 0.9 %copy-done.3 = bf16[768,128]{1,0:T(8,128)(2,1)S(1)} copy-done((bf16[768,128]{1,0:T(8,128)(2,1)S(1)}, bf16[768,128]{1,0:T(8,128)(2,1)}, u32[]{:S(2)}) %copy-start.3) | copy-done | bytes 196632
  56.4 0.0 copy-start.13
  56.4 2.0 %copy-done.13 = bf16[768,2304]{1,0:T(8,128)(2,1)S(1)} copy-done((bf16[768,2304]{1,0:T(8,128)(2,1)S(1)}, bf16[768,2304]{1,0:T(8,128)(2,1)}, u32[]{:S(2)}) %copy-start.13) | copy-done | bytes 3538968
  58.4 5.5 %token_stage.1 = (f32[16,16,8,256]{3,2,1,0:T(8,128)S(1)}, f32[16,16,8,256]{3,2,1,0:T(8,128)S(1)}, bf16[8,16,1792]{2,1,0:T(8,128)(2,1)S(1)}) custom-call(bf16[256,896]{1,0:T(8,128)(2,1)} %bitcast.6.keys_ref, bf16[128,896]{1,0:T(8,128)(2,1)S(1)} %bitcast.20, f32[16,16,8,256]{3,2,1,0:T(8,128)S(1)} %pair_bias.1.bias_ref, bf16[768,2304]{1,0:T(8,128)(2,1)S(1)} %copy-done.13, ...), custom_call_target="tpu_custom_call" | custom-call | flops 2147483648 | bytes 12582912 | tf_op jit(solution)/shard_map/token_stage/pallas_call | solution.py:433
  63.9 14.3 %all_to_all.16.parts_ref = bf16[8,16,1792]{2,1,0:T(8,128)(2,1)S(1)} all-to-all(bf16[8,16,1792]{2,1,0:T(8,128)(2,1)S(1)} %get-tuple-element.18), channel_id=1, replica_groups=mesh['row'=16,'col'=8] {'col'}, dimensions={0} | all-to-all | bytes 917504 | tf_op jit(solution)/shard_map/all_to_all | solution.py:442
  78.2 0.0 copy-done.6
  78.2 1.0 %merge.1 = (f32[128,128]{1,0:T(8,128)S(1)}, f32[128,128]{1,0:T(8,128)S(1)}, bf16[2,16,128]{2,1,0:T(8,128)(2,1)S(1)}) custom-call(s32[1]{0:T(128)} %bitcast.2.flag_ref, bf16[8,16,1792]{2,1,0:T(8,128)(2,1)S(1)} %all_to_all.16.parts_ref, f32[16,768]{1,0:T(8,128)S(1)} %copy-done.6, bf16[768,768]{1,0:T(8,128)(2,1)S(1)} %copy-done.2, bf16[768,128]{1,0:T(8,128)(2,1)S(1)} %copy-done.3), custom_call_target="tpu_custom_call" | custom-call | flops 67108864 | bytes 2097152 | tf_op jit(solution)/shard_map/merge/pallas_call | solution.py:445
  79.2 0.0 copy-start.11
  79.2 3.0 %collective-permute-start.3 = (bf16[16,128]{1,0:T(8,128)(2,1)S(1)}, bf16[16,128]{1,0:T(8,128)(2,1)S(1)}, u32[]{:S(2)}, u32[]{:S(2)}) collective-permute-start(bf16[16,128]{1,0:T(8,128)(2,1)S(1)} %slice_bitcast_fusion), channel_id=1, source_target_pairs={{1,2},{3,4},{5,6},{7,8},{9,10},{11,12},{13,14},{15,16},{17,18},{19... | collective-permute-start | bytes 12296 | tf_op jit(solution)/shard_map/ppermute | solution.py:456
  82.2 0.1 collective-permute-start.2
  82.3 6.7 %pair_grad.1 = bf16[128,256,128]{2,1,0:T(8,128)(2,1)} custom-call(f32[16,16,8,256]{3,2,1,0:T(8,128)S(1)} %get-tuple-element.22.prob_ref, f32[16,16,8,256]{3,2,1,0:T(8,128)S(1)} %get-tuple-element.23.grad_ref, f32[128,128]{1,0:T(8,128)S(1)} %get-tuple-element.24.scale_ref, f32[128,128]{1,0:T(8,128)S(1)} %get-tuple-element.25.diag_ref, ...), custom_call_target="tpu_custom_call" | custom-call | flops 1073741824 | bytes 14680064 | tf_op jit(solution)/shard_map/pair_grad/pallas_call | solution.py:458
  89.1 0.0 copy-done.11
  89.1 0.0 collective-permute-done.3.far_ref
  89.1 0.0 copy-start.17
  89.1 0.0 collective-permute-done.2.near_ref
  89.1 0.0 copy-start.18
  89.1 0.6 copy-done.17
  89.7 0.0 copy-done.18
  89.7 1.6 %atom_out.1 = bf16[128,128]{1,0:T(8,128)(2,1)} custom-call(s32[3]{0:T(128)} %pad_add_fusion.flag_ref, bf16[16,128]{1,0:T(8,128)(2,1)} %copy-done.18, bf16[16,128]{1,0:T(8,128)(2,1)} %copy-done.17, bf16[2,16,128]{2,1,0:T(8,128)(2,1)} %copy-done.11, bf16[16,128]{1,0:T(8,128)(2,1)} %maximum_maximum_fusion.aux_ref, bf16[128,128]{1,0:T(8,128)(2,1)} %copy-done.10), custom_call_target="tpu_custom_call" | custom-call | flops 2097152 | bytes 131072 | tf_op jit(solution)/shard_map/atom_out/pallas_call | solution.py:476
  (4 shorter events, 0.0 us)
Async XLA Ops:
  0.6 46.1 %copy-start = (bf16[128,16]{0,1:T(8,128)(2,1)S(1)}, bf16[128,16]{0,1:T(8,128)(2,1)}, u32[]{:S(2)}) copy-start(bf16[128,16]{0,1:T(8,128)(2,1)} %param.27) | copy-start | bytes 12292
  5.1 6.0 %collective-permute-start = (bf16[464,128]{1,0:T(8,128)(2,1)}, bf16[464,128]{1,0:T(8,128)(2,1)S(1)}, u32[]{:S(2)}, u32[]{:S(2)}) collective-permute-start(bf16[464,128]{1,0:T(8,128)(2,1)} %get-tuple-element.14), channel_id=1, source_target_pairs={{0,1},{1,0},{2,3},{3,2},{4,5},{5,4},{6,7},{7,6},{8,9},{9,8},{10,11... | collective-permute-start | bytes 356360 | tf_op jit(solution)/shard_map/ppermute | solution.py:379
  6.5 6.4 %collective-permute-start.1 = (bf16[464,128]{1,0:T(8,128)(2,1)}, bf16[464,128]{1,0:T(8,128)(2,1)S(1)}, u32[]{:S(2)}, u32[]{:S(2)}) collective-permute-start(bf16[464,128]{1,0:T(8,128)(2,1)} %get-tuple-element.15), channel_id=1, source_target_pairs={{1,2},{3,4},{5,6},{7,8},{9,10},{11,12},{13,14},{15,16},{17,18},{19... | collective-permute-start | bytes 356360 | tf_op jit(solution)/shard_map/ppermute | solution.py:380
  12.9 0.9 copy-start.4
  13.8 0.7 copy-start.7
  14.5 0.8 copy-start.8
  15.2 0.8 copy-start.9
  16.0 0.7 copy-start.12
  16.7 0.9 %copy-start.14 = (bf16[128,768]{1,0:T(8,128)(2,1)S(1)}, bf16[128,768]{1,0:T(8,128)(2,1)}, u32[]{:S(2)}) copy-start(bf16[128,768]{1,0:T(8,128)(2,1)} %w_pool_ref.1) | copy-start | bytes 589828
  17.6 0.9 copy-start.15
  18.5 0.8 copy-start.16
  24.5 12.3 %copy-start.5 = (f32[16,768]{1,0:T(8,128)}, f32[16,768]{1,0:T(8,128)S(1)}, u32[]{:S(2)}) copy-start(f32[16,768]{1,0:T(8,128)S(1)} %get-tuple-element.19.pooled_ref) | copy-start | bytes 147460
  24.5 12.3 %copy-start.10 = (bf16[128,128]{1,0:T(8,128)(2,1)}, bf16[128,128]{1,0:T(8,128)(2,1)S(1)}, u32[]{:S(2)}) copy-start(bf16[128,128]{1,0:T(8,128)(2,1)S(1)} %get-tuple-element.21.hidden_ref) | copy-start | bytes 98308
  36.8 18.6 %all-to-all-start = ((bf16[16,16,896]{2,1,0:T(8,128)(2,1)}), bf16[16,16,896]{2,1,0:T(8,128)(2,1)}, u32[]{:S(2)}, u32[]{:S(2)}) async-start(bf16[16,16,896]{2,1,0:T(8,128)(2,1)} %get-tuple-element.16), calls=%async_computation | async-start | bytes 917504 | tf_op jit(solution)/shard_map/all_to_all | solution.py:430
  46.8 3.4 %copy-start.1 = (bf16[128,16,1,16,128]{4,3,2,1,0:T(8,128)(2,1)S(1)}, bf16[128,16,1,16,128]{4,3,2,1,0:T(8,128)(2,1)}, u32[]{:S(2)}) copy-start(bf16[128,16,1,16,128]{4,3,2,1,0:T(8,128)(2,1)} %param.21) | copy-start | bytes 25165828
  50.2 5.3 %copy-start.2 = (bf16[768,768]{1,0:T(8,128)(2,1)S(1)}, bf16[768,768]{1,0:T(8,128)(2,1)}, u32[]{:S(2)}) copy-start(bf16[768,768]{1,0:T(8,128)(2,1)} %w_out_ref.5) | copy-start | bytes 3538948
  55.4 0.9 %copy-start.3 = (bf16[768,128]{1,0:T(8,128)(2,1)S(1)}, bf16[768,128]{1,0:T(8,128)(2,1)}, u32[]{:S(2)}) copy-start(bf16[768,128]{1,0:T(8,128)(2,1)} %w_back_ref.3) | copy-start | bytes 589828
  56.4 2.0 %copy-start.13 = (bf16[768,2304]{1,0:T(8,128)(2,1)S(1)}, bf16[768,2304]{1,0:T(8,128)(2,1)}, u32[]{:S(2)}) copy-start(bf16[768,2304]{1,0:T(8,128)(2,1)} %w_qkv_ref.3) | copy-start | bytes 10616836
  58.4 19.8 %copy-start.6 = (f32[16,768]{1,0:T(8,128)S(1)}, f32[16,768]{1,0:T(8,128)}, u32[]{:S(2)}) copy-start(f32[16,768]{1,0:T(8,128)} %copy-done.5) | copy-start | bytes 147460
  79.2 9.9 %copy-start.11 = (bf16[2,16,128]{2,1,0:T(8,128)(2,1)}, bf16[2,16,128]{2,1,0:T(8,128)(2,1)S(1)}, u32[]{:S(2)}) copy-start(bf16[2,16,128]{2,1,0:T(8,128)(2,1)S(1)} %get-tuple-element.20.low_ref) | copy-start | bytes 24580
  79.2 9.9 %collective-permute-start.3 = (bf16[16,128]{1,0:T(8,128)(2,1)S(1)}, bf16[16,128]{1,0:T(8,128)(2,1)S(1)}, u32[]{:S(2)}, u32[]{:S(2)}) collective-permute-start(bf16[16,128]{1,0:T(8,128)(2,1)S(1)} %slice_bitcast_fusion), channel_id=1, source_target_pairs={{1,2},{3,4},{5,6},{7,8},{9,10},{11,12},{13,14},{15,16},{17,18},{19... | collective-permute-start | bytes 12296 | tf_op jit(solution)/shard_map/ppermute | solution.py:456
  82.2 6.9 %collective-permute-start.2 = (bf16[16,128]{1,0:T(8,128)(2,1)S(1)}, bf16[16,128]{1,0:T(8,128)(2,1)S(1)}, u32[]{:S(2)}, u32[]{:S(2)}) collective-permute-start(bf16[16,128]{1,0:T(8,128)(2,1)S(1)} %slice_bitcast_fusion), channel_id=1, source_target_pairs={{0,1},{1,0},{2,3},{3,2},{4,5},{5,4},{6,7},{7,6},{8,9},{9,8},{10,11... | collective-permute-start | bytes 12296 | tf_op jit(solution)/shard_map/ppermute | solution.py:455
  89.1 0.6 copy-start.17
  89.1 0.6 copy-start.18

commit v2 on v1

v2 whole, which is shorter than its diff:
```python
import functools
import math

import jax
import jax.numpy as jnp
from jax import lax
from jax.experimental import pallas as pl
from jax.experimental.pallas import tpu as pltpu
from jax.sharding import PartitionSpec as P

HA = 4
HT = 16
QB = 32
KW = 128
SHIFT = 16
HALF = 64
EARLY = 8
GROUP = 8
AUX = 16
EPSILON = 1e-05
LOWEST = -1e30
F32 = jnp.float32
BF16 = jnp.bfloat16
NT = (((1,), (1,)), ((), ()))
TN = (((0,), (0,)), ((), ()))

VMEM = pl.BlockSpec(memory_space=pltpu.VMEM)
HBM = pl.BlockSpec(memory_space=pltpu.HBM)
SMEM = pl.BlockSpec(memory_space=pltpu.SMEM)


def params(mib):
    return pltpu.CompilerParams(vmem_limit_bytes=mib << 20)


def outside(value):
    return pltpu.with_memory_space_constraint(value, pltpu.HBM)


def inside(value):
    return pltpu.with_memory_space_constraint(value, pltpu.VMEM)


def place():
    return lax.axis_index("row"), lax.axis_index("col")


def iota(shape, dim):
    return lax.broadcasted_iota(jnp.int32, shape, dim)


def dot(a, b, dims=None):
    if dims is None:
        return jnp.dot(a, b, preferred_element_type=F32)
    return lax.dot_general(a, b, dims, preferred_element_type=F32)


def normal(values):
    centred = values - jnp.mean(values, axis=-1, keepdims=True)
    return centred * lax.rsqrt(jnp.mean(centred * centred, axis=-1, keepdims=True) + EPSILON)


def split(values):
    high = values.astype(BF16)
    return high, (values - high.astype(F32)).astype(BF16)


def grouped_weight(head_rows, member):
    rows = iota(head_rows.shape, 0)
    return jnp.where(rows % GROUP == member, head_rows, 0.0).astype(BF16)


def pair_bias_kernel(first, pair_ref, head_ref, out_ref, tile_ref, arrived):
    groups = out_ref.shape[0]
    window = min(8, groups)

    def copy(g):
        rows = pl.ds(g * GROUP, GROUP)
        here = pl.ds((g + first) * GROUP, GROUP)
        return pltpu.make_async_copy(pair_ref.at[here], tile_ref.at[rows], arrived.at[g])

    for g in range(window):
        copy(g).start()
    weight = head_ref[...].astype(F32).reshape(HT, GROUP, 128)[:, 0].astype(BF16)

    def step(g, carry):
        copy(g).wait()
        if window < groups:

            @pl.when(g + window < groups)
            def _():
                copy(g + window).start()

        for i in range(GROUP):
            out_ref[g, :, i, :] = dot(weight, tile_ref[g * GROUP + i], NT)
        return carry

    lax.fori_loop(0, groups, step, 0)


def pack_kernel(shift_ref, atoms_ref, bias_ref, cot_ref, token_ref, near_ref, far_ref):
    row, col = place()
    odd = lax.rem(col, 2)
    line = iota((AUX, 128), 0)
    device = row * lax.axis_size("col") + col
    aux = jnp.where(line == 0, token_ref[...] - (16 * device - 17), 0)
    for n in range(4):
        aux = jnp.where(line == 1 + n, shift_ref[n], aux)
    aux = aux.astype(F32).astype(BF16)

    def fill(out_ref, at):
        out_ref[0:128] = atoms_ref[...]
        for h in range(HA):
            out_ref[128 + HALF * h : 128 + HALF * (h + 1)] = bias_ref[h, at : at + HALF]
        out_ref[384:448] = cot_ref[at : at + HALF]
        out_ref[448:464] = aux

    @pl.when(odd == 1)
    def _():
        fill(near_ref, 0)
        fill(far_ref, HALF)

    @pl.when(odd == 0)
    def _():
        fill(near_ref, HALF)
        fill(far_ref, 0)


def atom_kernel(
    shift_ref,
    count_ref,
    mask_ref,
    near_ref,
    far_ref,
    atoms_ref,
    bias_ref,
    cot_ref,
    token_ref,
    after_ref,
    w_qkv_ref,
    w_out_ref,
    w_pool_ref,
    token_out_ref,
    back_ref,
    hidden_ref,
    pooled_ref,
    to_row_ref,
    to_col_ref,
    inner_out_ref,
    inner_back_ref,
    prev_ref,
    next_ref,
    arrived,
):
    pairs = (
        (token_out_ref, inner_out_ref),
        (back_ref, inner_back_ref),
    )
    copies = [pltpu.make_async_copy(a, b, arrived.at[n]) for n, (a, b) in enumerate(pairs)]
    for copy in copies:
        copy.start()
    row, col = place()
    odd = lax.rem(col, 2)
    device = row * lax.axis_size("col") + col
    atom_count = 128 * lax.axis_size("row") * lax.axis_size("col")

    @pl.when(odd == 1)
    def _():
        prev_ref[...] = near_ref[...]
        next_ref[...] = far_ref[...]

    @pl.when(odd == 0)
    def _():
        prev_ref[...] = far_ref[...]
        next_ref[...] = near_ref[...]

    first = device * 128
    extended = jnp.concatenate([prev_ref[0:128], atoms_ref[...], next_ref[0:128]], axis=0)
    wide = extended.astype(F32)
    project = dot(normal(wide).astype(BF16), w_qkv_ref[...]).astype(BF16)
    head_lane = iota((QB, 128), 1) // 32
    head_mask = [jnp.where(head_lane == h, 1.0, 0.0) for h in range(HA)]
    slot = iota((1, KW), 1)
    offset = iota((KW, 160), 1) - iota((KW, 160), 0) - SHIFT
    order = (2, 3, 4, 5, 6, 7, 0, 1)
    biases, shifts, windows, stacks = [], [], [], []
    for block in order:
        if block < 2:
            source, local = prev_ref, block
            shift = prev_ref[451 + local : 452 + local].astype(F32).astype(jnp.int32)
        elif block > 5:
            source, local = next_ref, block - 6
            shift = next_ref[449 + local : 450 + local].astype(F32).astype(jnp.int32)
        else:
            source, local = None, block - 2
            shift = jnp.full((1, 128), shift_ref[local], jnp.int32)
        for h in range(HA):
            if source is None:
                biases.append(bias_ref[h, 32 * local : 32 * local + 32])
            else:
                at = 128 + HALF * h + 32 * local
                biases.append(source[at : at + 32])
        shifts.append(shift)
    for block, shift in zip(order, shifts):
        pick = jnp.where(offset == shift[:, 0:1], 1.0, 0.0).astype(BF16)
        windows.append(dot(pick, project[32 * block : 32 * block + 160, 128:]).astype(BF16))
        query = project[64 + 32 * block : 96 + 32 * block, :128].astype(F32)
        stacks.append(
            jnp.concatenate([query * head_mask[h] for h in range(HA)], axis=0).astype(BF16)
        )
    scores = [
        dot(stack, window[:, :128], NT) * (1.0 / math.sqrt(32))
        for stack, window in zip(stacks, windows)
    ]
    weights = []
    for n, block in enumerate(order):
        score = scores[n] + jnp.concatenate(biases[HA * n : HA * n + HA], axis=0).astype(F32)
        position = slot + (first + 32 * block - 112) + shifts[n]
        inside = (position >= 0) & (position < atom_count)
        score = jnp.where(inside, score, LOWEST)
        raised = jnp.exp(score - jnp.max(score, axis=-1, keepdims=True))
        weights.append((raised / jnp.sum(raised, axis=-1, keepdims=True)).astype(BF16))
    mixes = []
    for weight, window in zip(weights, windows):
        mixed = dot(weight, window[:, 128:])
        mix = mixed[0:32] * head_mask[0]
        for h in range(1, HA):
            mix = mix + mixed[32 * h : 32 * h + 32] * head_mask[h]
        mixes.append(mix)
    mixture = jnp.concatenate(mixes, axis=0).astype(BF16)
    base = jnp.concatenate([wide[128:320], wide[64:128]], axis=0)
    hidden = (base + dot(mixture, w_out_ref[...])).astype(BF16)
    hidden_ref[...] = hidden[:128]
    lifted = jnp.maximum(dot(hidden, w_pool_ref[...]), 0.0)
    own_token = (token_ref[...] - 16 * device).astype(F32)
    prev_token = prev_ref[448:449].astype(F32) - 33.0
    next_token = next_ref[448:449].astype(F32) - 1.0
    beside = jnp.where(iota((1, 128), 1) < HALF, next_token, prev_token)
    token = jnp.concatenate([own_token, beside], axis=1)
    select = jnp.where(iota((16, 256), 0).astype(F32) == token, 1.0, 0.0).astype(BF16)
    high, low = split(lifted)
    line = iota((16, 128), 0)
    count = jnp.zeros((16, 128), jnp.int32)
    live = jnp.zeros((16, 128), jnp.int32)
    for t in range(16):
        count = jnp.where(line == t, count_ref[t], count)
        live = jnp.where(line == t, mask_ref[t], live)
    count = jnp.concatenate([count.astype(F32)] * 6, axis=1)
    pooled = (dot(select, high) + dot(select, low)) / count
    pooled_ref[...] = pooled
    normed = normal(pooled).astype(BF16)
    cot = jnp.concatenate([cot_ref[...], next_ref[384:448], prev_ref[384:448]], axis=0)
    grad_up = dot(select, cot).astype(BF16)
    live = live.astype(F32).astype(BF16)
    for r in range(to_row_ref.shape[0]):
        to_row_ref[r, :, :768] = normed
        to_row_ref[r, :, 768:] = live
    to_col_ref[:, :768] = normed
    to_col_ref[:, 768:] = grad_up
    for copy in copies:
        copy.wait()


def window_of(head):
    block, rest = divmod(head, 8)
    return 384 * block + (0 if rest < 5 else 128)


def stack_kernel(first_ref, second_ref, third_ref, fourth_ref, out_ref):
    for n, part in enumerate((first_ref, second_ref, third_ref, fourth_ref)):
        out_ref[n] = part[...]


def token_kernel(
    keys_ref,
    own_ref,
    partner_ref,
    early_ref,
    late_ref,
    w_qkv_ref,
    w_out_ref,
    w_back_ref,
    prob_ref,
    grad_ref,
    stats_ref,
    keep_ref,
    give_ref,
    rows_ref,
    inner_ref,
    mixed_ref,
    arrived,
):
    copies = []
    for n in range(6):
        rows = slice(128 * n, 128 * (n + 1))
        copies.append(
            pltpu.make_async_copy(w_qkv_ref.at[rows], inner_ref.at[rows], arrived.at[n])
        )
    for copy in copies:
        copy.start()
    row, col = place()
    chip, core = lax.div(col, 2), lax.rem(col, 2)
    for s in range(4):
        there = lax.rem(chip + 4 - s, 4) * 32
        rows_ref[pl.ds(pl.multiple_of(there + core * 16, 16), 16)] = own_ref[s]
        rows_ref[pl.ds(pl.multiple_of(there + 16 - core * 16, 16), 16)] = partner_ref[s]
    middle = dot(rows_ref[:, 768:], w_back_ref[...], NT).astype(BF16)
    grad = dot(middle, w_out_ref[...], NT).astype(BF16)
    for copy in copies:
        copy.wait()
    query = dot(rows_ref[:, :768], inner_ref[:, :768]).astype(BF16)
    key = dot(keys_ref[:, :768], inner_ref[:, 768:1536]).astype(BF16)
    value = dot(keys_ref[:, :768], inner_ref[:, 1536:]).astype(BF16)
    live = keys_ref[:, 768:].astype(F32).T[0:1]
    closed = jnp.where(live > 0, 0.0, -jnp.inf)
    lane = iota((128, 256), 1)
    stat_lane = iota((128, 128), 1)

    def within(h):
        at = window_of(h)
        return (lane >= 48 * h - at) & (lane < 48 * (h + 1) - at)

    for h in range(HT):
        at = window_of(h)
        query_h = jnp.where(within(h), query[:, at : at + 256].astype(F32), 0.0).astype(BF16)
        scores = dot(query_h, key[:, at : at + 256], NT) * (1.0 / math.sqrt(48))
        bias = jnp.concatenate([early_ref[:, h], late_ref[:, h]], axis=0).reshape(128, 256)
        prob_ref[:, h] = (scores + bias + closed).reshape(16, GROUP, 256)
    for h in range(HT):
        at = window_of(h)
        grad_h = jnp.where(within(h), grad[:, at : at + 256].astype(F32), 0.0).astype(BF16)
        grads = dot(grad_h, value[:, at : at + 256], NT)
        grad_ref[:, h] = grads.reshape(16, GROUP, 256)
    tops = jnp.zeros((128, 128), F32)
    sums = jnp.zeros((128, 128), F32)
    diags = jnp.zeros((128, 128), F32)
    for h in range(HT):
        scores = prob_ref[:, h].reshape(128, 256)
        top = jnp.maximum(jnp.max(scores, axis=-1, keepdims=True), LOWEST)
        high = top.astype(BF16).astype(F32)
        top = high + (top - high).astype(BF16).astype(F32)
        raised = jnp.exp(scores - top)
        prob_ref[:, h] = raised.reshape(16, GROUP, 256)
        total = jnp.sum(raised, axis=-1, keepdims=True)
        diag = jnp.sum(raised * grad_ref[:, h].reshape(128, 256), axis=-1, keepdims=True)
        here = stat_lane == h
        tops = jnp.where(here, top, tops)
        sums = jnp.where(here, total, sums)
        diags = jnp.where(here, diag, diags)
    for at in (0, 128, 384, 512):
        out = None
        for h in range(HT):
            if window_of(h) == at:
                raised = prob_ref[:, h].reshape(128, 256).astype(BF16)
                part = jnp.where(within(h), dot(raised, value[:, at : at + 256]), 0.0)
                out = part if out is None else out + part
        if at % 384 == 0:
            mixed_ref[:, at : at + 256] = out
        else:
            mixed_ref[:, at : at + 128] = mixed_ref[:, at : at + 128] + out[:, :128]
            mixed_ref[:, at + 128 : at + 256] = out[:, 128:]
    stats_ref[...] = tops + pltpu.roll(sums, 32, axis=1) + pltpu.roll(diags, 64, axis=1)
    packed = packed_stats(tops, sums, diags)
    for n in range(4):
        there = 32 * n + 16 * core
        keep_ref[n] = mixed_ref[pl.ds(pl.multiple_of(there, 16), 16)]
        there = 32 * n + 16 - 16 * core
        part = mixed_ref[pl.ds(pl.multiple_of(there, 16), 16)]
        give_ref[n, :, :768] = part.astype(BF16)
        for k in range(2):
            at = 32 * n + 16 * k
            give_ref[n, :, 768 + 128 * k : 896 + 128 * k] = packed[at : at + 16]


def packed_stats(tops, sums, diags):
    stats = jnp.zeros((128, 128), F32)
    for k, part in enumerate((tops, sums, diags)):
        high = part.astype(BF16).astype(F32)
        for n, piece in enumerate((high, part - high)):
            turn = 32 * k + 16 * n
            stats = stats + (pltpu.roll(piece, turn, axis=1) if turn else piece)
    return stats.astype(BF16)


def spread_heads(factors):
    spread = jnp.where(iota((128, 768), 1) // 48 == iota((128, 768), 0), 1.0, 0.0).astype(BF16)
    high, low = split(factors)
    return dot(high, spread) + dot(low, spread)


def parted_stats(stats):
    lane = iota((128, 128), 1)
    parts = [stats, pltpu.roll(stats, 96, axis=1), pltpu.roll(stats, 64, axis=1)]
    return [jnp.where(lane < HT, part, 0.0) for part in parts]


def fold_kernel(
    keep_ref,
    stats_ref,
    given_ref,
    first_ref,
    second_ref,
    third_ref,
    own_ref,
    joint_ref,
    ratio_ref,
    mixed_ref,
):
    row, col = place()
    chip, core = lax.div(col, 2), lax.rem(col, 2)
    given = jnp.concatenate(
        [given_ref[n, :, 768 + 128 * k : 896 + 128 * k] for n in range(4) for k in range(2)],
        axis=0,
    ).astype(F32)
    given = given + pltpu.roll(given, 112, axis=1)
    sides = [parted_stats(stats_ref[...]), parted_stats(given)]
    top = jnp.maximum(sides[0][0], sides[1][0])
    ratios = [jnp.exp(side[0] - top) for side in sides]
    total = ratios[0] * sides[0][1] + ratios[1] * sides[1][1]
    diag = ratios[0] * sides[0][2] + ratios[1] * sides[1][2]
    joint_ref[...] = top + pltpu.roll(total, 32, axis=1) + pltpu.roll(diag, 64, axis=1)
    ratio_ref[0] = ratios[0]
    ratio_ref[1] = ratios[1]
    rows = [pl.ds(pl.multiple_of(32 * n + 16 * core, 16), 16) for n in range(4)]
    factors = spread_heads(
        jnp.concatenate([ratio_ref[side, rows[n]] for side in range(2) for n in range(4)], axis=0)
    )
    for n in range(4):
        given_n = given_ref[n, :, :768].astype(F32)
        mixed_ref[n] = (
            keep_ref[n] * factors[16 * n : 16 * n + 16]
            + given_n * factors[64 + 16 * n : 80 + 16 * n]
        )
    packed = packed_stats(top, total, diag)
    for s, out_ref in enumerate((first_ref, second_ref, third_ref)):
        out_ref[:, :768] = mixed_ref[lax.rem(chip + s + 1, 4)].astype(BF16)
        for k in range(8):
            out_ref[:, 768 + 128 * k : 896 + 128 * k] = packed[16 * k : 16 * k + 16]
    own_ref[...] = mixed_ref[chip]


def merge_kernel(
    stats_ref,
    own_ref,
    joint_ref,
    first_ref,
    second_ref,
    third_ref,
    pooled_ref,
    w_out_ref,
    w_back_ref,
    scale_ref,
    diag_ref,
    low_ref,
    ratio_ref,
):
    row, col = place()
    lane = iota((128, 128), 1)
    sides = [parted_stats(joint_ref[...])]
    for part_ref in (first_ref, second_ref, third_ref):
        stats = jnp.concatenate(
            [part_ref[:, 768 + 128 * k : 896 + 128 * k] for k in range(8)], axis=0
        ).astype(F32)
        sides.append(parted_stats(stats + pltpu.roll(stats, 112, axis=1)))
    top = functools.reduce(jnp.maximum, [side[0] for side in sides])
    ratios = [jnp.exp(side[0] - top) for side in sides]
    total = functools.reduce(jnp.add, [r * side[1] for r, side in zip(ratios, sides)])
    diag = functools.reduce(jnp.add, [r * side[2] for r, side in zip(ratios, sides)])
    inverse = 1.0 / jnp.where(lane < HT, total, 1.0)
    for n in range(4):
        ratio_ref[n] = ratios[n] * inverse
    own_top = parted_stats(stats_ref[...])[0]
    scale_ref[...] = jnp.exp(own_top - top) * inverse
    diag_ref[...] = diag * inverse
    rows = pl.ds(pl.multiple_of(col * 16, 16), 16)
    factors = spread_heads(jnp.concatenate([ratio_ref[n, rows] for n in range(4)], axis=0))
    mixed = own_ref[...] * factors[0:16]
    for n, part_ref in enumerate((first_ref, second_ref, third_ref)):
        mixed = mixed + part_ref[:, :768].astype(F32) * factors[16 * n + 16 : 16 * n + 32]
    updated = (pooled_ref[...] + dot(mixed.astype(BF16), w_out_ref[...])).astype(BF16)
    high, low = split(dot(updated, w_back_ref[...]))
    low_ref[0] = high
    low_ref[1] = low


def pair_grad_kernel(prob_ref, grad_ref, scale_ref, diag_ref, head_ref, out_ref, tile_ref, left):
    groups = prob_ref.shape[0]

    def copy(g):
        rows = pl.ds(g * GROUP, GROUP)
        return pltpu.make_async_copy(tile_ref.at[rows], out_ref.at[rows], left.at[g])

    head_rows = head_ref[...].astype(F32)
    weights = jnp.concatenate([grouped_weight(head_rows, i) for i in range(GROUP)], axis=1)

    def score_of(g):
        rows = pl.ds(pl.multiple_of(g * GROUP, GROUP), GROUP)
        scale = scale_ref[rows]
        diag = diag_ref[rows]
        score = jnp.concatenate(
            [
                prob_ref[g, h] * scale[:, h : h + 1] * (grad_ref[g, h] - diag[:, h : h + 1])
                for h in range(HT)
            ],
            axis=0,
        )
        return score.T.astype(BF16)

    def step(g, score):
        following = score_of(jnp.minimum(g + 1, groups - 1))
        result = dot(score, weights)
        for i in range(GROUP):
            tile_ref[g * GROUP + i] = result[:, 128 * i : 128 * (i + 1)].astype(BF16)
        copy(g).start()
        return following

    lax.fori_loop(0, groups, step, score_of(0), unroll=2)
    for g in range(groups):
        copy(g).wait()


def atom_out_kernel(near_ref, far_ref, low_ref, token_ref, hidden_ref, out_ref):
    row, col = place()
    odd = lax.rem(col, 2) == 1
    device = row * lax.axis_size("col") + col
    near = near_ref[...].astype(F32)
    far = far_ref[...].astype(F32)
    before = jnp.where(odd, near, far).astype(BF16)
    after = jnp.where(odd, far, near).astype(BF16)
    rows = jnp.concatenate([before, low_ref[0], after, low_ref[1]], axis=0)
    token = (token_ref[...] - (16 * device - 16)).astype(F32)
    index = iota((64, 128), 0)
    index = jnp.where(index < 48, index, index - 32).astype(F32)
    select = jnp.where(index == token, 1.0, 0.0).astype(BF16)
    out_ref[...] = (hidden_ref[...].astype(F32) + dot(select, rows, TN)).astype(BF16)


def shards(
    atoms,
    atom_bias,
    key_shift,
    atom_token,
    token_atoms,
    token_mask,
    pair,
    w_atom_qkv,
    w_atom_out,
    w_pool,
    w_token_qkv,
    w_token_out,
    w_bias,
    w_back,
    cotangent,
):
    row_count, col_count = lax.axis_size("row"), lax.axis_size("col")
    devices = row_count * col_count
    core_pairs = [(i, i ^ 1) for i in range(col_count)]
    chip_pairs = [(i, i + 1) for i in range(1, devices - 1, 2)]
    chip_pairs = chip_pairs + [(j, i) for i, j in chip_pairs]

    def chip_shift(steps):
        return [(i, (i + 2 * steps) % col_count) for i in range(col_count)]

    tokens = atom_token.reshape(1, 128)
    payload = jax.ShapeDtypeStruct((464, 128), BF16)
    near, far = pl.pallas_call(
        pack_kernel,
        in_specs=[SMEM] + [VMEM] * 4,
        out_specs=[VMEM, VMEM],
        out_shape=[payload, payload],
        compiler_params=params(4),
        name="pack",
        cost_estimate=pl.CostEstimate(flops=0, bytes_accessed=1 << 20, transcendentals=0),
    )(
        outside(key_shift),
        outside(atoms),
        outside(atom_bias),
        outside(cotangent),
        outside(tokens),
    )
    near = lax.ppermute(near, "col", core_pairs)
    far = lax.ppermute(far, ("row", "col"), chip_pairs)

    tile = pair.reshape(128, 256, 128)
    head_rows = jnp.repeat(jnp.transpose(w_bias), GROUP, axis=0)
    def pair_bias(first, groups, name):
        return pl.pallas_call(
            functools.partial(pair_bias_kernel, first),
            in_specs=[HBM, VMEM],
            out_specs=VMEM,
            out_shape=pltpu.VMEM((groups, HT, GROUP, 256), F32),
            scratch_shapes=[
                pltpu.VMEM((groups * GROUP, 256, 128), BF16),
                pltpu.SemaphoreType.DMA((groups,)),
            ],
            compiler_params=params(14),
            name=name,
            cost_estimate=pl.CostEstimate(
                flops=groups << 26, bytes_accessed=groups << 19, transcendentals=0
            ),
        )(outside(tile), head_rows)

    half = EARLY
    early = pair_bias(0, half, "pair_bias_early")
    late = pair_bias(half, 16 - half, "pair_bias_late")

    hidden, pooled, to_row, to_col, token_out, back = pl.pallas_call(
        atom_kernel,
        in_specs=[SMEM] * 3 + [VMEM] * 6 + [pl.BlockSpec(memory_space=pl.ANY)] + [VMEM] * 3 + [HBM] * 2,
        out_specs=[VMEM] * 6,
        out_shape=[
            pltpu.VMEM((128, 128), BF16),
            pltpu.HBM((16, 768), F32),
            pltpu.HBM((row_count, 16, 896), BF16),
            pltpu.HBM((16, 896), BF16),
            pltpu.VMEM(w_token_out.shape, BF16),
            pltpu.VMEM(w_back.shape, BF16),
        ],
        scratch_shapes=[
            pltpu.VMEM((464, 128), BF16),
            pltpu.VMEM((464, 128), BF16),
            pltpu.SemaphoreType.DMA((2,)),
        ],
        compiler_params=params(8),
        name="atom_stage",
        cost_estimate=pl.CostEstimate(flops=1 << 28, bytes_accessed=2 << 20, transcendentals=1 << 17),
    )(
        outside(key_shift),
        outside(token_atoms),
        outside(token_mask),
        near,
        far,
        outside(atoms),
        outside(atom_bias),
        outside(cotangent),
        outside(tokens),
        inside(early),
        outside(w_atom_qkv),
        outside(w_atom_out),
        outside(w_pool),
        outside(w_token_out),
        outside(w_back),
    )
    shifted = [lax.ppermute(to_col, "col", chip_shift(s)) for s in range(1, 4)]
    keys = lax.all_to_all(to_row, "row", 0, 0).reshape(256, 896)
    own = pl.pallas_call(
        stack_kernel,
        in_specs=[VMEM] * 4,
        out_specs=VMEM,
        out_shape=pltpu.HBM((4, 16, 896), BF16),
        compiler_params=params(4),
        name="stack",
        cost_estimate=pl.CostEstimate(flops=1 << 32, bytes_accessed=1 << 18, transcendentals=0),
    )(outside(to_col), *shifted)
    partner = lax.ppermute(own, "col", core_pairs)

    stat = pltpu.VMEM((128, 128), F32)
    swapped = jax.ShapeDtypeStruct((4, 16, 1024), BF16)
    folded = jax.ShapeDtypeStruct((16, 1792), BF16)
    table = pltpu.VMEM((16, HT, GROUP, 256), F32)
    prob, grad, stats, keep, give = pl.pallas_call(
        token_kernel,
        in_specs=[VMEM] * 5 + [HBM] + [VMEM] * 2,
        out_specs=[VMEM] * 5,
        scratch_shapes=[
            pltpu.VMEM((128, 896), BF16),
            pltpu.VMEM((768, 2304), BF16),
            pltpu.VMEM((128, 768), F32),
            pltpu.SemaphoreType.DMA((6,)),
        ],
        out_shape=[table, table, stat, pltpu.VMEM((4, 16, 768), F32), swapped],
        compiler_params=params(16),
        name="token_stage",
        cost_estimate=pl.CostEstimate(flops=1 << 31, bytes_accessed=12 << 20, transcendentals=1 << 19),
    )(
        outside(keys),
        outside(own),
        outside(partner),
        inside(early),
        inside(late),
        outside(w_token_qkv),
        inside(token_out),
        inside(back),
    )
    given = lax.ppermute(give, "col", core_pairs)
    *sent, mixed, joint = pl.pallas_call(
        fold_kernel,
        in_specs=[VMEM] * 3,
        out_specs=[VMEM] * 5,
        out_shape=[folded, folded, folded, pltpu.VMEM((16, 768), F32), stat],
        scratch_shapes=[pltpu.VMEM((2, 128, 128), F32), pltpu.VMEM((4, 16, 768), F32)],
        compiler_params=params(6),
        name="fold",
        cost_estimate=pl.CostEstimate(flops=1 << 26, bytes_accessed=2 << 20, transcendentals=1 << 17),
    )(inside(keep), inside(stats), given)
    parts = [lax.ppermute(part, "col", chip_shift(s + 1)) for s, part in enumerate(sent)]

    scale, diag, low = pl.pallas_call(
        merge_kernel,
        in_specs=[VMEM] * 9,
        out_specs=[VMEM] * 3,
        out_shape=[stat, stat, pltpu.VMEM((2, 16, 128), BF16)],
        scratch_shapes=[pltpu.VMEM((4, 128, 128), F32)],
        compiler_params=params(6),
        name="merge",
        cost_estimate=pl.CostEstimate(flops=1 << 26, bytes_accessed=2 << 20, transcendentals=1 << 17),
    )(
        inside(stats),
        inside(mixed),
        inside(joint),
        *parts,
        outside(pooled),
        inside(token_out),
        inside(back),
    )
    near = lax.ppermute(low[0], "col", core_pairs)
    far = lax.ppermute(low[0], ("row", "col"), chip_pairs)

    pair_grad = pl.pallas_call(
        pair_grad_kernel,
        in_specs=[VMEM] * 5,
        out_specs=HBM,
        out_shape=jax.ShapeDtypeStruct((128, 256, 128), BF16),
        scratch_shapes=[pltpu.VMEM((128, 256, 128), BF16), pltpu.SemaphoreType.DMA((16,))],
        compiler_params=params(14),
        name="pair_grad",
        cost_estimate=pl.CostEstimate(
            flops=2 * 128 * 256 * 128 * 16 * 8, bytes_accessed=14 << 20, transcendentals=0
        ),
    )(inside(prob), inside(grad), inside(scale), inside(diag), head_rows)
    atom_out = pl.pallas_call(
        atom_out_kernel,
        in_specs=[VMEM] * 5,
        out_specs=VMEM,
        out_shape=jax.ShapeDtypeStruct((128, 128), BF16),
        compiler_params=params(4),
        name="atom_out",
        cost_estimate=pl.CostEstimate(flops=1 << 21, bytes_accessed=1 << 17, transcendentals=0),
    )(near, far, inside(low), outside(tokens), inside(hidden))
    return (atom_out, pair_grad.reshape(pair.shape))


def solution(mesh):
    return jax.shard_map(
        shards,
        mesh=mesh,
        in_specs=(
            P(("row", "col"), None),
            P(None, ("row", "col"), None),
            P(("row", "col")),
            P(("row", "col")),
            P(("row", "col")),
            P(("row", "col")),
            P("row", None, "col", None, None),
            P(),
            P(),
            P(),
            P(),
            P(),
            P(),
            P(),
            P(("row", "col"), None),
        ),
        out_specs=(P(("row", "col"), None), P("row", None, "col", None, None)),
        check_vma=False,
    )
```

time: 92.2 us -> 65.3 us (0.71)
  blocking collectives: 26.6 us -> 0 us
  local copies, waits for them, and re-layouts: 14.9 us -> 0.02 us
  starting transfers between devices: 17.5 us -> 30.1 us
  waiting for transfers between devices: 3.19 us -> 6.97 us
  other arithmetic: 2.65 us -> 0 us
  Pallas kernels: 25.6 us -> 27 us
    all_to_all x2 -> x0, blocking collectives: 26.6 us -> none  [the longest x1 14.3 us: shards(): parts = lax.all_to_all(to_col, 'col', 0, 0)]
    unnamed x38 -> x2, local copies, waits for them, and re-layouts: 13.3 us -> 0.01 us
    ppermute x0 -> x8, starting transfers between devices: none -> 10.9 us  [the longest x3 5.7 us: shards(): lax.ppermute(part, 'col', chip_shift(s + 1))]
    all_to_all x1, waiting for transfers between devices: 1.39 us -> 4.27 us  [shards(): keys = lax.all_to_all(to_row, 'row', 0, 0).reshape(256, 896)]
    ppermute x0 -> x8, waiting for transfers between devices: none -> 2.69 us  [the longest x3 1.34 us: shards(): lax.ppermute(part, 'col', chip_shift(s + 1))]
    ppermute x1, waiting for transfers between devices: 1.8 us -> 0.01 us  [shards(): far = lax.ppermute(far, ('row', 'col'), chip_pairs)]
    ppermute x1, starting transfers between devices: 3.03 us -> 4.52 us  [shards(): far = lax.ppermute(low[0], ('row', 'col'), chip_pairs)]
    broadcast_in_dim x3 -> x0, local copies, waits for them, and re-layouts: 1.47 us -> none  [the longest x1 0.73 us: shards(): token_atoms[:, None]]
  transfers between devices with their start and end apart: 5 -> 13, of which waited for: 2 -> 4; matrix products, arithmetic and copies ran while one was open for 2% -> 0% of each run, Pallas kernels for 12% -> 19%
where the time goes in v2:
time: 65.3 us; the launch traced here: 64.9 us
  starting transfers between devices  30.1 us (46%)
  Pallas kernels  27 us (41%)
  waiting for transfers between devices  6.97 us (11%)
  between operations  0.82 us (1%)
    all_to_all x1, starting transfers between devices, shards(): keys = lax.all_to_all(to_row, 'row', 0, 0).reshape(256, 896)  9.92 us
    pallas_call x2, Pallas kernels, pair_bias(): pl.pallas_call(functools.partial(pair_bias_kernel, first), in_specs=[HBM,...  6.45 us
    pallas_call x1, Pallas kernels, shards(): pl.pallas_call(token_kernel, in_specs=[VMEM] * 5 + [HBM] + [VMEM] * 2, ou...  6.13 us
    ppermute x3, starting transfers between devices, shards(): lax.ppermute(part, 'col', chip_shift(s + 1))  5.7 us
    ppermute x3, starting transfers between devices, shards(): shifted = [lax.ppermute(to_col, 'col', chip_shift(s)) for s in range(1, 4)]  5.15 us
    pallas_call x1, Pallas kernels, shards(): pl.pallas_call(pair_grad_kernel, in_specs=[VMEM] * 5, out_specs=HBM, out_...  4.71 us
    ppermute x1, starting transfers between devices, shards(): far = lax.ppermute(low[0], ('row', 'col'), chip_pairs)  4.52 us
    all_to_all x1, waiting for transfers between devices, shards(): keys = lax.all_to_all(to_row, 'row', 0, 0).reshape(256, 896)  4.27 us
  transfers between devices with their start and end apart: 13, of which 4 were waited for; matrix products, arithmetic and copies ran while one was open for 0% of the time, Pallas kernels for 19%

profile of v2, /device:TPU:1, one launch (start us, length us, event | category | flops | bytes accessed | tf_op | source)
XLA Modules:
  0.0 64.9 jit_solution(209044920261553941)
XLA Ops:
  0.6 0.0 copy-start
  0.6 1.0 %pack.1 = (bf16[464,128]{1,0:T(8,128)(2,1)S(1)}, bf16[464,128]{1,0:T(8,128)(2,1)S(1)}) custom-call(s32[4]{0:T(128)} %shift_ref.3, bf16[128,128]{1,0:T(8,128)(2,1)} %atoms_ref.3, bf16[4,128,128]{2,1,0:T(8,128)(2,1)} %bias_ref.3, bf16[128,128]{1,0:T(8,128)(2,1)} %cot_ref.3, s32[1,128]{1,0:T(1,128)} %bitcast.15), custom_call_target="tpu_custom_call" | custom-call | bytes 1048576 | tf_op jit(solution)/shard_map/pack/pallas_call | solution.py:566
  1.6 1.5 %collective-permute-start = (bf16[464,128]{1,0:T(8,128)(2,1)S(1)}, bf16[464,128]{1,0:T(8,128)(2,1)S(1)}, u32[]{:S(2)}, u32[]{:S(2)}) collective-permute-start(bf16[464,128]{1,0:T(8,128)(2,1)S(1)} %get-tuple-element.23), channel_id=1, source_target_pairs={{0,1},{1,0},{2,3},{3,2},{4,5},{5,4},{6,7},{7,6},{8,9},{9,8},{10,11... | collective-permute-start | bytes 356360 | tf_op jit(solution)/shard_map/ppermute | solution.py:581
  3.1 3.1 %collective-permute-start.1 = (bf16[464,128]{1,0:T(8,128)(2,1)S(1)}, bf16[464,128]{1,0:T(8,128)(2,1)S(1)}, u32[]{:S(2)}, u32[]{:S(2)}) collective-permute-start(bf16[464,128]{1,0:T(8,128)(2,1)S(1)} %get-tuple-element.24), channel_id=1, source_target_pairs={{1,2},{3,4},{5,6},{7,8},{9,10},{11,12},{13,14},{15,16},{17,18},{19... | collective-permute-start | bytes 356360 | tf_op jit(solution)/shard_map/ppermute | solution.py:582
  6.2 0.0 copy-done
  6.2 3.2 %pair_bias_early.1.after_ref.early_ref = f32[8,16,8,256]{3,2,1,0:T(8,128)S(1)} custom-call(bf16[128,256,128]{2,1,0:T(8,128)(2,1)} %bitcast.12, bf16[128,128]{1,0:T(8,128)(2,1)S(1)} %broadcast_bitcast_fusion.head_ref), custom_call_target="tpu_custom_call" | custom-call | flops 536870912 | bytes 4194304 | tf_op jit(solution)/shard_map/pair_bias_early/pallas_call | solution.py:587
  9.5 0.0 collective-permute-done.near_ref
  9.5 0.0 collective-permute-done.1.far_ref
  9.5 3.9 %atom_stage.1 = (bf16[128,128]{1,0:T(8,128)(2,1)S(1)}, f32[16,768]{1,0:T(8,128)}, bf16[16,16,896]{2,1,0:T(8,128)(2,1)}, bf16[16,896]{1,0:T(8,128)(2,1)}, bf16[76...) custom-call(s32[4]{0:T(128)} %shift_ref.3, s32[16]{0:T(128)} %count_ref.1, s32[16]{0:T(128)} %mask_ref.1, ...), custom_call_target="tpu_custom_call" | custom-call | flops 268435456 | bytes 2097152 | tf_op jit(solution)/shard_map/atom_stage/pallas_call | solution.py:607
  13.4 4.5 %collective-permute-start.4 = (bf16[16,896]{1,0:T(8,128)(2,1)}, bf16[16,896]{1,0:T(8,128)(2,1)S(1)}, u32[]{:S(2)}, u32[]{:S(2)}) collective-permute-start(bf16[16,896]{1,0:T(8,128)(2,1)} %get-tuple-element.26.first_ref), channel_id=1, source_target_pairs={{0,6},{1,7},{2,0},{3,1},{4,2},{5,3},{6,4},{7,5},{8,14},{9,15},{10,... | collective-permute-start | bytes 86024 | tf_op jit(solution)/shard_map/ppermute | solution.py:644
  17.9 0.0 collective-permute-start.3
  17.9 0.7 %collective-permute-start.2 = (bf16[16,896]{1,0:T(8,128)(2,1)}, bf16[16,896]{1,0:T(8,128)(2,1)S(1)}, u32[]{:S(2)}, u32[]{:S(2)}) collective-permute-start(bf16[16,896]{1,0:T(8,128)(2,1)} %get-tuple-element.26.first_ref), channel_id=1, source_target_pairs={{0,2},{1,3},{2,4},{3,5},{4,6},{5,7},{6,0},{7,1},{8,10},{9,11},{10,... | collective-permute-start | bytes 86024 | tf_op jit(solution)/shard_map/ppermute | solution.py:644
  18.6 9.9 %all-to-all-start = ((bf16[16,16,896]{2,1,0:T(8,128)(2,1)}), bf16[16,16,896]{2,1,0:T(8,128)(2,1)}, u32[]{:S(2)}, u32[]{:S(2)}) async-start(bf16[16,16,896]{2,1,0:T(8,128)(2,1)} %get-tuple-element.25), calls=%async_computation | async-start | bytes 917504 | tf_op jit(solution)/shard_map/all_to_all | solution.py:645
  28.5 0.0 collective-permute-done.4.fourth_ref
  28.5 0.0 collective-permute-done.3.third_ref
  28.5 0.0 collective-permute-done.2.second_ref
  28.5 1.4 %stack.1.own_ref = bf16[4,16,896]{2,1,0:T(8,128)(2,1)} custom-call(bf16[16,896]{1,0:T(8,128)(2,1)} %get-tuple-element.26.first_ref, bf16[16,896]{1,0:T(8,128)(2,1)S(1)} %collective-permute-done.2.second_ref, bf16[16,896]{1,0:T(8,128)(2,1)S(1)} %collective-permute-done.3.third_ref, bf16[16,896]{1,0:T(8,128)(2,1)S(1)} %collective-permute-done.4.fourth_ref), custom_call_target="tpu_custom_call" | custom-call | flops 4294967296 | bytes 262144 | tf_op jit(solution)/shard_map/stack/pallas_call | solution.py:646
  29.9 0.0 collective-permute-start.5
  29.9 3.2 %pair_bias_late.1.late_ref = f32[8,16,8,256]{3,2,1,0:T(8,128)S(1)} custom-call(bf16[128,256,128]{2,1,0:T(8,128)(2,1)} %bitcast.13, bf16[128,128]{1,0:T(8,128)(2,1)S(1)} %broadcast_bitcast_fusion.head_ref), custom_call_target="tpu_custom_call" | custom-call | flops 536870912 | bytes 4194304 | tf_op jit(solution)/shard_map/pair_bias_late/pallas_call | solution.py:587
  33.2 0.0 collective-permute-done.5.partner_ref
  33.2 4.3 %all-to-all-done = bf16[16,16,896]{2,1,0:T(8,128)(2,1)} async-done(((bf16[16,16,896]{2,1,0:T(8,128)(2,1)}), bf16[16,16,896]{2,1,0:T(8,128)(2,1)}, u32[]{:S(2)}, u32[]{:S(2)}) %all-to-all-start) | async-done | bytes 458784 | tf_op jit(solution)/shard_map/all_to_all | solution.py:645
  37.4 6.1 %token_stage.1 = (f32[16,16,8,256]{3,2,1,0:T(8,128)S(1)}, f32[16,16,8,256]{3,2,1,0:T(8,128)S(1)}, f32[128,128]{1,0:T(8,128)S(1)}, f32[4,16,768]{2,1,0:T(8,128)S(1)}, bf16[4,16,1024]{2,1,0:T(8,128)(2,1)S(1)}) custom-call(bf16[256,896]{1,0:T(8,128)(2,1)} %bitcast.4.keys_ref, bf16[4,16,896]{2,1,0:T(8,128)(2,1)} %stack.1.own_ref, ...), custom_call_target="tpu_custom_call" | custom-call | flops 2147483648 | bytes 12582912 | tf_op jit(solution)/shard_map/token_stage/pallas_call | solution.py:661
  43.6 0.1 collective-permute-start.6
  43.7 1.3 %collective-permute-done.6.given_ref = bf16[4,16,1024]{2,1,0:T(8,128)(2,1)S(1)} collective-permute-done((bf16[4,16,1024]{2,1,0:T(8,128)(2,1)S(1)}, bf16[4,16,1024]{2,1,0:T(8,128)(2,1)S(1)}, u32[]{:S(2)}, u32[]{:S(2)}) %collective-permute-start.6) | collective-permute-done | bytes 131104 | tf_op jit(solution)/shard_map/ppermute | solution.py:685
  45.0 0.4 fold.1
  45.4 1.7 %collective-permute-start.7 = (bf16[16,1792]{1,0:T(8,128)(2,1)S(1)}, bf16[16,1792]{1,0:T(8,128)(2,1)S(1)}, u32[]{:S(2)}, u32[]{:S(2)}) collective-permute-start(bf16[16,1792]{1,0:T(8,128)(2,1)S(1)} %get-tuple-element.34), channel_id=1, source_target_pairs={{0,2},{1,3},{2,4},{3,5},{4,6},{5,7},{6,0},{7,1},{8,10},{9,11},{10,... | collective-permute-start | bytes 172040 | tf_op jit(solution)/shard_map/ppermute | solution.py:696
  47.1 2.0 %collective-permute-start.8 = (bf16[16,1792]{1,0:T(8,128)(2,1)S(1)}, bf16[16,1792]{1,0:T(8,128)(2,1)S(1)}, u32[]{:S(2)}, u32[]{:S(2)}) collective-permute-start(bf16[16,1792]{1,0:T(8,128)(2,1)S(1)} %get-tuple-element.35), channel_id=1, source_target_pairs={{0,4},{1,5},{2,6},{3,7},{4,0},{5,1},{6,2},{7,3},{8,12},{9,13},{10,... | collective-permute-start | bytes 172040 | tf_op jit(solution)/shard_map/ppermute | solution.py:696
  49.1 2.0 %collective-permute-start.9 = (bf16[16,1792]{1,0:T(8,128)(2,1)S(1)}, bf16[16,1792]{1,0:T(8,128)(2,1)S(1)}, u32[]{:S(2)}, u32[]{:S(2)}) collective-permute-start(bf16[16,1792]{1,0:T(8,128)(2,1)S(1)} %get-tuple-element.36), channel_id=1, source_target_pairs={{0,6},{1,7},{2,0},{3,1},{4,2},{5,3},{6,4},{7,5},{8,14},{9,15},{10,... | collective-permute-start | bytes 172040 | tf_op jit(solution)/shard_map/ppermute | solution.py:696
  51.1 0.0 collective-permute-done.7.first_ref
  51.1 0.7 %collective-permute-done.8.second_ref = bf16[16,1792]{1,0:T(8,128)(2,1)S(1)} collective-permute-done((bf16[16,1792]{1,0:T(8,128)(2,1)S(1)}, bf16[16,1792]{1,0:T(8,128)(2,1)S(1)}, u32[]{:S(2)}, u32[]{:S(2)}) %collective-permute-start.8) | collective-permute-done | bytes 57376 | tf_op jit(solution)/shard_map/ppermute | solution.py:696
  51.8 0.6 collective-permute-done.9.third_ref
  52.4 1.6 %merge.1 = (f32[128,128]{1,0:T(8,128)S(1)}, f32[128,128]{1,0:T(8,128)S(1)}, bf16[2,16,128]{2,1,0:T(8,128)(2,1)S(1)}) custom-call(f32[128,128]{1,0:T(8,128)S(1)} %get-tuple-element.29.stats_ref, f32[16,768]{1,0:T(8,128)S(1)} %get-tuple-element.32.own_ref, f32[128,128]{1,0:T(8,128)S(1)} %get-tuple-element.33.joint_ref, ...), custom_call_target="tpu_custom_call" | custom-call | flops 67108864 | bytes 2097152 | tf_op jit(solution)/shard_map/merge/pallas_call | solution.py:698
  54.1 4.5 %collective-permute-start.11 = (bf16[16,128]{1,0:T(8,128)(2,1)S(1)}, bf16[16,128]{1,0:T(8,128)(2,1)S(1)}, u32[]{:S(2)}, u32[]{:S(2)}) collective-permute-start(bf16[16,128]{1,0:T(8,128)(2,1)S(1)} %slice_bitcast_fusion), channel_id=1, source_target_pairs={{1,2},{3,4},{5,6},{7,8},{9,10},{11,12},{13,14},{15,16},{17,18},{19... | collective-permute-start | bytes 12296 | tf_op jit(solution)/shard_map/ppermute | solution.py:717
  58.6 0.1 collective-permute-start.10
  58.7 4.7 %pair_grad.1 = bf16[128,256,128]{2,1,0:T(8,128)(2,1)} custom-call(f32[16,16,8,256]{3,2,1,0:T(8,128)S(1)} %get-tuple-element.40.prob_ref, f32[16,16,8,256]{3,2,1,0:T(8,128)S(1)} %get-tuple-element.41.grad_ref, f32[128,128]{1,0:T(8,128)S(1)} %get-tuple-element.42.scale_ref, f32[128,128]{1,0:T(8,128)S(1)} %get-tuple-element.43.diag_ref, ...), custom_call_target="tpu_custom_call" | custom-call | flops 1073741824 | bytes 14680064 | tf_op jit(solution)/shard_map/pair_grad/pallas_call | solution.py:719
  63.4 0.0 collective-permute-done.11.far_ref
  63.4 0.0 collective-permute-done.10.near_ref
  63.4 1.5 %atom_out.1 = bf16[128,128]{1,0:T(8,128)(2,1)} custom-call(bf16[16,128]{1,0:T(8,128)(2,1)S(1)} %collective-permute-done.10.near_ref, bf16[16,128]{1,0:T(8,128)(2,1)S(1)} %collective-permute-done.11.far_ref, bf16[2,16,128]{2,1,0:T(8,128)(2,1)S(1)} %get-tuple-element.38.low_ref, s32[1,128]{1,0:T(1,128)} %bitcast.17, ...), custom_call_target="tpu_custom_call" | custom-call | flops 2097152 | bytes 131072 | tf_op jit(solution)/shard_map/atom_out/pallas_call | solution.py:731
  (2 shorter events, 0.0 us)
Async XLA Ops:
  0.6 5.6 %copy-start = (bf16[128,16]{0,1:T(8,128)(2,1)S(1)}, bf16[128,16]{0,1:T(8,128)(2,1)}, u32[]{:S(2)}) copy-start(bf16[128,16]{0,1:T(8,128)(2,1)} %param.27) | copy-start | bytes 12292
  1.6 7.9 %collective-permute-start = (bf16[464,128]{1,0:T(8,128)(2,1)S(1)}, bf16[464,128]{1,0:T(8,128)(2,1)S(1)}, u32[]{:S(2)}, u32[]{:S(2)}) collective-permute-start(bf16[464,128]{1,0:T(8,128)(2,1)S(1)} %get-tuple-element.23), channel_id=1, source_target_pairs={{0,1},{1,0},{2,3},{3,2},{4,5},{5,4},{6,7},{7,6},{8,9},{9,8},{10,11... | collective-permute-start | bytes 356360 | tf_op jit(solution)/shard_map/ppermute | solution.py:581
  3.1 6.4 %collective-permute-start.1 = (bf16[464,128]{1,0:T(8,128)(2,1)S(1)}, bf16[464,128]{1,0:T(8,128)(2,1)S(1)}, u32[]{:S(2)}, u32[]{:S(2)}) collective-permute-start(bf16[464,128]{1,0:T(8,128)(2,1)S(1)} %get-tuple-element.24), channel_id=1, source_target_pairs={{1,2},{3,4},{5,6},{7,8},{9,10},{11,12},{13,14},{15,16},{17,18},{19... | collective-permute-start | bytes 356360 | tf_op jit(solution)/shard_map/ppermute | solution.py:582
  13.4 15.1 %collective-permute-start.4 = (bf16[16,896]{1,0:T(8,128)(2,1)}, bf16[16,896]{1,0:T(8,128)(2,1)S(1)}, u32[]{:S(2)}, u32[]{:S(2)}) collective-permute-start(bf16[16,896]{1,0:T(8,128)(2,1)} %get-tuple-element.26.first_ref), channel_id=1, source_target_pairs={{0,6},{1,7},{2,0},{3,1},{4,2},{5,3},{6,4},{7,5},{8,14},{9,15},{10,... | collective-permute-start | bytes 86024 | tf_op jit(solution)/shard_map/ppermute | solution.py:644
  17.9 10.6 %collective-permute-start.3 = (bf16[16,896]{1,0:T(8,128)(2,1)}, bf16[16,896]{1,0:T(8,128)(2,1)S(1)}, u32[]{:S(2)}, u32[]{:S(2)}) collective-permute-start(bf16[16,896]{1,0:T(8,128)(2,1)} %get-tuple-element.26.first_ref), channel_id=1, source_target_pairs={{0,4},{1,5},{2,6},{3,7},{4,0},{5,1},{6,2},{7,3},{8,12},{9,13},{10,... | collective-permute-start | bytes 86024 | tf_op jit(solution)/shard_map/ppermute | solution.py:644
  17.9 10.6 %collective-permute-start.2 = (bf16[16,896]{1,0:T(8,128)(2,1)}, bf16[16,896]{1,0:T(8,128)(2,1)S(1)}, u32[]{:S(2)}, u32[]{:S(2)}) collective-permute-start(bf16[16,896]{1,0:T(8,128)(2,1)} %get-tuple-element.26.first_ref), channel_id=1, source_target_pairs={{0,2},{1,3},{2,4},{3,5},{4,6},{5,7},{6,0},{7,1},{8,10},{9,11},{10,... | collective-permute-start | bytes 86024 | tf_op jit(solution)/shard_map/ppermute | solution.py:644
  18.6 18.9 %all-to-all-start = ((bf16[16,16,896]{2,1,0:T(8,128)(2,1)}), bf16[16,16,896]{2,1,0:T(8,128)(2,1)}, u32[]{:S(2)}, u32[]{:S(2)}) async-start(bf16[16,16,896]{2,1,0:T(8,128)(2,1)} %get-tuple-element.25), calls=%async_computation | async-start | bytes 917504 | tf_op jit(solution)/shard_map/all_to_all | solution.py:645
  29.9 3.2 %collective-permute-start.5 = (bf16[4,16,896]{2,1,0:T(8,128)(2,1)}, bf16[4,16,896]{2,1,0:T(8,128)(2,1)}, u32[]{:S(2)}, u32[]{:S(2)}) collective-permute-start(bf16[4,16,896]{2,1,0:T(8,128)(2,1)} %stack.1.own_ref), channel_id=1, source_target_pairs={{0,1},{1,0},{2,3},{3,2},{4,5},{5,4},{6,7},{7,6},{8,9},{9,8},{10,11... | collective-permute-start | bytes 344072 | tf_op jit(solution)/shard_map/ppermute | solution.py:655
  43.6 1.4 %collective-permute-start.6 = (bf16[4,16,1024]{2,1,0:T(8,128)(2,1)S(1)}, bf16[4,16,1024]{2,1,0:T(8,128)(2,1)S(1)}, u32[]{:S(2)}, u32[]{:S(2)}) collective-permute-start(bf16[4,16,1024]{2,1,0:T(8,128)(2,1)S(1)} %get-tuple-element.31), channel_id=1, source_target_pairs={{0,1},{1,0},{2,3},{3,2},{4,5},{5,4},{6,7},{7,6},{8,9},{9,8},{10,11... | collective-permute-start | bytes 393224 | tf_op jit(solution)/shard_map/ppermute | solution.py:685
  45.4 5.7 %collective-permute-start.7 = (bf16[16,1792]{1,0:T(8,128)(2,1)S(1)}, bf16[16,1792]{1,0:T(8,128)(2,1)S(1)}, u32[]{:S(2)}, u32[]{:S(2)}) collective-permute-start(bf16[16,1792]{1,0:T(8,128)(2,1)S(1)} %get-tuple-element.34), channel_id=1, source_target_pairs={{0,2},{1,3},{2,4},{3,5},{4,6},{5,7},{6,0},{7,1},{8,10},{9,11},{10,... | collective-permute-start | bytes 172040 | tf_op jit(solution)/shard_map/ppermute | solution.py:696
  47.1 4.7 %collective-permute-start.8 = (bf16[16,1792]{1,0:T(8,128)(2,1)S(1)}, bf16[16,1792]{1,0:T(8,128)(2,1)S(1)}, u32[]{:S(2)}, u32[]{:S(2)}) collective-permute-start(bf16[16,1792]{1,0:T(8,128)(2,1)S(1)} %get-tuple-element.35), channel_id=1, source_target_pairs={{0,4},{1,5},{2,6},{3,7},{4,0},{5,1},{6,2},{7,3},{8,12},{9,13},{10,... | collective-permute-start | bytes 172040 | tf_op jit(solution)/shard_map/ppermute | solution.py:696
  49.1 3.3 %collective-permute-start.9 = (bf16[16,1792]{1,0:T(8,128)(2,1)S(1)}, bf16[16,1792]{1,0:T(8,128)(2,1)S(1)}, u32[]{:S(2)}, u32[]{:S(2)}) collective-permute-start(bf16[16,1792]{1,0:T(8,128)(2,1)S(1)} %get-tuple-element.36), channel_id=1, source_target_pairs={{0,6},{1,7},{2,0},{3,1},{4,2},{5,3},{6,4},{7,5},{8,14},{9,15},{10,... | collective-permute-start | bytes 172040 | tf_op jit(solution)/shard_map/ppermute | solution.py:696
  54.1 9.3 %collective-permute-start.11 = (bf16[16,128]{1,0:T(8,128)(2,1)S(1)}, bf16[16,128]{1,0:T(8,128)(2,1)S(1)}, u32[]{:S(2)}, u32[]{:S(2)}) collective-permute-start(bf16[16,128]{1,0:T(8,128)(2,1)S(1)} %slice_bitcast_fusion), channel_id=1, source_target_pairs={{1,2},{3,4},{5,6},{7,8},{9,10},{11,12},{13,14},{15,16},{17,18},{19... | collective-permute-start | bytes 12296 | tf_op jit(solution)/shard_map/ppermute | solution.py:717
  58.6 4.8 %collective-permute-start.10 = (bf16[16,128]{1,0:T(8,128)(2,1)S(1)}, bf16[16,128]{1,0:T(8,128)(2,1)S(1)}, u32[]{:S(2)}, u32[]{:S(2)}) collective-permute-start(bf16[16,128]{1,0:T(8,128)(2,1)S(1)} %slice_bitcast_fusion), channel_id=1, source_target_pairs={{0,1},{1,0},{2,3},{3,2},{4,5},{5,4},{6,7},{7,6},{8,9},{9,8},{10,11... | collective-permute-start | bytes 12296 | tf_op jit(solution)/shard_map/ppermute | solution.py:716

commit v3 on v2

--- a/solution.py
+++ b/solution.py
@@ -19,6 +19,7 @@
 AUX = 16
 EPSILON = 1e-05
 LOWEST = -1e30
+MASKED = 1024.0
 F32 = jnp.float32
 BF16 = jnp.bfloat16
 NT = (((1,), (1,)), ((), ()))
@@ -70,7 +71,9 @@
     return jnp.where(rows % GROUP == member, head_rows, 0.0).astype(BF16)
 
 
-def pair_bias_kernel(first, pair_ref, head_ref, out_ref, tile_ref, arrived):
+def pair_bias_kernel(
+    first, pair_ref, head_ref, out_ref, tile_ref, bias_ref, arrived, left
+):
     groups = out_ref.shape[0]
     window = min(8, groups)
 
@@ -79,6 +82,9 @@
         here = pl.ds((g + first) * GROUP, GROUP)
         return pltpu.make_async_copy(pair_ref.at[here], tile_ref.at[rows], arrived.at[g])
 
+    def leave(g):
+        return pltpu.make_async_copy(bias_ref.at[g], out_ref.at[g], left.at[g])
+
     for g in range(window):
         copy(g).start()
     weight = head_ref[...].astype(F32).reshape(HT, GROUP, 128)[:, 0].astype(BF16)
@@ -92,10 +98,13 @@
                 copy(g + window).start()
 
         for i in range(GROUP):
-            out_ref[g, :, i, :] = dot(weight, tile_ref[g * GROUP + i], NT)
+            bias_ref[g, :, i, :] = dot(weight, tile_ref[g * GROUP + i], NT)
+        leave(g).start()
         return carry
 
     lax.fori_loop(0, groups, step, 0)
+    for g in range(groups):
+        leave(g).wait()
 
 
 def pack_kernel(shift_ref, atoms_ref, bias_ref, cot_ref, token_ref, near_ref, far_ref):
@@ -140,23 +149,24 @@
     w_qkv_ref,
     w_out_ref,
     w_pool_ref,
-    token_out_ref,
-    back_ref,
+    token_qkv_ref,
     hidden_ref,
     pooled_ref,
     to_row_ref,
     to_col_ref,
-    inner_out_ref,
-    inner_back_ref,
+    token_kv_ref,
     prev_ref,
     next_ref,
     arrived,
 ):
-    pairs = (
-        (token_out_ref, inner_out_ref),
-        (back_ref, inner_back_ref),
-    )
-    copies = [pltpu.make_async_copy(a, b, arrived.at[n]) for n, (a, b) in enumerate(pairs)]
+    copies = []
+    for n in range(4):
+        rows = slice(192 * n, 192 * (n + 1))
+        copies.append(
+            pltpu.make_async_copy(
+                token_qkv_ref.at[rows, 768:2304], token_kv_ref.at[rows], arrived.at[n]
+            )
+        )
     for copy in copies:
         copy.start()
     row, col = place()
@@ -230,7 +240,9 @@
     mixture = jnp.concatenate(mixes, axis=0).astype(BF16)
     base = jnp.concatenate([wide[128:320], wide[64:128]], axis=0)
     hidden = (base + dot(mixture, w_out_ref[...])).astype(BF16)
-    hidden_ref[...] = hidden[:128]
+    hidden_ref[0:128] = hidden[:128]
+    relative = (token_ref[...] - (16 * device - 16)).astype(F32)
+    hidden_ref[128:144] = jnp.broadcast_to(relative, (16, 128)).astype(BF16)
     lifted = jnp.maximum(dot(hidden, w_pool_ref[...]), 0.0)
     own_token = (token_ref[...] - 16 * device).astype(F32)
     prev_token = prev_ref[448:449].astype(F32) - 33.0
@@ -251,10 +263,10 @@
     normed = normal(pooled).astype(BF16)
     cot = jnp.concatenate([cot_ref[...], next_ref[384:448], prev_ref[384:448]], axis=0)
     grad_up = dot(select, cot).astype(BF16)
-    live = live.astype(F32).astype(BF16)
+    live = jnp.concatenate([live] * 6, axis=1)
+    marked = jnp.where(live > 0, normed.astype(F32), MASKED).astype(BF16)
     for r in range(to_row_ref.shape[0]):
-        to_row_ref[r, :, :768] = normed
-        to_row_ref[r, :, 768:] = live
+        to_row_ref[r] = marked
     to_col_ref[:, :768] = normed
     to_col_ref[:, 768:] = grad_up
     for copy in copies:
@@ -266,53 +278,76 @@
     return 384 * block + (0 if rest < 5 else 128)
 
 
-def stack_kernel(first_ref, second_ref, third_ref, fourth_ref, out_ref):
-    for n, part in enumerate((first_ref, second_ref, third_ref, fourth_ref)):
-        out_ref[n] = part[...]
+def stack_kernel(own_ref, partner_ref, out_ref):
+    row, col = place()
+    core = lax.rem(col, 2)
+    out_ref[core] = own_ref[...]
+    out_ref[1 - core] = partner_ref[...]
 
 
 def token_kernel(
     keys_ref,
     own_ref,
-    partner_ref,
+    first_ref,
+    second_ref,
+    third_ref,
     early_ref,
     late_ref,
+    w_kv_ref,
     w_qkv_ref,
     w_out_ref,
     w_back_ref,
+    pooled_ref,
     prob_ref,
     grad_ref,
     stats_ref,
     keep_ref,
     give_ref,
+    pooled_out_ref,
+    inner_out_ref,
+    inner_back_ref,
     rows_ref,
+    mixed_ref,
     inner_ref,
-    mixed_ref,
+    bias_ref,
     arrived,
 ):
     copies = []
-    for n in range(6):
-        rows = slice(128 * n, 128 * (n + 1))
-        copies.append(
-            pltpu.make_async_copy(w_qkv_ref.at[rows], inner_ref.at[rows], arrived.at[n])
-        )
+    for n in range(2):
+        rows = slice(384 * n, 384 * (n + 1))
+        copies.append((w_qkv_ref.at[rows, 0:768], inner_ref.at[rows]))
+    copies.append((w_back_ref, inner_back_ref))
+    for n in range(2):
+        rows = slice(384 * n, 384 * (n + 1))
+        copies.append((w_out_ref.at[rows], inner_out_ref.at[rows]))
+    early = early_ref.shape[0]
+    for first, count, source in ((0, early, early_ref), (early, 16 - early, late_ref)):
+        for start, stop in ((0, count // 2), (count // 2, count)):
+            copies.append(
+                (source.at[start:stop], bias_ref.at[first + start : first + stop])
+            )
+    copies.append((pooled_ref, pooled_out_ref))
+    copies = [pltpu.make_async_copy(a, b, arrived.at[n]) for n, (a, b) in enumerate(copies)]
     for copy in copies:
         copy.start()
+
     row, col = place()
     chip, core = lax.div(col, 2), lax.rem(col, 2)
-    for s in range(4):
+    for s, part_ref in enumerate((own_ref, first_ref, second_ref, third_ref)):
         there = lax.rem(chip + 4 - s, 4) * 32
-        rows_ref[pl.ds(pl.multiple_of(there + core * 16, 16), 16)] = own_ref[s]
-        rows_ref[pl.ds(pl.multiple_of(there + 16 - core * 16, 16), 16)] = partner_ref[s]
-    middle = dot(rows_ref[:, 768:], w_back_ref[...], NT).astype(BF16)
-    grad = dot(middle, w_out_ref[...], NT).astype(BF16)
-    for copy in copies:
+        rows_ref[pl.ds(pl.multiple_of(there, 32), 16)] = part_ref[0]
+        rows_ref[pl.ds(pl.multiple_of(there + 16, 16), 16)] = part_ref[1]
+    key = dot(keys_ref[...], w_kv_ref[:, :768]).astype(BF16)
+    value = dot(keys_ref[...], w_kv_ref[:, 768:]).astype(BF16)
+    for copy in copies[:2]:
         copy.wait()
-    query = dot(rows_ref[:, :768], inner_ref[:, :768]).astype(BF16)
-    key = dot(keys_ref[:, :768], inner_ref[:, 768:1536]).astype(BF16)
-    value = dot(keys_ref[:, :768], inner_ref[:, 1536:]).astype(BF16)
-    live = keys_ref[:, 768:].astype(F32).T[0:1]
-    closed = jnp.where(live > 0, 0.0, -jnp.inf)
+    query = dot(rows_ref[:, :768], inner_ref[...]).astype(BF16)
+    for copy in copies[2:5]:
+        copy.wait()
+    middle = dot(rows_ref[:, 768:], inner_back_ref[...], NT).astype(BF16)
+    grad = dot(middle, inner_out_ref[...], NT).astype(BF16)
+    first = keys_ref[:, :128].astype(F32).T[0:1]
+    closed = jnp.where(first < MASKED, 0.0, -jnp.inf)
     lane = iota((128, 256), 1)
     stat_lane = iota((128, 128), 1)
 
@@ -320,17 +355,19 @@
         at = window_of(h)
         return (lane >= 48 * h - at) & (lane < 48 * (h + 1) - at)
 
-    for h in range(HT):
-        at = window_of(h)
-        query_h = jnp.where(within(h), query[:, at : at + 256].astype(F32), 0.0).astype(BF16)
-        scores = dot(query_h, key[:, at : at + 256], NT) * (1.0 / math.sqrt(48))
-        bias = jnp.concatenate([early_ref[:, h], late_ref[:, h]], axis=0).reshape(128, 256)
-        prob_ref[:, h] = (scores + bias + closed).reshape(16, GROUP, 256)
     for h in range(HT):
         at = window_of(h)
         grad_h = jnp.where(within(h), grad[:, at : at + 256].astype(F32), 0.0).astype(BF16)
         grads = dot(grad_h, value[:, at : at + 256], NT)
         grad_ref[:, h] = grads.reshape(16, GROUP, 256)
+    for copy in copies[5:]:
+        copy.wait()
+    for h in range(HT):
+        at = window_of(h)
+        query_h = jnp.where(within(h), query[:, at : at + 256].astype(F32), 0.0).astype(BF16)
+        scores = dot(query_h, key[:, at : at + 256], NT) * (1.0 / math.sqrt(48))
+        bias = bias_ref[:, h].reshape(128, 256)
+        prob_ref[:, h] = (scores + bias + closed).reshape(16, GROUP, 256)
     tops = jnp.zeros((128, 128), F32)
     sums = jnp.zeros((128, 128), F32)
     diags = jnp.zeros((128, 128), F32)
@@ -452,6 +489,8 @@
     scale_ref,
     diag_ref,
     low_ref,
+    near_ref,
+    far_ref,
     ratio_ref,
 ):
     row, col = place()
@@ -479,6 +518,8 @@
         mixed = mixed + part_ref[:, :768].astype(F32) * factors[16 * n + 16 : 16 * n + 32]
     updated = (pooled_ref[...] + dot(mixed.astype(BF16), w_out_ref[...])).astype(BF16)
     high, low = split(dot(updated, w_back_ref[...]))
+    near_ref[...] = high
+    far_ref[...] = high
     low_ref[0] = high
     low_ref[1] = low
 
@@ -519,20 +560,19 @@
         copy(g).wait()
 
 
-def atom_out_kernel(near_ref, far_ref, low_ref, token_ref, hidden_ref, out_ref):
+def atom_out_kernel(near_ref, far_ref, low_ref, hidden_ref, out_ref):
     row, col = place()
     odd = lax.rem(col, 2) == 1
-    device = row * lax.axis_size("col") + col
     near = near_ref[...].astype(F32)
     far = far_ref[...].astype(F32)
     before = jnp.where(odd, near, far).astype(BF16)
     after = jnp.where(odd, far, near).astype(BF16)
     rows = jnp.concatenate([before, low_ref[0], after, low_ref[1]], axis=0)
-    token = (token_ref[...] - (16 * device - 16)).astype(F32)
+    token = hidden_ref[128:144].astype(F32)[0:1]
     index = iota((64, 128), 0)
     index = jnp.where(index < 48, index, index - 32).astype(F32)
     select = jnp.where(index == token, 1.0, 0.0).astype(BF16)
-    out_ref[...] = (hidden_ref[...].astype(F32) + dot(select, rows, TN)).astype(BF16)
+    out_ref[...] = (hidden_ref[0:128].astype(F32) + dot(select, rows, TN)).astype(BF16)
 
 
 def shards(
@@ -587,10 +627,12 @@
         return pl.pallas_call(
             functools.partial(pair_bias_kernel, first),
             in_specs=[HBM, VMEM],
-            out_specs=VMEM,
-            out_shape=pltpu.VMEM((groups, HT, GROUP, 256), F32),
+            out_specs=HBM,
+            out_shape=pltpu.HBM((groups, HT, GROUP, 256), F32),
             scratch_shapes=[
                 pltpu.VMEM((groups * GROUP, 256, 128), BF16),
+                pltpu.VMEM((groups, HT, GROUP, 256), F32),
+                pltpu.SemaphoreType.DMA((groups,)),
                 pltpu.SemaphoreType.DMA((groups,)),
             ],
             compiler_params=params(14),
@@ -604,22 +646,21 @@
     early = pair_bias(0, half, "pair_bias_early")
     late = pair_bias(half, 16 - half, "pair_bias_late")
 
-    hidden, pooled, to_row, to_col, token_out, back = pl.pallas_call(
+    hidden, pooled, to_row, to_col, token_kv = pl.pallas_call(
         atom_kernel,
-        in_specs=[SMEM] * 3 + [VMEM] * 6 + [pl.BlockSpec(memory_space=pl.ANY)] + [VMEM] * 3 + [HBM] * 2,
-        out_specs=[VMEM] * 6,
+        in_specs=[SMEM] * 3 + [VMEM] * 6 + [pl.BlockSpec(memory_space=pl.ANY)] + [VMEM] * 3 + [HBM],
+        out_specs=[VMEM] * 5,
         out_shape=[
-            pltpu.VMEM((128, 128), BF16),
+            pltpu.VMEM((144, 128), BF16),
             pltpu.HBM((16, 768), F32),
-            pltpu.HBM((row_count, 16, 896), BF16),
-            pltpu.HBM((16, 896), BF16),
-            pltpu.VMEM(w_token_out.shape, BF16),
-            pltpu.VMEM(w_back.shape, BF16),
+            pltpu.VMEM((row_count, 16, 768), BF16),
+            pltpu.VMEM((16, 896), BF16),
+            pltpu.VMEM((768, 1536), BF16),
         ],
         scratch_shapes=[
             pltpu.VMEM((464, 128), BF16),
             pltpu.VMEM((464, 128), BF16),
-            pltpu.SemaphoreType.DMA((2,)),
+            pltpu.SemaphoreType.DMA((4,)),
         ],
         compiler_params=params(8),
         name="atom_stage",
@@ -634,53 +675,64 @@
         outside(atom_bias),
         outside(cotangent),
         outside(tokens),
-        inside(early),
+        outside(early),
         outside(w_atom_qkv),
         outside(w_atom_out),
         outside(w_pool),
-        outside(w_token_out),
-        outside(w_back),
+        outside(w_token_qkv),
     )
-    shifted = [lax.ppermute(to_col, "col", chip_shift(s)) for s in range(1, 4)]
-    keys = lax.all_to_all(to_row, "row", 0, 0).reshape(256, 896)
+    partner = lax.ppermute(to_col, "col", core_pairs)
+    keys = lax.all_to_all(to_row, "row", 0, 0).reshape(256, 768)
     own = pl.pallas_call(
         stack_kernel,
-        in_specs=[VMEM] * 4,
+        in_specs=[VMEM] * 2,
         out_specs=VMEM,
-        out_shape=pltpu.HBM((4, 16, 896), BF16),
+        out_shape=pltpu.VMEM((2, 16, 896), BF16),
         compiler_params=params(4),
         name="stack",
         cost_estimate=pl.CostEstimate(flops=1 << 32, bytes_accessed=1 << 18, transcendentals=0),
-    )(outside(to_col), *shifted)
-    partner = lax.ppermute(own, "col", core_pairs)
+    )(inside(to_col), partner)
+    shifted = [lax.ppermute(own, "col", chip_shift(s)) for s in range(1, 4)]
 
     stat = pltpu.VMEM((128, 128), F32)
     swapped = jax.ShapeDtypeStruct((4, 16, 1024), BF16)
     folded = jax.ShapeDtypeStruct((16, 1792), BF16)
     table = pltpu.VMEM((16, HT, GROUP, 256), F32)
-    prob, grad, stats, keep, give = pl.pallas_call(
+    prob, grad, stats, keep, give, pooled, token_out, back = pl.pallas_call(
         token_kernel,
-        in_specs=[VMEM] * 5 + [HBM] + [VMEM] * 2,
-        out_specs=[VMEM] * 5,
+        in_specs=[VMEM] * 5 + [HBM] * 2 + [VMEM] + [HBM] * 4,
+        out_specs=[VMEM] * 8,
         scratch_shapes=[
             pltpu.VMEM((128, 896), BF16),
-            pltpu.VMEM((768, 2304), BF16),
             pltpu.VMEM((128, 768), F32),
-            pltpu.SemaphoreType.DMA((6,)),
+            pltpu.VMEM((768, 768), BF16),
+            pltpu.VMEM((16, HT, GROUP, 256), F32),
+            pltpu.SemaphoreType.DMA((10,)),
         ],
-        out_shape=[table, table, stat, pltpu.VMEM((4, 16, 768), F32), swapped],
+        out_shape=[
+            table,
+            table,
+            stat,
+            pltpu.VMEM((4, 16, 768), F32),
+            swapped,
+            pltpu.VMEM((16, 768), F32),
+            pltpu.VMEM(w_token_out.shape, BF16),
+            pltpu.VMEM(w_back.shape, BF16),
+        ],
         compiler_params=params(16),
         name="token_stage",
         cost_estimate=pl.CostEstimate(flops=1 << 31, bytes_accessed=12 << 20, transcendentals=1 << 19),
     )(
-        outside(keys),
-        outside(own),
-        outside(partner),
-        inside(early),
-        inside(late),
+        inside(keys),
+        inside(own),
+        *shifted,
+        outside(early),
+        outside(late),
+        inside(token_kv),
         outside(w_token_qkv),
-        inside(token_out),
-        inside(back),
+        outside(w_token_out),
+        outside(w_back),
+        outside(pooled),
     )
     given = lax.ppermute(give, "col", core_pairs)
     *sent, mixed, joint = pl.pallas_call(
@@ -695,11 +747,17 @@
     )(inside(keep), inside(stats), given)
     parts = [lax.ppermute(part, "col", chip_shift(s + 1)) for s, part in enumerate(sent)]
 
-    scale, diag, low = pl.pallas_call(
+    scale, diag, low, near, far = pl.pallas_call(
         merge_kernel,
         in_specs=[VMEM] * 9,
-        out_specs=[VMEM] * 3,
-        out_shape=[stat, stat, pltpu.VMEM((2, 16, 128), BF16)],
+        out_specs=[VMEM] * 5,
+        out_shape=[
+            stat,
+            stat,
+            pltpu.VMEM((2, 16, 128), BF16),
+            jax.ShapeDtypeStruct((16, 128), BF16),
+            jax.ShapeDtypeStruct((16, 128), BF16),
+        ],
         scratch_shapes=[pltpu.VMEM((4, 128, 128), F32)],
         compiler_params=params(6),
         name="merge",
@@ -709,12 +767,12 @@
         inside(mixed),
         inside(joint),
         *parts,
-        outside(pooled),
+        inside(pooled),
         inside(token_out),
         inside(back),
     )
-    near = lax.ppermute(low[0], "col", core_pairs)
-    far = lax.ppermute(low[0], ("row", "col"), chip_pairs)
+    near = lax.ppermute(near, "col", core_pairs)
+    far = lax.ppermute(far, ("row", "col"), chip_pairs)
 
     pair_grad = pl.pallas_call(
         pair_grad_kernel,
@@ -730,13 +788,13 @@
     )(inside(prob), inside(grad), inside(scale), inside(diag), head_rows)
     atom_out = pl.pallas_call(
         atom_out_kernel,
-        in_specs=[VMEM] * 5,
+        in_specs=[VMEM] * 4,
         out_specs=VMEM,
         out_shape=jax.ShapeDtypeStruct((128, 128), BF16),
         compiler_params=params(4),
         name="atom_out",
         cost_estimate=pl.CostEstimate(flops=1 << 21, bytes_accessed=1 << 17, transcendentals=0),
-    )(near, far, inside(low), outside(tokens), inside(hidden))
+    )(near, far, inside(low), inside(hidden))
     return (atom_out, pair_grad.reshape(pair.shape))
 
 

time: 65.3 us -> 61.9 us (0.948)
  the two profiles are of different devices: /device:TPU:1 before, /device:TPU:8 now
where the time goes in v3:
time: 61.9 us; the launch traced here: 61.6 us
  starting transfers between devices  30 us (48%)
  Pallas kernels  25 us (40%)
  waiting for transfers between devices  5.77 us (9%)
  between operations  0.81 us (1%)
    ppermute x2, starting transfers between devices, shards(): far = lax.ppermute(far, ('row', 'col'), chip_pairs)  14.4 us
    pallas_call x2, Pallas kernels, pair_bias(): pl.pallas_call(functools.partial(pair_bias_kernel, first), in_specs=[HBM,...  7.88 us
    ppermute x3, starting transfers between devices, shards(): shifted = [lax.ppermute(own, 'col', chip_shift(s)) for s in range(1, 4)]  5.82 us
    pallas_call x1, Pallas kernels, shards(): pl.pallas_call(token_kernel, in_specs=[VMEM] * 5 + [HBM] * 2 + [VMEM] + [...  5.51 us
    all_to_all x1, starting transfers between devices, shards(): keys = lax.all_to_all(to_row, 'row', 0, 0).reshape(256, 768)  5.05 us
    pallas_call x1, Pallas kernels, shards(): pl.pallas_call(pair_grad_kernel, in_specs=[VMEM] * 5, out_specs=HBM, out_...  4.71 us
    ppermute x3, starting transfers between devices, shards(): lax.ppermute(part, 'col', chip_shift(s + 1))  4.41 us
    pallas_call x1, Pallas kernels, shards(): pl.pallas_call(atom_kernel, in_specs=[SMEM] * 3 + [VMEM] * 6 + [pl.BlockS...  3.94 us
  transfers between devices with their start and end apart: 13, of which 6 were waited for; matrix products, arithmetic and copies ran while one was open for 0% of the time, Pallas kernels for 20%

profile of v3, /device:TPU:8, one launch (start us, length us, event | category | flops | bytes accessed | tf_op | source)
XLA Modules:
  0.0 61.6 jit_solution(2150040979086561286)
XLA Ops:
  0.6 0.0 copy-start
  0.6 1.0 %pack.1 = (bf16[464,128]{1,0:T(8,128)(2,1)S(1)}, bf16[464,128]{1,0:T(8,128)(2,1)S(1)}) custom-call(s32[4]{0:T(128)} %shift_ref.3, bf16[128,128]{1,0:T(8,128)(2,1)} %atoms_ref.3, bf16[4,128,128]{2,1,0:T(8,128)(2,1)} %bias_ref.3, bf16[128,128]{1,0:T(8,128)(2,1)} %cot_ref.3, s32[1,128]{1,0:T(1,128)} %bitcast.14), custom_call_target="tpu_custom_call" | custom-call | bytes 1048576 | tf_op jit(solution)/shard_map/pack/pallas_call | solution.py:606
  1.6 0.1 collective-permute-start
  1.7 8.1 %collective-permute-start.1 = (bf16[464,128]{1,0:T(8,128)(2,1)S(1)}, bf16[464,128]{1,0:T(8,128)(2,1)S(1)}, u32[]{:S(2)}, u32[]{:S(2)}) collective-permute-start(bf16[464,128]{1,0:T(8,128)(2,1)S(1)} %get-tuple-element.28), channel_id=1, source_target_pairs={{1,2},{3,4},{5,6},{7,8},{9,10},{11,12},{13,14},{15,16},{17,18},{19... | collective-permute-start | bytes 356360 | tf_op jit(solution)/shard_map/ppermute | solution.py:622
  9.8 0.0 copy-done
  9.9 4.0 %pair_bias_early.1.after_ref.early_ref = f32[8,16,8,256]{3,2,1,0:T(8,128)} custom-call(bf16[128,256,128]{2,1,0:T(8,128)(2,1)} %bitcast.11, bf16[128,128]{1,0:T(8,128)(2,1)S(1)} %broadcast_bitcast_fusion.head_ref), custom_call_target="tpu_custom_call" | custom-call | flops 536870912 | bytes 4194304 | tf_op jit(solution)/shard_map/pair_bias_early/pallas_call | solution.py:627
  13.8 0.0 collective-permute-done.near_ref
  13.8 0.0 collective-permute-done.1.far_ref
  13.8 3.9 %atom_stage.1 = (bf16[144,128]{1,0:T(8,128)(2,1)S(1)}, f32[16,768]{1,0:T(8,128)}, bf16[16,16,768]{2,1,0:T(8,128)(2,1)}, bf16[16,896]{1,0:T(8,128)(2,1)S(1)}, bf16[768,1536]{1,0:T(8,128)(2,1)S(1)}) custom-call(s32[4]{0:T(128)} %shift_ref.3, s32[16]{0:T(128)} %count_ref.1, s32[16]{0:T(128)} %mask_ref.1, bf16[464,128]{1,0:T(8,128)(2,1)S(1)} %collective-permute-done.near_ref, ...), custom_call_target="tpu_custom_call" | custom-call | flops 268435456 | bytes 2097152 | tf_op jit(solution)/shard_map/atom_stage/pallas_call | solution.py:649
  17.8 0.1 collective-permute-start.2
  17.9 5.1 %all-to-all-start = ((bf16[16,16,768]{2,1,0:T(8,128)(2,1)}), bf16[16,16,768]{2,1,0:T(8,128)(2,1)S(1)}, u32[]{:S(2)}, u32[]{:S(2)}) async-start(bf16[16,16,768]{2,1,0:T(8,128)(2,1)} %get-tuple-element.29), calls=%async_computation | async-start | bytes 786432 | tf_op jit(solution)/shard_map/all_to_all | solution.py:685
  22.9 0.0 collective-permute-done.2.partner_ref
  23.0 4.9 %collective-permute-start.5 = (bf16[2,16,896]{2,1,0:T(8,128)(2,1)S(1)}, bf16[2,16,896]{2,1,0:T(8,128)(2,1)S(1)}, u32[]{:S(2)}, u32[]{:S(2)}) collective-permute-start(bf16[2,16,896]{2,1,0:T(8,128)(2,1)S(1)} %stack.1.own_ref), channel_id=1, source_target_pairs={{0,6},{1,7},{2,0},{3,1},{4,2},{5,3},{6,4},{7,5},{8,14},{9,15},{10,... | collective-permute-start | bytes 172040 | tf_op jit(solution)/shard_map/ppermute | solution.py:695
  27.8 0.0 collective-permute-start.4
  27.8 0.9 %collective-permute-start.3 = (bf16[2,16,896]{2,1,0:T(8,128)(2,1)S(1)}, bf16[2,16,896]{2,1,0:T(8,128)(2,1)S(1)}, u32[]{:S(2)}, u32[]{:S(2)}) collective-permute-start(bf16[2,16,896]{2,1,0:T(8,128)(2,1)S(1)} %stack.1.own_ref), channel_id=1, source_target_pairs={{0,2},{1,3},{2,4},{3,5},{4,6},{5,7},{6,0},{7,1},{8,10},{9,11},{10,... | collective-permute-start | bytes 172040 | tf_op jit(solution)/shard_map/ppermute | solution.py:695
  28.8 3.9 %pair_bias_late.1.late_ref = f32[8,16,8,256]{3,2,1,0:T(8,128)} custom-call(bf16[128,256,128]{2,1,0:T(8,128)(2,1)} %bitcast.12, bf16[128,128]{1,0:T(8,128)(2,1)S(1)} %broadcast_bitcast_fusion.head_ref), custom_call_target="tpu_custom_call" | custom-call | flops 536870912 | bytes 4194304 | tf_op jit(solution)/shard_map/pair_bias_late/pallas_call | solution.py:627
  32.7 0.0 collective-permute-done.5.third_ref
  32.7 0.9 %collective-permute-done.4.second_ref = bf16[2,16,896]{2,1,0:T(8,128)(2,1)S(1)} collective-permute-done((bf16[2,16,896]{2,1,0:T(8,128)(2,1)S(1)}, bf16[2,16,896]{2,1,0:T(8,128)(2,1)S(1)}, u32[]{:S(2)}, u32[]{:S(2)}) %collective-permute-start.4) | collective-permute-done | bytes 57376 | tf_op jit(solution)/shard_map/ppermute | solution.py:695
  33.6 0.2 collective-permute-done.3.first_ref
  33.8 0.0 all-to-all-done
  33.8 5.5 %token_stage.1 = (f32[16,16,8,256]{3,2,1,0:T(8,128)S(1)}, f32[16,16,8,256]{3,2,1,0:T(8,128)S(1)}, f32[128,128]{1,0:T(8,128)S(1)}, f32[4,16,768]{2,1,0:T(8,128)S(...) custom-call(bf16[256,768]{1,0:T(8,128)(2,1)S(1)} %bitcast.10, ...), custom_call_target="tpu_custom_call" | custom-call | flops 2147483648 | bytes 12582912 | tf_op jit(solution)/shard_map/token_stage/pallas_call | solution.py:701
  39.4 0.1 collective-permute-start.6
  39.5 1.3 %collective-permute-done.6.given_ref = bf16[4,16,1024]{2,1,0:T(8,128)(2,1)S(1)} collective-permute-done((bf16[4,16,1024]{2,1,0:T(8,128)(2,1)S(1)}, bf16[4,16,1024]{2,1,0:T(8,128)(2,1)S(1)}, u32[]{:S(2)}, u32[]{:S(2)}) %collective-permute-start.6) | collective-permute-done | bytes 131104 | tf_op jit(solution)/shard_map/ppermute | solution.py:737
  40.8 0.4 fold.1
  41.2 1.5 %collective-permute-start.7 = (bf16[16,1792]{1,0:T(8,128)(2,1)S(1)}, bf16[16,1792]{1,0:T(8,128)(2,1)S(1)}, u32[]{:S(2)}, u32[]{:S(2)}) collective-permute-start(bf16[16,1792]{1,0:T(8,128)(2,1)S(1)} %get-tuple-element.38), channel_id=1, source_target_pairs={{0,2},{1,3},{2,4},{3,5},{4,6},{5,7},{6,0},{7,1},{8,10},{9,11},{10,... | collective-permute-start | bytes 172040 | tf_op jit(solution)/shard_map/ppermute | solution.py:748
  42.7 2.0 %collective-permute-start.8 = (bf16[16,1792]{1,0:T(8,128)(2,1)S(1)}, bf16[16,1792]{1,0:T(8,128)(2,1)S(1)}, u32[]{:S(2)}, u32[]{:S(2)}) collective-permute-start(bf16[16,1792]{1,0:T(8,128)(2,1)S(1)} %get-tuple-element.39), channel_id=1, source_target_pairs={{0,4},{1,5},{2,6},{3,7},{4,0},{5,1},{6,2},{7,3},{8,12},{9,13},{10,... | collective-permute-start | bytes 172040 | tf_op jit(solution)/shard_map/ppermute | solution.py:748
  44.7 0.9 %collective-permute-start.9 = (bf16[16,1792]{1,0:T(8,128)(2,1)S(1)}, bf16[16,1792]{1,0:T(8,128)(2,1)S(1)}, u32[]{:S(2)}, u32[]{:S(2)}) collective-permute-start(bf16[16,1792]{1,0:T(8,128)(2,1)S(1)} %get-tuple-element.40), channel_id=1, source_target_pairs={{0,6},{1,7},{2,0},{3,1},{4,2},{5,3},{6,4},{7,5},{8,14},{9,15},{10,... | collective-permute-start | bytes 172040 | tf_op jit(solution)/shard_map/ppermute | solution.py:748
  45.6 1.0 %collective-permute-done.7.first_ref = bf16[16,1792]{1,0:T(8,128)(2,1)S(1)} collective-permute-done((bf16[16,1792]{1,0:T(8,128)(2,1)S(1)}, bf16[16,1792]{1,0:T(8,128)(2,1)S(1)}, u32[]{:S(2)}, u32[]{:S(2)}) %collective-permute-start.7) | collective-permute-done | bytes 57376 | tf_op jit(solution)/shard_map/ppermute | solution.py:748
  46.6 1.8 %collective-permute-done.8.second_ref = bf16[16,1792]{1,0:T(8,128)(2,1)S(1)} collective-permute-done((bf16[16,1792]{1,0:T(8,128)(2,1)S(1)}, bf16[16,1792]{1,0:T(8,128)(2,1)S(1)}, u32[]{:S(2)}, u32[]{:S(2)}) %collective-permute-start.8) | collective-permute-done | bytes 57376 | tf_op jit(solution)/shard_map/ppermute | solution.py:748
  48.4 0.5 collective-permute-done.9.third_ref
  48.9 0.8 %merge.1 = (f32[128,128]{1,0:T(8,128)S(1)}, f32[128,128]{1,0:T(8,128)S(1)}, bf16[2,16,128]{2,1,0:T(8,128)(2,1)S(1)}, bf16[16,128]{1,0:T(8,128)(2,1)S(1)}, bf16[16,128]{1,0:T(8,128)(2,1)S(1)}) custom-call(f32[128,128]{1,0:T(8,128)S(1)} %get-tuple-element.33.stats_ref, f32[16,768]{1,0:T(8,128)S(1)} %get-tuple-element.36.own_ref, ...), custom_call_target="tpu_custom_call" | custom-call | flops 67108864 | bytes 2097152 | tf_op jit(solution)/shard_map/merge/pallas_call | solution.py:750
  49.7 0.0 collective-permute-start.10
  49.7 6.3 %collective-permute-start.11 = (bf16[16,128]{1,0:T(8,128)(2,1)S(1)}, bf16[16,128]{1,0:T(8,128)(2,1)S(1)}, u32[]{:S(2)}, u32[]{:S(2)}) collective-permute-start(bf16[16,128]{1,0:T(8,128)(2,1)S(1)} %get-tuple-element.45), channel_id=1, source_target_pairs={{1,2},{3,4},{5,6},{7,8},{9,10},{11,12},{13,14},{15,16},{17,18},{19... | collective-permute-start | bytes 12296 | tf_op jit(solution)/shard_map/ppermute | solution.py:775
  56.1 4.7 %pair_grad.1 = bf16[128,256,128]{2,1,0:T(8,128)(2,1)} custom-call(f32[16,16,8,256]{3,2,1,0:T(8,128)S(1)} %get-tuple-element.48.prob_ref, f32[16,16,8,256]{3,2,1,0:T(8,128)S(1)} %get-tuple-element.49.grad_ref, f32[128,128]{1,0:T(8,128)S(1)} %get-tuple-element.50.scale_ref, f32[128,128]{1,0:T(8,128)S(1)} %get-tuple-element.51.diag_ref, ...), custom_call_target="tpu_custom_call" | custom-call | flops 1073741824 | bytes 14680064 | tf_op jit(solution)/shard_map/pair_grad/pallas_call | solution.py:777
  60.8 0.0 collective-permute-done.10.near_ref
  60.8 0.0 collective-permute-done.11.far_ref
  60.8 0.8 %atom_out.1 = bf16[128,128]{1,0:T(8,128)(2,1)} custom-call(bf16[16,128]{1,0:T(8,128)(2,1)S(1)} %collective-permute-done.10.near_ref, bf16[16,128]{1,0:T(8,128)(2,1)S(1)} %collective-permute-done.11.far_ref, bf16[2,16,128]{2,1,0:T(8,128)(2,1)S(1)} %get-tuple-element.46.low_ref, bf16[144,128]{1,0:T(8,128)(2,1)S(1)} %get-tuple-element.47.hidden_ref), custom_call_target="tpu_custom_call" | custom-call | flops 2097152 | bytes 131072 | tf_op jit(solution)/shard_map/atom_out/pallas_call | solution.py:789
  (2 shorter events, 0.0 us)
Async XLA Ops:
  0.6 9.2 %copy-start = (bf16[128,16]{0,1:T(8,128)(2,1)S(1)}, bf16[128,16]{0,1:T(8,128)(2,1)}, u32[]{:S(2)}) copy-start(bf16[128,16]{0,1:T(8,128)(2,1)} %param.27) | copy-start | bytes 12292
  1.6 12.2 %collective-permute-start = (bf16[464,128]{1,0:T(8,128)(2,1)S(1)}, bf16[464,128]{1,0:T(8,128)(2,1)S(1)}, u32[]{:S(2)}, u32[]{:S(2)}) collective-permute-start(bf16[464,128]{1,0:T(8,128)(2,1)S(1)} %get-tuple-element.27), channel_id=1, source_target_pairs={{0,1},{1,0},{2,3},{3,2},{4,5},{5,4},{6,7},{7,6},{8,9},{9,8},{10,11... | collective-permute-start | bytes 356360 | tf_op jit(solution)/shard_map/ppermute | solution.py:621
  1.7 12.1 %collective-permute-start.1 = (bf16[464,128]{1,0:T(8,128)(2,1)S(1)}, bf16[464,128]{1,0:T(8,128)(2,1)S(1)}, u32[]{:S(2)}, u32[]{:S(2)}) collective-permute-start(bf16[464,128]{1,0:T(8,128)(2,1)S(1)} %get-tuple-element.28), channel_id=1, source_target_pairs={{1,2},{3,4},{5,6},{7,8},{9,10},{11,12},{13,14},{15,16},{17,18},{19... | collective-permute-start | bytes 356360 | tf_op jit(solution)/shard_map/ppermute | solution.py:622
  17.8 5.2 %collective-permute-start.2 = (bf16[16,896]{1,0:T(8,128)(2,1)S(1)}, bf16[16,896]{1,0:T(8,128)(2,1)S(1)}, u32[]{:S(2)}, u32[]{:S(2)}) collective-permute-start(bf16[16,896]{1,0:T(8,128)(2,1)S(1)} %get-tuple-element.30.own_ref), channel_id=1, source_target_pairs={{0,1},{1,0},{2,3},{3,2},{4,5},{5,4},{6,7},{7,6},{8,9},{9,8},{10,11... | collective-permute-start | bytes 86024 | tf_op jit(solution)/shard_map/ppermute | solution.py:684
  17.9 16.0 %all-to-all-start = ((bf16[16,16,768]{2,1,0:T(8,128)(2,1)}), bf16[16,16,768]{2,1,0:T(8,128)(2,1)S(1)}, u32[]{:S(2)}, u32[]{:S(2)}) async-start(bf16[16,16,768]{2,1,0:T(8,128)(2,1)} %get-tuple-element.29), calls=%async_computation | async-start | bytes 786432 | tf_op jit(solution)/shard_map/all_to_all | solution.py:685
  23.0 9.8 %collective-permute-start.5 = (bf16[2,16,896]{2,1,0:T(8,128)(2,1)S(1)}, bf16[2,16,896]{2,1,0:T(8,128)(2,1)S(1)}, u32[]{:S(2)}, u32[]{:S(2)}) collective-permute-start(bf16[2,16,896]{2,1,0:T(8,128)(2,1)S(1)} %stack.1.own_ref), channel_id=1, source_target_pairs={{0,6},{1,7},{2,0},{3,1},{4,2},{5,3},{6,4},{7,5},{8,14},{9,15},{10,... | collective-permute-start | bytes 172040 | tf_op jit(solution)/shard_map/ppermute | solution.py:695
  27.8 5.8 %collective-permute-start.4 = (bf16[2,16,896]{2,1,0:T(8,128)(2,1)S(1)}, bf16[2,16,896]{2,1,0:T(8,128)(2,1)S(1)}, u32[]{:S(2)}, u32[]{:S(2)}) collective-permute-start(bf16[2,16,896]{2,1,0:T(8,128)(2,1)S(1)} %stack.1.own_ref), channel_id=1, source_target_pairs={{0,4},{1,5},{2,6},{3,7},{4,0},{5,1},{6,2},{7,3},{8,12},{9,13},{10,... | collective-permute-start | bytes 172040 | tf_op jit(solution)/shard_map/ppermute | solution.py:695
  27.8 6.0 %collective-permute-start.3 = (bf16[2,16,896]{2,1,0:T(8,128)(2,1)S(1)}, bf16[2,16,896]{2,1,0:T(8,128)(2,1)S(1)}, u32[]{:S(2)}, u32[]{:S(2)}) collective-permute-start(bf16[2,16,896]{2,1,0:T(8,128)(2,1)S(1)} %stack.1.own_ref), channel_id=1, source_target_pairs={{0,2},{1,3},{2,4},{3,5},{4,6},{5,7},{6,0},{7,1},{8,10},{9,11},{10,... | collective-permute-start | bytes 172040 | tf_op jit(solution)/shard_map/ppermute | solution.py:695
  39.4 1.4 %collective-permute-start.6 = (bf16[4,16,1024]{2,1,0:T(8,128)(2,1)S(1)}, bf16[4,16,1024]{2,1,0:T(8,128)(2,1)S(1)}, u32[]{:S(2)}, u32[]{:S(2)}) collective-permute-start(bf16[4,16,1024]{2,1,0:T(8,128)(2,1)S(1)} %get-tuple-element.35), channel_id=1, source_target_pairs={{0,1},{1,0},{2,3},{3,2},{4,5},{5,4},{6,7},{7,6},{8,9},{9,8},{10,11... | collective-permute-start | bytes 393224 | tf_op jit(solution)/shard_map/ppermute | solution.py:737
  41.2 5.5 %collective-permute-start.7 = (bf16[16,1792]{1,0:T(8,128)(2,1)S(1)}, bf16[16,1792]{1,0:T(8,128)(2,1)S(1)}, u32[]{:S(2)}, u32[]{:S(2)}) collective-permute-start(bf16[16,1792]{1,0:T(8,128)(2,1)S(1)} %get-tuple-element.38), channel_id=1, source_target_pairs={{0,2},{1,3},{2,4},{3,5},{4,6},{5,7},{6,0},{7,1},{8,10},{9,11},{10,... | collective-permute-start | bytes 172040 | tf_op jit(solution)/shard_map/ppermute | solution.py:748
  42.7 5.7 %collective-permute-start.8 = (bf16[16,1792]{1,0:T(8,128)(2,1)S(1)}, bf16[16,1792]{1,0:T(8,128)(2,1)S(1)}, u32[]{:S(2)}, u32[]{:S(2)}) collective-permute-start(bf16[16,1792]{1,0:T(8,128)(2,1)S(1)} %get-tuple-element.39), channel_id=1, source_target_pairs={{0,4},{1,5},{2,6},{3,7},{4,0},{5,1},{6,2},{7,3},{8,12},{9,13},{10,... | collective-permute-start | bytes 172040 | tf_op jit(solution)/shard_map/ppermute | solution.py:748
  44.7 4.2 %collective-permute-start.9 = (bf16[16,1792]{1,0:T(8,128)(2,1)S(1)}, bf16[16,1792]{1,0:T(8,128)(2,1)S(1)}, u32[]{:S(2)}, u32[]{:S(2)}) collective-permute-start(bf16[16,1792]{1,0:T(8,128)(2,1)S(1)} %get-tuple-element.40), channel_id=1, source_target_pairs={{0,6},{1,7},{2,0},{3,1},{4,2},{5,3},{6,4},{7,5},{8,14},{9,15},{10,... | collective-permute-start | bytes 172040 | tf_op jit(solution)/shard_map/ppermute | solution.py:748
  49.7 11.1 %collective-permute-start.10 = (bf16[16,128]{1,0:T(8,128)(2,1)S(1)}, bf16[16,128]{1,0:T(8,128)(2,1)S(1)}, u32[]{:S(2)}, u32[]{:S(2)}) collective-permute-start(bf16[16,128]{1,0:T(8,128)(2,1)S(1)} %get-tuple-element.44), channel_id=1, source_target_pairs={{0,1},{1,0},{2,3},{3,2},{4,5},{5,4},{6,7},{7,6},{8,9},{9,8},{10,11... | collective-permute-start | bytes 12296 | tf_op jit(solution)/shard_map/ppermute | solution.py:774
  49.7 11.1 %collective-permute-start.11 = (bf16[16,128]{1,0:T(8,128)(2,1)S(1)}, bf16[16,128]{1,0:T(8,128)(2,1)S(1)}, u32[]{:S(2)}, u32[]{:S(2)}) collective-permute-start(bf16[16,128]{1,0:T(8,128)(2,1)S(1)} %get-tuple-element.45), channel_id=1, source_target_pairs={{1,2},{3,4},{5,6},{7,8},{9,10},{11,12},{13,14},{15,16},{17,18},{19... | collective-permute-start | bytes 12296 | tf_op jit(solution)/shard_map/ppermute | solution.py:775

commit v4 on v3

--- a/solution.py
+++ b/solution.py
@@ -71,9 +71,13 @@
     return jnp.where(rows % GROUP == member, head_rows, 0.0).astype(BF16)
 
 
-def pair_bias_kernel(
-    first, pair_ref, head_ref, out_ref, tile_ref, bias_ref, arrived, left
-):
+def pair_bias_kernel(first, pair_ref, head_ref, *refs):
+    *brought, tile_ref, bias_ref, arrived, left, came = refs
+    extra = len(brought) // 2
+    out_ref = brought[extra]
+    extras = [
+        pltpu.make_async_copy(brought[n], brought[extra + 1 + n], came.at[n]) for n in range(extra)
+    ]
     groups = out_ref.shape[0]
     window = min(8, groups)
 
@@ -87,6 +91,8 @@
 
     for g in range(window):
         copy(g).start()
+    for extra_copy in extras:
+        extra_copy.start()
     weight = head_ref[...].astype(F32).reshape(HT, GROUP, 128)[:, 0].astype(BF16)
 
     def step(g, carry):
@@ -102,12 +108,25 @@
         leave(g).start()
         return carry
 
-    lax.fori_loop(0, groups, step, 0)
+    lax.fori_loop(0, groups, step, 0, unroll=groups)
     for g in range(groups):
         leave(g).wait()
-
-
-def pack_kernel(shift_ref, atoms_ref, bias_ref, cot_ref, token_ref, near_ref, far_ref):
+    for extra_copy in extras:
+        extra_copy.wait()
+
+
+def pack_kernel(
+    shift_ref,
+    count_ref,
+    mask_ref,
+    atoms_ref,
+    bias_ref,
+    cot_ref,
+    token_ref,
+    near_ref,
+    far_ref,
+    side_ref,
+):
     row, col = place()
     odd = lax.rem(col, 2)
     line = iota((AUX, 128), 0)
@@ -115,7 +134,8 @@
     aux = jnp.where(line == 0, token_ref[...] - (16 * device - 17), 0)
     for n in range(4):
         aux = jnp.where(line == 1 + n, shift_ref[n], aux)
-    aux = aux.astype(F32).astype(BF16)
+    wide = aux.astype(F32)
+    aux = wide.astype(BF16)
 
     def fill(out_ref, at):
         out_ref[0:128] = atoms_ref[...]
@@ -124,6 +144,15 @@
         out_ref[384:448] = cot_ref[at : at + HALF]
         out_ref[448:464] = aux
 
+    side_ref[0:16] = wide
+    count = jnp.zeros((16, 128), jnp.int32)
+    live = jnp.zeros((16, 128), jnp.int32)
+    for t in range(16):
+        count = jnp.where(line == t, count_ref[t], count)
+        live = jnp.where(line == t, mask_ref[t], live)
+    side_ref[16:32] = count.astype(F32)
+    side_ref[32:48] = live.astype(F32)
+
     @pl.when(odd == 1)
     def _():
         fill(near_ref, 0)
@@ -136,16 +165,12 @@
 
 
 def atom_kernel(
-    shift_ref,
-    count_ref,
-    mask_ref,
+    side_ref,
     near_ref,
     far_ref,
     atoms_ref,
     bias_ref,
     cot_ref,
-    token_ref,
-    after_ref,
     w_qkv_ref,
     w_out_ref,
     w_pool_ref,
@@ -203,7 +228,7 @@
             shift = next_ref[449 + local : 450 + local].astype(F32).astype(jnp.int32)
         else:
             source, local = None, block - 2
-            shift = jnp.full((1, 128), shift_ref[local], jnp.int32)
+            shift = side_ref[1 + local : 2 + local].astype(jnp.int32)
         for h in range(HA):
             if source is None:
                 biases.append(bias_ref[h, 32 * local : 32 * local + 32])
@@ -241,29 +266,23 @@
     base = jnp.concatenate([wide[128:320], wide[64:128]], axis=0)
     hidden = (base + dot(mixture, w_out_ref[...])).astype(BF16)
     hidden_ref[0:128] = hidden[:128]
-    relative = (token_ref[...] - (16 * device - 16)).astype(F32)
+    relative = side_ref[0:1] - 1.0
     hidden_ref[128:144] = jnp.broadcast_to(relative, (16, 128)).astype(BF16)
     lifted = jnp.maximum(dot(hidden, w_pool_ref[...]), 0.0)
-    own_token = (token_ref[...] - 16 * device).astype(F32)
+    own_token = side_ref[0:1] - 17.0
     prev_token = prev_ref[448:449].astype(F32) - 33.0
     next_token = next_ref[448:449].astype(F32) - 1.0
     beside = jnp.where(iota((1, 128), 1) < HALF, next_token, prev_token)
     token = jnp.concatenate([own_token, beside], axis=1)
     select = jnp.where(iota((16, 256), 0).astype(F32) == token, 1.0, 0.0).astype(BF16)
     high, low = split(lifted)
-    line = iota((16, 128), 0)
-    count = jnp.zeros((16, 128), jnp.int32)
-    live = jnp.zeros((16, 128), jnp.int32)
-    for t in range(16):
-        count = jnp.where(line == t, count_ref[t], count)
-        live = jnp.where(line == t, mask_ref[t], live)
-    count = jnp.concatenate([count.astype(F32)] * 6, axis=1)
+    count = jnp.concatenate([side_ref[16:32]] * 6, axis=1)
     pooled = (dot(select, high) + dot(select, low)) / count
     pooled_ref[...] = pooled
     normed = normal(pooled).astype(BF16)
     cot = jnp.concatenate([cot_ref[...], next_ref[384:448], prev_ref[384:448]], axis=0)
     grad_up = dot(select, cot).astype(BF16)
-    live = jnp.concatenate([live] * 6, axis=1)
+    live = jnp.concatenate([side_ref[32:48]] * 6, axis=1)
     marked = jnp.where(live > 0, normed.astype(F32), MASKED).astype(BF16)
     for r in range(to_row_ref.shape[0]):
         to_row_ref[r] = marked
@@ -328,7 +347,7 @@
             )
     copies.append((pooled_ref, pooled_out_ref))
     copies = [pltpu.make_async_copy(a, b, arrived.at[n]) for n, (a, b) in enumerate(copies)]
-    for copy in copies:
+    for copy in copies[:5]:
         copy.start()
 
     row, col = place()
@@ -339,6 +358,8 @@
         rows_ref[pl.ds(pl.multiple_of(there + 16, 16), 16)] = part_ref[1]
     key = dot(keys_ref[...], w_kv_ref[:, :768]).astype(BF16)
     value = dot(keys_ref[...], w_kv_ref[:, 768:]).astype(BF16)
+    for copy in copies[5:]:
+        copy.start()
     for copy in copies[:2]:
         copy.wait()
     query = dot(rows_ref[:, :768], inner_ref[...]).astype(BF16)
@@ -555,7 +576,7 @@
         copy(g).start()
         return following
 
-    lax.fori_loop(0, groups, step, score_of(0), unroll=2)
+    lax.fori_loop(0, groups, step, score_of(0), unroll=groups)
     for g in range(groups):
         copy(g).wait()
 
@@ -603,16 +624,18 @@
 
     tokens = atom_token.reshape(1, 128)
     payload = jax.ShapeDtypeStruct((464, 128), BF16)
-    near, far = pl.pallas_call(
+    near, far, side = pl.pallas_call(
         pack_kernel,
-        in_specs=[SMEM] + [VMEM] * 4,
-        out_specs=[VMEM, VMEM],
-        out_shape=[payload, payload],
+        in_specs=[SMEM] * 3 + [VMEM] * 4,
+        out_specs=[VMEM] * 3,
+        out_shape=[payload, payload, pltpu.VMEM((48, 128), F32)],
         compiler_params=params(4),
         name="pack",
         cost_estimate=pl.CostEstimate(flops=0, bytes_accessed=1 << 20, transcendentals=0),
     )(
         outside(key_shift),
+        outside(token_atoms),
+        outside(token_mask),
         outside(atoms),
         outside(atom_bias),
         outside(cotangent),
@@ -623,32 +646,44 @@
 
     tile = pair.reshape(128, 256, 128)
     head_rows = jnp.repeat(jnp.transpose(w_bias), GROUP, axis=0)
-    def pair_bias(first, groups, name):
+    def pair_bias(first, groups, name, *brought):
         return pl.pallas_call(
             functools.partial(pair_bias_kernel, first),
-            in_specs=[HBM, VMEM],
-            out_specs=HBM,
-            out_shape=pltpu.HBM((groups, HT, GROUP, 256), F32),
+            in_specs=[HBM, VMEM] + [HBM] * len(brought),
+            out_specs=[HBM] + [VMEM] * len(brought),
+            out_shape=[pltpu.HBM((groups, HT, GROUP, 256), F32)]
+            + [pltpu.VMEM(value.shape, value.dtype) for value in brought],
             scratch_shapes=[
                 pltpu.VMEM((groups * GROUP, 256, 128), BF16),
                 pltpu.VMEM((groups, HT, GROUP, 256), F32),
                 pltpu.SemaphoreType.DMA((groups,)),
                 pltpu.SemaphoreType.DMA((groups,)),
+                pltpu.SemaphoreType.DMA((max(len(brought), 1),)),
             ],
             compiler_params=params(14),
             name=name,
             cost_estimate=pl.CostEstimate(
                 flops=groups << 26, bytes_accessed=groups << 19, transcendentals=0
             ),
-        )(outside(tile), head_rows)
+        )(outside(tile), head_rows, *[outside(value) for value in brought])
 
     half = EARLY
-    early = pair_bias(0, half, "pair_bias_early")
-    late = pair_bias(half, 16 - half, "pair_bias_late")
+    early, *atom_inputs = pair_bias(
+        0,
+        half,
+        "pair_bias_early",
+        atoms,
+        atom_bias,
+        cotangent,
+        w_atom_qkv,
+        w_atom_out,
+        w_pool,
+    )
+    (late,) = pair_bias(half, 16 - half, "pair_bias_late")
 
     hidden, pooled, to_row, to_col, token_kv = pl.pallas_call(
         atom_kernel,
-        in_specs=[SMEM] * 3 + [VMEM] * 6 + [pl.BlockSpec(memory_space=pl.ANY)] + [VMEM] * 3 + [HBM],
+        in_specs=[VMEM] * 9 + [HBM],
         out_specs=[VMEM] * 5,
         out_shape=[
             pltpu.VMEM((144, 128), BF16),
@@ -666,19 +701,10 @@
         name="atom_stage",
         cost_estimate=pl.CostEstimate(flops=1 << 28, bytes_accessed=2 << 20, transcendentals=1 << 17),
     )(
-        outside(key_shift),
-        outside(token_atoms),
-        outside(token_mask),
+        inside(side),
         near,
         far,
-        outside(atoms),
-        outside(atom_bias),
-        outside(cotangent),
-        outside(tokens),
-        outside(early),
-        outside(w_atom_qkv),
-        outside(w_atom_out),
-        outside(w_pool),
+        *[inside(value) for value in atom_inputs],
         outside(w_token_qkv),
     )
     partner = lax.ppermute(to_col, "col", core_pairs)

time: 61.9 us -> 60.1 us (0.971)
  Pallas kernels: 25 us -> 23.1 us
    pallas_call x2, Pallas kernels: 4.9 us -> 3.78 us  [the longest x1 2.81 us: shards(): pl.pallas_call(atom_kernel, in_specs=[VMEM] * 9 + [HBM], out_specs=[VMEM]...]
    pallas_call x1, Pallas kernels: 4.71 us -> 3.85 us  [shards(): pl.pallas_call(pair_grad_kernel, in_specs=[VMEM] * 5, out_specs=HBM, out_...]
where the time goes in v4:
time: 60.1 us; the launch traced here: 59.8 us
  starting transfers between devices  30.1 us (50%)
  Pallas kernels  23.1 us (38%)
  waiting for transfers between devices  5.77 us (10%)
  between operations  0.81 us (1%)
    ppermute x2, starting transfers between devices, shards(): far = lax.ppermute(far, ('row', 'col'), chip_pairs)  14.6 us
    pallas_call x2, Pallas kernels, pair_bias(): pl.pallas_call(functools.partial(pair_bias_kernel, first), in_specs=[HBM,...  7.95 us
    ppermute x3, starting transfers between devices, shards(): shifted = [lax.ppermute(own, 'col', chip_shift(s)) for s in range(1, 4)]  5.76 us
    pallas_call x1, Pallas kernels, shards(): pl.pallas_call(token_kernel, in_specs=[VMEM] * 5 + [HBM] * 2 + [VMEM] + [...  5.51 us
    all_to_all x1, starting transfers between devices, shards(): keys = lax.all_to_all(to_row, 'row', 0, 0).reshape(256, 768)  5.06 us
    ppermute x3, starting transfers between devices, shards(): lax.ppermute(part, 'col', chip_shift(s + 1))  4.4 us
    pallas_call x1, Pallas kernels, shards(): pl.pallas_call(pair_grad_kernel, in_specs=[VMEM] * 5, out_specs=HBM, out_...  3.85 us
    ppermute x3, waiting for transfers between devices, shards(): lax.ppermute(part, 'col', chip_shift(s + 1))  3.32 us
  transfers between devices with their start and end apart: 13, of which 6 were waited for; matrix products, arithmetic and copies ran while one was open for 0% of the time, Pallas kernels for 20%

profile of v4, /device:TPU:8, one launch (start us, length us, event | category | flops | bytes accessed | tf_op | source)
XLA Modules:
  0.0 59.8 jit_solution(13567357834933606741)
XLA Ops:
  0.6 0.0 copy-start
  0.6 1.0 %pack.1 = (bf16[464,128]{1,0:T(8,128)(2,1)S(1)}, bf16[464,128]{1,0:T(8,128)(2,1)S(1)}, f32[48,128]{1,0:T(8,128)S(1)}) custom-call(s32[4]{0:T(128)} %shift_ref.1, s32[16]{0:T(128)} %count_ref.1, s32[16]{0:T(128)} %mask_ref.1, bf16[128,128]{1,0:T(8,128)(2,1)} %refs_0_.1, bf16[4,128,128]{2,1,0:T(8,128)(2,1)} %refs_1_.1, bf16[128,128]{1,0:T(8,128)(2,1)} %refs_2_.1, ...), custom_call_target="tpu_custom_call" | custom-call | bytes 1048576 | tf_op jit(solution)/shard_map/pack/pallas_call | solution.py:627
  1.6 0.1 collective-permute-start
  1.7 8.1 %collective-permute-start.1 = (bf16[464,128]{1,0:T(8,128)(2,1)S(1)}, bf16[464,128]{1,0:T(8,128)(2,1)S(1)}, u32[]{:S(2)}, u32[]{:S(2)}) collective-permute-start(bf16[464,128]{1,0:T(8,128)(2,1)S(1)} %get-tuple-element.37), channel_id=1, source_target_pairs={{1,2},{3,4},{5,6},{7,8},{9,10},{11,12},{13,14},{15,16},{17,18},{19... | collective-permute-start | bytes 356360 | tf_op jit(solution)/shard_map/ppermute | solution.py:645
  9.8 0.0 copy-done
  9.9 4.0 %pair_bias_early.1 = (f32[8,16,8,256]{3,2,1,0:T(8,128)}, bf16[128,128]{1,0:T(8,128)(2,1)S(1)}, bf16[4,128,128]{2,1,0:T(8,128)(2,1)S(1)}, bf16[128,128]{1,0:T(8,1...) custom-call(bf16[128,256,128]{2,1,0:T(8,128)(2,1)} %bitcast.11, ...), custom_call_target="tpu_custom_call" | custom-call | flops 536870912 | bytes 4194304 | tf_op jit(solution)/shard_map/pair_bias_early/pallas_call | solution.py:650
  13.9 0.0 collective-permute-done.near_ref
  13.9 0.0 collective-permute-done.1.far_ref
  13.9 2.8 %atom_stage.1 = (bf16[144,128]{1,0:T(8,128)(2,1)S(1)}, f32[16,768]{1,0:T(8,128)}, bf16[16,16,768]{2,1,0:T(8,128)(2,1)}, bf16[16,896]{1,0:T(8,128)(2,1)S(1)}, bf16[768,1536]{1,0:T(8,128)(2,1)S(1)}) custom-call(f32[48,128]{1,0:T(8,128)S(1)} %get-tuple-element.35.side_ref, bf16[464,128]{1,0:T(8,128)(2,1)S(1)} %collective-permute-done.near_ref, ...), custom_call_target="tpu_custom_call" | custom-call | flops 268435456 | bytes 2097152 | tf_op jit(solution)/shard_map/atom_stage/pallas_call | solution.py:684
  16.7 0.1 collective-permute-start.2
  16.8 5.1 %all-to-all-start = ((bf16[16,16,768]{2,1,0:T(8,128)(2,1)}), bf16[16,16,768]{2,1,0:T(8,128)(2,1)S(1)}, u32[]{:S(2)}, u32[]{:S(2)}) async-start(bf16[16,16,768]{2,1,0:T(8,128)(2,1)} %get-tuple-element.44), calls=%async_computation | async-start | bytes 786432 | tf_op jit(solution)/shard_map/all_to_all | solution.py:711
  21.9 0.0 collective-permute-done.2.partner_ref
  21.9 4.8 %collective-permute-start.5 = (bf16[2,16,896]{2,1,0:T(8,128)(2,1)S(1)}, bf16[2,16,896]{2,1,0:T(8,128)(2,1)S(1)}, u32[]{:S(2)}, u32[]{:S(2)}) collective-permute-start(bf16[2,16,896]{2,1,0:T(8,128)(2,1)S(1)} %stack.1.own_ref), channel_id=1, source_target_pairs={{0,6},{1,7},{2,0},{3,1},{4,2},{5,3},{6,4},{7,5},{8,14},{9,15},{10,... | collective-permute-start | bytes 172040 | tf_op jit(solution)/shard_map/ppermute | solution.py:721
  26.7 0.0 collective-permute-start.4
  26.7 0.9 %collective-permute-start.3 = (bf16[2,16,896]{2,1,0:T(8,128)(2,1)S(1)}, bf16[2,16,896]{2,1,0:T(8,128)(2,1)S(1)}, u32[]{:S(2)}, u32[]{:S(2)}) collective-permute-start(bf16[2,16,896]{2,1,0:T(8,128)(2,1)S(1)} %stack.1.own_ref), channel_id=1, source_target_pairs={{0,2},{1,3},{2,4},{3,5},{4,6},{5,7},{6,0},{7,1},{8,10},{9,11},{10,... | collective-permute-start | bytes 172040 | tf_op jit(solution)/shard_map/ppermute | solution.py:721
  27.7 3.9 %pair_bias_late.1.late_ref = f32[8,16,8,256]{3,2,1,0:T(8,128)} custom-call(bf16[128,256,128]{2,1,0:T(8,128)(2,1)} %bitcast.12, bf16[128,128]{1,0:T(8,128)(2,1)S(1)} %broadcast_bitcast_fusion.head_ref), custom_call_target="tpu_custom_call" | custom-call | flops 536870912 | bytes 4194304 | tf_op jit(solution)/shard_map/pair_bias_late/pallas_call | solution.py:650
  31.6 0.0 collective-permute-done.5.third_ref
  31.6 0.9 %collective-permute-done.4.second_ref = bf16[2,16,896]{2,1,0:T(8,128)(2,1)S(1)} collective-permute-done((bf16[2,16,896]{2,1,0:T(8,128)(2,1)S(1)}, bf16[2,16,896]{2,1,0:T(8,128)(2,1)S(1)}, u32[]{:S(2)}, u32[]{:S(2)}) %collective-permute-start.4) | collective-permute-done | bytes 57376 | tf_op jit(solution)/shard_map/ppermute | solution.py:721
  32.5 0.2 collective-permute-done.3.first_ref
  32.7 0.0 all-to-all-done
  32.7 5.5 %token_stage.1 = (f32[16,16,8,256]{3,2,1,0:T(8,128)S(1)}, f32[16,16,8,256]{3,2,1,0:T(8,128)S(1)}, f32[128,128]{1,0:T(8,128)S(1)}, f32[4,16,768]{2,1,0:T(8,128)S(...) custom-call(bf16[256,768]{1,0:T(8,128)(2,1)S(1)} %bitcast.10, ...), custom_call_target="tpu_custom_call" | custom-call | flops 2147483648 | bytes 12582912 | tf_op jit(solution)/shard_map/token_stage/pallas_call | solution.py:727
  38.2 0.1 collective-permute-start.6
  38.3 1.3 %collective-permute-done.6.given_ref = bf16[4,16,1024]{2,1,0:T(8,128)(2,1)S(1)} collective-permute-done((bf16[4,16,1024]{2,1,0:T(8,128)(2,1)S(1)}, bf16[4,16,1024]{2,1,0:T(8,128)(2,1)S(1)}, u32[]{:S(2)}, u32[]{:S(2)}) %collective-permute-start.6) | collective-permute-done | bytes 131104 | tf_op jit(solution)/shard_map/ppermute | solution.py:763
  39.7 0.4 fold.1
  40.0 1.6 %collective-permute-start.7 = (bf16[16,1792]{1,0:T(8,128)(2,1)S(1)}, bf16[16,1792]{1,0:T(8,128)(2,1)S(1)}, u32[]{:S(2)}, u32[]{:S(2)}) collective-permute-start(bf16[16,1792]{1,0:T(8,128)(2,1)S(1)} %get-tuple-element.54), channel_id=1, source_target_pairs={{0,2},{1,3},{2,4},{3,5},{4,6},{5,7},{6,0},{7,1},{8,10},{9,11},{10,... | collective-permute-start | bytes 172040 | tf_op jit(solution)/shard_map/ppermute | solution.py:774
  41.6 2.0 %collective-permute-start.8 = (bf16[16,1792]{1,0:T(8,128)(2,1)S(1)}, bf16[16,1792]{1,0:T(8,128)(2,1)S(1)}, u32[]{:S(2)}, u32[]{:S(2)}) collective-permute-start(bf16[16,1792]{1,0:T(8,128)(2,1)S(1)} %get-tuple-element.55), channel_id=1, source_target_pairs={{0,4},{1,5},{2,6},{3,7},{4,0},{5,1},{6,2},{7,3},{8,12},{9,13},{10,... | collective-permute-start | bytes 172040 | tf_op jit(solution)/shard_map/ppermute | solution.py:774
  43.6 0.9 %collective-permute-start.9 = (bf16[16,1792]{1,0:T(8,128)(2,1)S(1)}, bf16[16,1792]{1,0:T(8,128)(2,1)S(1)}, u32[]{:S(2)}, u32[]{:S(2)}) collective-permute-start(bf16[16,1792]{1,0:T(8,128)(2,1)S(1)} %get-tuple-element.56), channel_id=1, source_target_pairs={{0,6},{1,7},{2,0},{3,1},{4,2},{5,3},{6,4},{7,5},{8,14},{9,15},{10,... | collective-permute-start | bytes 172040 | tf_op jit(solution)/shard_map/ppermute | solution.py:774
  44.5 1.1 %collective-permute-done.7.first_ref = bf16[16,1792]{1,0:T(8,128)(2,1)S(1)} collective-permute-done((bf16[16,1792]{1,0:T(8,128)(2,1)S(1)}, bf16[16,1792]{1,0:T(8,128)(2,1)S(1)}, u32[]{:S(2)}, u32[]{:S(2)}) %collective-permute-start.7) | collective-permute-done | bytes 57376 | tf_op jit(solution)/shard_map/ppermute | solution.py:774
  45.5 1.8 %collective-permute-done.8.second_ref = bf16[16,1792]{1,0:T(8,128)(2,1)S(1)} collective-permute-done((bf16[16,1792]{1,0:T(8,128)(2,1)S(1)}, bf16[16,1792]{1,0:T(8,128)(2,1)S(1)}, u32[]{:S(2)}, u32[]{:S(2)}) %collective-permute-start.8) | collective-permute-done | bytes 57376 | tf_op jit(solution)/shard_map/ppermute | solution.py:774
  47.3 0.5 collective-permute-done.9.third_ref
  47.8 0.8 %merge.1 = (f32[128,128]{1,0:T(8,128)S(1)}, f32[128,128]{1,0:T(8,128)S(1)}, bf16[2,16,128]{2,1,0:T(8,128)(2,1)S(1)}, bf16[16,128]{1,0:T(8,128)(2,1)S(1)}, bf16[16,128]{1,0:T(8,128)(2,1)S(1)}) custom-call(f32[128,128]{1,0:T(8,128)S(1)} %get-tuple-element.49.stats_ref, f32[16,768]{1,0:T(8,128)S(1)} %get-tuple-element.52.own_ref, ...), custom_call_target="tpu_custom_call" | custom-call | flops 67108864 | bytes 2097152 | tf_op jit(solution)/shard_map/merge/pallas_call | solution.py:776
  48.6 0.0 collective-permute-start.10
  48.6 6.5 %collective-permute-start.11 = (bf16[16,128]{1,0:T(8,128)(2,1)S(1)}, bf16[16,128]{1,0:T(8,128)(2,1)S(1)}, u32[]{:S(2)}, u32[]{:S(2)}) collective-permute-start(bf16[16,128]{1,0:T(8,128)(2,1)S(1)} %get-tuple-element.61), channel_id=1, source_target_pairs={{1,2},{3,4},{5,6},{7,8},{9,10},{11,12},{13,14},{15,16},{17,18},{19... | collective-permute-start | bytes 12296 | tf_op jit(solution)/shard_map/ppermute | solution.py:801
  55.2 3.8 %pair_grad.1 = bf16[128,256,128]{2,1,0:T(8,128)(2,1)} custom-call(f32[16,16,8,256]{3,2,1,0:T(8,128)S(1)} %get-tuple-element.64.prob_ref, f32[16,16,8,256]{3,2,1,0:T(8,128)S(1)} %get-tuple-element.65.grad_ref, f32[128,128]{1,0:T(8,128)S(1)} %get-tuple-element.66.scale_ref, f32[128,128]{1,0:T(8,128)S(1)} %get-tuple-element.67.diag_ref, ...), custom_call_target="tpu_custom_call" | custom-call | flops 1073741824 | bytes 14680064 | tf_op jit(solution)/shard_map/pair_grad/pallas_call | solution.py:803
  59.0 0.0 collective-permute-done.10.near_ref
  59.0 0.0 collective-permute-done.11.far_ref
  59.0 0.8 %atom_out.1 = bf16[128,128]{1,0:T(8,128)(2,1)} custom-call(bf16[16,128]{1,0:T(8,128)(2,1)S(1)} %collective-permute-done.10.near_ref, bf16[16,128]{1,0:T(8,128)(2,1)S(1)} %collective-permute-done.11.far_ref, bf16[2,16,128]{2,1,0:T(8,128)(2,1)S(1)} %get-tuple-element.62.low_ref, bf16[144,128]{1,0:T(8,128)(2,1)S(1)} %get-tuple-element.63.hidden_ref), custom_call_target="tpu_custom_call" | custom-call | flops 2097152 | bytes 131072 | tf_op jit(solution)/shard_map/atom_out/pallas_call | solution.py:815
  (2 shorter events, 0.0 us)
Async XLA Ops:
  0.6 9.2 %copy-start = (bf16[128,16]{0,1:T(8,128)(2,1)S(1)}, bf16[128,16]{0,1:T(8,128)(2,1)}, u32[]{:S(2)}) copy-start(bf16[128,16]{0,1:T(8,128)(2,1)} %param.27) | copy-start | bytes 12292
  1.6 12.3 %collective-permute-start = (bf16[464,128]{1,0:T(8,128)(2,1)S(1)}, bf16[464,128]{1,0:T(8,128)(2,1)S(1)}, u32[]{:S(2)}, u32[]{:S(2)}) collective-permute-start(bf16[464,128]{1,0:T(8,128)(2,1)S(1)} %get-tuple-element.36), channel_id=1, source_target_pairs={{0,1},{1,0},{2,3},{3,2},{4,5},{5,4},{6,7},{7,6},{8,9},{9,8},{10,11... | collective-permute-start | bytes 356360 | tf_op jit(solution)/shard_map/ppermute | solution.py:644
  1.7 12.2 %collective-permute-start.1 = (bf16[464,128]{1,0:T(8,128)(2,1)S(1)}, bf16[464,128]{1,0:T(8,128)(2,1)S(1)}, u32[]{:S(2)}, u32[]{:S(2)}) collective-permute-start(bf16[464,128]{1,0:T(8,128)(2,1)S(1)} %get-tuple-element.37), channel_id=1, source_target_pairs={{1,2},{3,4},{5,6},{7,8},{9,10},{11,12},{13,14},{15,16},{17,18},{19... | collective-permute-start | bytes 356360 | tf_op jit(solution)/shard_map/ppermute | solution.py:645
  16.7 5.2 %collective-permute-start.2 = (bf16[16,896]{1,0:T(8,128)(2,1)S(1)}, bf16[16,896]{1,0:T(8,128)(2,1)S(1)}, u32[]{:S(2)}, u32[]{:S(2)}) collective-permute-start(bf16[16,896]{1,0:T(8,128)(2,1)S(1)} %get-tuple-element.45.own_ref), channel_id=1, source_target_pairs={{0,1},{1,0},{2,3},{3,2},{4,5},{5,4},{6,7},{7,6},{8,9},{9,8},{10,11... | collective-permute-start | bytes 86024 | tf_op jit(solution)/shard_map/ppermute | solution.py:710
  16.8 15.9 %all-to-all-start = ((bf16[16,16,768]{2,1,0:T(8,128)(2,1)}), bf16[16,16,768]{2,1,0:T(8,128)(2,1)S(1)}, u32[]{:S(2)}, u32[]{:S(2)}) async-start(bf16[16,16,768]{2,1,0:T(8,128)(2,1)} %get-tuple-element.44), calls=%async_computation | async-start | bytes 786432 | tf_op jit(solution)/shard_map/all_to_all | solution.py:711
  21.9 9.7 %collective-permute-start.5 = (bf16[2,16,896]{2,1,0:T(8,128)(2,1)S(1)}, bf16[2,16,896]{2,1,0:T(8,128)(2,1)S(1)}, u32[]{:S(2)}, u32[]{:S(2)}) collective-permute-start(bf16[2,16,896]{2,1,0:T(8,128)(2,1)S(1)} %stack.1.own_ref), channel_id=1, source_target_pairs={{0,6},{1,7},{2,0},{3,1},{4,2},{5,3},{6,4},{7,5},{8,14},{9,15},{10,... | collective-permute-start | bytes 172040 | tf_op jit(solution)/shard_map/ppermute | solution.py:721
  26.7 5.8 %collective-permute-start.4 = (bf16[2,16,896]{2,1,0:T(8,128)(2,1)S(1)}, bf16[2,16,896]{2,1,0:T(8,128)(2,1)S(1)}, u32[]{:S(2)}, u32[]{:S(2)}) collective-permute-start(bf16[2,16,896]{2,1,0:T(8,128)(2,1)S(1)} %stack.1.own_ref), channel_id=1, source_target_pairs={{0,4},{1,5},{2,6},{3,7},{4,0},{5,1},{6,2},{7,3},{8,12},{9,13},{10,... | collective-permute-start | bytes 172040 | tf_op jit(solution)/shard_map/ppermute | solution.py:721
  26.7 6.0 %collective-permute-start.3 = (bf16[2,16,896]{2,1,0:T(8,128)(2,1)S(1)}, bf16[2,16,896]{2,1,0:T(8,128)(2,1)S(1)}, u32[]{:S(2)}, u32[]{:S(2)}) collective-permute-start(bf16[2,16,896]{2,1,0:T(8,128)(2,1)S(1)} %stack.1.own_ref), channel_id=1, source_target_pairs={{0,2},{1,3},{2,4},{3,5},{4,6},{5,7},{6,0},{7,1},{8,10},{9,11},{10,... | collective-permute-start | bytes 172040 | tf_op jit(solution)/shard_map/ppermute | solution.py:721
  38.2 1.4 %collective-permute-start.6 = (bf16[4,16,1024]{2,1,0:T(8,128)(2,1)S(1)}, bf16[4,16,1024]{2,1,0:T(8,128)(2,1)S(1)}, u32[]{:S(2)}, u32[]{:S(2)}) collective-permute-start(bf16[4,16,1024]{2,1,0:T(8,128)(2,1)S(1)} %get-tuple-element.51), channel_id=1, source_target_pairs={{0,1},{1,0},{2,3},{3,2},{4,5},{5,4},{6,7},{7,6},{8,9},{9,8},{10,11... | collective-permute-start | bytes 393224 | tf_op jit(solution)/shard_map/ppermute | solution.py:763
  40.0 5.5 %collective-permute-start.7 = (bf16[16,1792]{1,0:T(8,128)(2,1)S(1)}, bf16[16,1792]{1,0:T(8,128)(2,1)S(1)}, u32[]{:S(2)}, u32[]{:S(2)}) collective-permute-start(bf16[16,1792]{1,0:T(8,128)(2,1)S(1)} %get-tuple-element.54), channel_id=1, source_target_pairs={{0,2},{1,3},{2,4},{3,5},{4,6},{5,7},{6,0},{7,1},{8,10},{9,11},{10,... | collective-permute-start | bytes 172040 | tf_op jit(solution)/shard_map/ppermute | solution.py:774
  41.6 5.7 %collective-permute-start.8 = (bf16[16,1792]{1,0:T(8,128)(2,1)S(1)}, bf16[16,1792]{1,0:T(8,128)(2,1)S(1)}, u32[]{:S(2)}, u32[]{:S(2)}) collective-permute-start(bf16[16,1792]{1,0:T(8,128)(2,1)S(1)} %get-tuple-element.55), channel_id=1, source_target_pairs={{0,4},{1,5},{2,6},{3,7},{4,0},{5,1},{6,2},{7,3},{8,12},{9,13},{10,... | collective-permute-start | bytes 172040 | tf_op jit(solution)/shard_map/ppermute | solution.py:774
  43.6 4.2 %collective-permute-start.9 = (bf16[16,1792]{1,0:T(8,128)(2,1)S(1)}, bf16[16,1792]{1,0:T(8,128)(2,1)S(1)}, u32[]{:S(2)}, u32[]{:S(2)}) collective-permute-start(bf16[16,1792]{1,0:T(8,128)(2,1)S(1)} %get-tuple-element.56), channel_id=1, source_target_pairs={{0,6},{1,7},{2,0},{3,1},{4,2},{5,3},{6,4},{7,5},{8,14},{9,15},{10,... | collective-permute-start | bytes 172040 | tf_op jit(solution)/shard_map/ppermute | solution.py:774
  48.6 10.4 %collective-permute-start.10 = (bf16[16,128]{1,0:T(8,128)(2,1)S(1)}, bf16[16,128]{1,0:T(8,128)(2,1)S(1)}, u32[]{:S(2)}, u32[]{:S(2)}) collective-permute-start(bf16[16,128]{1,0:T(8,128)(2,1)S(1)} %get-tuple-element.60), channel_id=1, source_target_pairs={{0,1},{1,0},{2,3},{3,2},{4,5},{5,4},{6,7},{7,6},{8,9},{9,8},{10,11... | collective-permute-start | bytes 12296 | tf_op jit(solution)/shard_map/ppermute | solution.py:800
  48.6 10.4 %collective-permute-start.11 = (bf16[16,128]{1,0:T(8,128)(2,1)S(1)}, bf16[16,128]{1,0:T(8,128)(2,1)S(1)}, u32[]{:S(2)}, u32[]{:S(2)}) collective-permute-start(bf16[16,128]{1,0:T(8,128)(2,1)S(1)} %get-tuple-element.61), channel_id=1, source_target_pairs={{1,2},{3,4},{5,6},{7,8},{9,10},{11,12},{13,14},{15,16},{17,18},{19... | collective-permute-start | bytes 12296 | tf_op jit(solution)/shard_map/ppermute | solution.py:801

commit v5 on v4

--- a/solution.py
+++ b/solution.py
@@ -14,6 +14,8 @@
 KW = 128
 SHIFT = 16
 HALF = 64
+GATHER_SHIFTS = (1, 3, 2)
+FOLD_SHIFTS = (2, 1, 3)
 EARLY = 8
 GROUP = 8
 AUX = 16
@@ -352,7 +354,8 @@
 
     row, col = place()
     chip, core = lax.div(col, 2), lax.rem(col, 2)
-    for s, part_ref in enumerate((own_ref, first_ref, second_ref, third_ref)):
+    parts = (own_ref, first_ref, second_ref, third_ref)
+    for s, part_ref in zip((0,) + GATHER_SHIFTS, parts):
         there = lax.rem(chip + 4 - s, 4) * 32
         rows_ref[pl.ds(pl.multiple_of(there, 32), 16)] = part_ref[0]
         rows_ref[pl.ds(pl.multiple_of(there + 16, 16), 16)] = part_ref[1]
@@ -490,8 +493,8 @@
             + given_n * factors[64 + 16 * n : 80 + 16 * n]
         )
     packed = packed_stats(top, total, diag)
-    for s, out_ref in enumerate((first_ref, second_ref, third_ref)):
-        out_ref[:, :768] = mixed_ref[lax.rem(chip + s + 1, 4)].astype(BF16)
+    for s, out_ref in zip(FOLD_SHIFTS, (first_ref, second_ref, third_ref)):
+        out_ref[:, :768] = mixed_ref[lax.rem(chip + s, 4)].astype(BF16)
         for k in range(8):
             out_ref[:, 768 + 128 * k : 896 + 128 * k] = packed[16 * k : 16 * k + 16]
     own_ref[...] = mixed_ref[chip]
@@ -581,7 +584,7 @@
         copy(g).wait()
 
 
-def atom_out_kernel(near_ref, far_ref, low_ref, hidden_ref, out_ref):
+def atom_out_kernel(far_ref, near_ref, low_ref, hidden_ref, out_ref):
     row, col = place()
     odd = lax.rem(col, 2) == 1
     near = near_ref[...].astype(F32)
@@ -718,7 +721,7 @@
         name="stack",
         cost_estimate=pl.CostEstimate(flops=1 << 32, bytes_accessed=1 << 18, transcendentals=0),
     )(inside(to_col), partner)
-    shifted = [lax.ppermute(own, "col", chip_shift(s)) for s in range(1, 4)]
+    shifted = [lax.ppermute(own, "col", chip_shift(s)) for s in GATHER_SHIFTS]
 
     stat = pltpu.VMEM((128, 128), F32)
     swapped = jax.ShapeDtypeStruct((4, 16, 1024), BF16)
@@ -771,7 +774,9 @@
         name="fold",
         cost_estimate=pl.CostEstimate(flops=1 << 26, bytes_accessed=2 << 20, transcendentals=1 << 17),
     )(inside(keep), inside(stats), given)
-    parts = [lax.ppermute(part, "col", chip_shift(s + 1)) for s, part in enumerate(sent)]
+    parts = [
+        lax.ppermute(part, "col", chip_shift(s)) for s, part in zip(FOLD_SHIFTS, sent)
+    ]
 
     scale, diag, low, near, far = pl.pallas_call(
         merge_kernel,
@@ -820,7 +825,7 @@
         compiler_params=params(4),
         name="atom_out",
         cost_estimate=pl.CostEstimate(flops=1 << 21, bytes_accessed=1 << 17, transcendentals=0),
-    )(near, far, inside(low), inside(hidden))
+    )(far, near, inside(low), inside(hidden))
     return (atom_out, pair_grad.reshape(pair.shape))
 
 

time: 60.1 us -> 58.7 us (0.977)
  starting transfers between devices: 30.1 us -> 29.1 us
  waiting for transfers between devices: 5.77 us -> 4.97 us
    ppermute x2, starting transfers between devices: 14.6 us -> 12.9 us  [shards(): far = lax.ppermute(far, ('row', 'col'), chip_pairs)]
    ppermute x6, waiting for transfers between devices: 4.42 us -> 3.35 us  [the longest x3 2.71 us: shards(): lax.ppermute(part, 'col', chip_shift(s))]
where the time goes in v5:
time: 58.7 us; the launch traced here: 58 us
  starting transfers between devices  29.1 us (50%)
  Pallas kernels  23.1 us (39%)
  waiting for transfers between devices  4.97 us (8%)
  between operations  0.81 us (1%)
    ppermute x2, starting transfers between devices, shards(): far = lax.ppermute(far, ('row', 'col'), chip_pairs)  12.9 us
    pallas_call x2, Pallas kernels, pair_bias(): pl.pallas_call(functools.partial(pair_bias_kernel, first), in_specs=[HBM,...  7.95 us
    ppermute x3, starting transfers between devices, shards(): shifted = [lax.ppermute(own, 'col', chip_shift(s)) for s in GATHER_SHIFTS]  5.68 us
    pallas_call x1, Pallas kernels, shards(): pl.pallas_call(token_kernel, in_specs=[VMEM] * 5 + [HBM] * 2 + [VMEM] + [...  5.52 us
    all_to_all x1, starting transfers between devices, shards(): keys = lax.all_to_all(to_row, 'row', 0, 0).reshape(256, 768)  5.06 us
    ppermute x3, starting transfers between devices, shards(): lax.ppermute(part, 'col', chip_shift(s))  4.94 us
    pallas_call x1, Pallas kernels, shards(): pl.pallas_call(pair_grad_kernel, in_specs=[VMEM] * 5, out_specs=HBM, out_...  3.85 us
    pallas_call x1, Pallas kernels, shards(): pl.pallas_call(atom_kernel, in_specs=[VMEM] * 9 + [HBM], out_specs=[VMEM]...  2.81 us
  transfers between devices with their start and end apart: 13, of which 6 were waited for; matrix products, arithmetic and copies ran while one was open for 0% of the time, Pallas kernels for 20%

profile of v5, /device:TPU:8, one launch (start us, length us, event | category | flops | bytes accessed | tf_op | source)
XLA Modules:
  0.0 58.0 jit_solution(9414634575536003313)
XLA Ops:
  0.6 0.0 copy-start
  0.6 1.0 %pack.1 = (bf16[464,128]{1,0:T(8,128)(2,1)S(1)}, bf16[464,128]{1,0:T(8,128)(2,1)S(1)}, f32[48,128]{1,0:T(8,128)S(1)}) custom-call(s32[4]{0:T(128)} %shift_ref.1, s32[16]{0:T(128)} %count_ref.1, s32[16]{0:T(128)} %mask_ref.1, bf16[128,128]{1,0:T(8,128)(2,1)} %refs_0_.1, bf16[4,128,128]{2,1,0:T(8,128)(2,1)} %refs_1_.1, bf16[128,128]{1,0:T(8,128)(2,1)} %refs_2_.1, ...), custom_call_target="tpu_custom_call" | custom-call | bytes 1048576 | tf_op jit(solution)/shard_map/pack/pallas_call | solution.py:630
  1.6 0.1 collective-permute-start
  1.7 8.1 %collective-permute-start.1 = (bf16[464,128]{1,0:T(8,128)(2,1)S(1)}, bf16[464,128]{1,0:T(8,128)(2,1)S(1)}, u32[]{:S(2)}, u32[]{:S(2)}) collective-permute-start(bf16[464,128]{1,0:T(8,128)(2,1)S(1)} %get-tuple-element.37), channel_id=1, source_target_pairs={{1,2},{3,4},{5,6},{7,8},{9,10},{11,12},{13,14},{15,16},{17,18},{19... | collective-permute-start | bytes 356360 | tf_op jit(solution)/shard_map/ppermute | solution.py:648
  9.8 0.0 copy-done
  9.9 4.0 %pair_bias_early.1 = (f32[8,16,8,256]{3,2,1,0:T(8,128)}, bf16[128,128]{1,0:T(8,128)(2,1)S(1)}, bf16[4,128,128]{2,1,0:T(8,128)(2,1)S(1)}, bf16[128,128]{1,0:T(8,1...) custom-call(bf16[128,256,128]{2,1,0:T(8,128)(2,1)} %bitcast.11, ...), custom_call_target="tpu_custom_call" | custom-call | flops 536870912 | bytes 4194304 | tf_op jit(solution)/shard_map/pair_bias_early/pallas_call | solution.py:653
  13.9 0.0 collective-permute-done.near_ref
  13.9 0.0 collective-permute-done.1.far_ref
  13.9 2.8 %atom_stage.1 = (bf16[144,128]{1,0:T(8,128)(2,1)S(1)}, f32[16,768]{1,0:T(8,128)}, bf16[16,16,768]{2,1,0:T(8,128)(2,1)}, bf16[16,896]{1,0:T(8,128)(2,1)S(1)}, bf16[768,1536]{1,0:T(8,128)(2,1)S(1)}) custom-call(f32[48,128]{1,0:T(8,128)S(1)} %get-tuple-element.35.side_ref, bf16[464,128]{1,0:T(8,128)(2,1)S(1)} %collective-permute-done.near_ref, ...), custom_call_target="tpu_custom_call" | custom-call | flops 268435456 | bytes 2097152 | tf_op jit(solution)/shard_map/atom_stage/pallas_call | solution.py:687
  16.7 0.1 collective-permute-start.2
  16.8 5.1 %all-to-all-start = ((bf16[16,16,768]{2,1,0:T(8,128)(2,1)}), bf16[16,16,768]{2,1,0:T(8,128)(2,1)S(1)}, u32[]{:S(2)}, u32[]{:S(2)}) async-start(bf16[16,16,768]{2,1,0:T(8,128)(2,1)} %get-tuple-element.44), calls=%async_computation | async-start | bytes 786432 | tf_op jit(solution)/shard_map/all_to_all | solution.py:714
  21.9 0.0 collective-permute-done.2.partner_ref
  21.9 1.5 %collective-permute-start.5 = (bf16[2,16,896]{2,1,0:T(8,128)(2,1)S(1)}, bf16[2,16,896]{2,1,0:T(8,128)(2,1)S(1)}, u32[]{:S(2)}, u32[]{:S(2)}) collective-permute-start(bf16[2,16,896]{2,1,0:T(8,128)(2,1)S(1)} %stack.1.own_ref), channel_id=1, source_target_pairs={{0,4},{1,5},{2,6},{3,7},{4,0},{5,1},{6,2},{7,3},{8,12},{9,13},{10,... | collective-permute-start | bytes 172040 | tf_op jit(solution)/shard_map/ppermute | solution.py:724
  23.5 3.4 %collective-permute-start.4 = (bf16[2,16,896]{2,1,0:T(8,128)(2,1)S(1)}, bf16[2,16,896]{2,1,0:T(8,128)(2,1)S(1)}, u32[]{:S(2)}, u32[]{:S(2)}) collective-permute-start(bf16[2,16,896]{2,1,0:T(8,128)(2,1)S(1)} %stack.1.own_ref), channel_id=1, source_target_pairs={{0,6},{1,7},{2,0},{3,1},{4,2},{5,3},{6,4},{7,5},{8,14},{9,15},{10,... | collective-permute-start | bytes 172040 | tf_op jit(solution)/shard_map/ppermute | solution.py:724
  26.8 0.8 %collective-permute-start.3 = (bf16[2,16,896]{2,1,0:T(8,128)(2,1)S(1)}, bf16[2,16,896]{2,1,0:T(8,128)(2,1)S(1)}, u32[]{:S(2)}, u32[]{:S(2)}) collective-permute-start(bf16[2,16,896]{2,1,0:T(8,128)(2,1)S(1)} %stack.1.own_ref), channel_id=1, source_target_pairs={{0,2},{1,3},{2,4},{3,5},{4,6},{5,7},{6,0},{7,1},{8,10},{9,11},{10,... | collective-permute-start | bytes 172040 | tf_op jit(solution)/shard_map/ppermute | solution.py:724
  27.6 3.9 %pair_bias_late.1.late_ref = f32[8,16,8,256]{3,2,1,0:T(8,128)} custom-call(bf16[128,256,128]{2,1,0:T(8,128)(2,1)} %bitcast.12, bf16[128,128]{1,0:T(8,128)(2,1)S(1)} %broadcast_bitcast_fusion.head_ref), custom_call_target="tpu_custom_call" | custom-call | flops 536870912 | bytes 4194304 | tf_op jit(solution)/shard_map/pair_bias_late/pallas_call | solution.py:653
  31.5 0.0 collective-permute-done.5.third_ref
  31.5 0.0 collective-permute-done.4.second_ref
  31.6 0.6 %collective-permute-done.3.first_ref = bf16[2,16,896]{2,1,0:T(8,128)(2,1)S(1)} collective-permute-done((bf16[2,16,896]{2,1,0:T(8,128)(2,1)S(1)}, bf16[2,16,896]{2,1,0:T(8,128)(2,1)S(1)}, u32[]{:S(2)}, u32[]{:S(2)}) %collective-permute-start.3) | collective-permute-done | bytes 57376 | tf_op jit(solution)/shard_map/ppermute | solution.py:724
  32.2 0.0 all-to-all-done
  32.2 5.5 %token_stage.1 = (f32[16,16,8,256]{3,2,1,0:T(8,128)S(1)}, f32[16,16,8,256]{3,2,1,0:T(8,128)S(1)}, f32[128,128]{1,0:T(8,128)S(1)}, f32[4,16,768]{2,1,0:T(8,128)S(...) custom-call(bf16[256,768]{1,0:T(8,128)(2,1)S(1)} %bitcast.10, ...), custom_call_target="tpu_custom_call" | custom-call | flops 2147483648 | bytes 12582912 | tf_op jit(solution)/shard_map/token_stage/pallas_call | solution.py:730
  37.7 0.1 collective-permute-start.6
  37.8 1.3 %collective-permute-done.6.given_ref = bf16[4,16,1024]{2,1,0:T(8,128)(2,1)S(1)} collective-permute-done((bf16[4,16,1024]{2,1,0:T(8,128)(2,1)S(1)}, bf16[4,16,1024]{2,1,0:T(8,128)(2,1)S(1)}, u32[]{:S(2)}, u32[]{:S(2)}) %collective-permute-start.6) | collective-permute-done | bytes 131104 | tf_op jit(solution)/shard_map/ppermute | solution.py:766
  39.2 0.4 fold.1
  39.5 1.7 %collective-permute-start.7 = (bf16[16,1792]{1,0:T(8,128)(2,1)S(1)}, bf16[16,1792]{1,0:T(8,128)(2,1)S(1)}, u32[]{:S(2)}, u32[]{:S(2)}) collective-permute-start(bf16[16,1792]{1,0:T(8,128)(2,1)S(1)} %get-tuple-element.54), channel_id=1, source_target_pairs={{0,4},{1,5},{2,6},{3,7},{4,0},{5,1},{6,2},{7,3},{8,12},{9,13},{10,... | collective-permute-start | bytes 172040 | tf_op jit(solution)/shard_map/ppermute | solution.py:778
  41.2 1.8 %collective-permute-start.8 = (bf16[16,1792]{1,0:T(8,128)(2,1)S(1)}, bf16[16,1792]{1,0:T(8,128)(2,1)S(1)}, u32[]{:S(2)}, u32[]{:S(2)}) collective-permute-start(bf16[16,1792]{1,0:T(8,128)(2,1)S(1)} %get-tuple-element.55), channel_id=1, source_target_pairs={{0,2},{1,3},{2,4},{3,5},{4,6},{5,7},{6,0},{7,1},{8,10},{9,11},{10,... | collective-permute-start | bytes 172040 | tf_op jit(solution)/shard_map/ppermute | solution.py:778
  43.0 1.5 %collective-permute-start.9 = (bf16[16,1792]{1,0:T(8,128)(2,1)S(1)}, bf16[16,1792]{1,0:T(8,128)(2,1)S(1)}, u32[]{:S(2)}, u32[]{:S(2)}) collective-permute-start(bf16[16,1792]{1,0:T(8,128)(2,1)S(1)} %get-tuple-element.56), channel_id=1, source_target_pairs={{0,6},{1,7},{2,0},{3,1},{4,2},{5,3},{6,4},{7,5},{8,14},{9,15},{10,... | collective-permute-start | bytes 172040 | tf_op jit(solution)/shard_map/ppermute | solution.py:778
  44.5 0.9 %collective-permute-done.7.first_ref = bf16[16,1792]{1,0:T(8,128)(2,1)S(1)} collective-permute-done((bf16[16,1792]{1,0:T(8,128)(2,1)S(1)}, bf16[16,1792]{1,0:T(8,128)(2,1)S(1)}, u32[]{:S(2)}, u32[]{:S(2)}) %collective-permute-start.7) | collective-permute-done | bytes 57376 | tf_op jit(solution)/shard_map/ppermute | solution.py:778
  45.3 1.3 %collective-permute-done.8.second_ref = bf16[16,1792]{1,0:T(8,128)(2,1)S(1)} collective-permute-done((bf16[16,1792]{1,0:T(8,128)(2,1)S(1)}, bf16[16,1792]{1,0:T(8,128)(2,1)S(1)}, u32[]{:S(2)}, u32[]{:S(2)}) %collective-permute-start.8) | collective-permute-done | bytes 57376 | tf_op jit(solution)/shard_map/ppermute | solution.py:778
  46.6 0.6 collective-permute-done.9.third_ref
  47.2 0.8 %merge.1 = (f32[128,128]{1,0:T(8,128)S(1)}, f32[128,128]{1,0:T(8,128)S(1)}, bf16[2,16,128]{2,1,0:T(8,128)(2,1)S(1)}, bf16[16,128]{1,0:T(8,128)(2,1)S(1)}, bf16[16,128]{1,0:T(8,128)(2,1)S(1)}) custom-call(f32[128,128]{1,0:T(8,128)S(1)} %get-tuple-element.49.stats_ref, f32[16,768]{1,0:T(8,128)S(1)} %get-tuple-element.52.own_ref, ...), custom_call_target="tpu_custom_call" | custom-call | flops 67108864 | bytes 2097152 | tf_op jit(solution)/shard_map/merge/pallas_call | solution.py:781
  48.0 4.8 %collective-permute-start.10 = (bf16[16,128]{1,0:T(8,128)(2,1)S(1)}, bf16[16,128]{1,0:T(8,128)(2,1)S(1)}, u32[]{:S(2)}, u32[]{:S(2)}) collective-permute-start(bf16[16,128]{1,0:T(8,128)(2,1)S(1)} %get-tuple-element.60), channel_id=1, source_target_pairs={{1,2},{3,4},{5,6},{7,8},{9,10},{11,12},{13,14},{15,16},{17,18},{19... | collective-permute-start | bytes 12296 | tf_op jit(solution)/shard_map/ppermute | solution.py:806
  52.8 0.3 collective-permute-start.11
  53.1 3.8 %pair_grad.1 = bf16[128,256,128]{2,1,0:T(8,128)(2,1)} custom-call(f32[16,16,8,256]{3,2,1,0:T(8,128)S(1)} %get-tuple-element.64.prob_ref, f32[16,16,8,256]{3,2,1,0:T(8,128)S(1)} %get-tuple-element.65.grad_ref, f32[128,128]{1,0:T(8,128)S(1)} %get-tuple-element.66.scale_ref, f32[128,128]{1,0:T(8,128)S(1)} %get-tuple-element.67.diag_ref, ...), custom_call_target="tpu_custom_call" | custom-call | flops 1073741824 | bytes 14680064 | tf_op jit(solution)/shard_map/pair_grad/pallas_call | solution.py:808
  56.9 0.3 collective-permute-done.10.far_ref
  57.2 0.0 collective-permute-done.11.near_ref
  57.2 0.8 %atom_out.1 = bf16[128,128]{1,0:T(8,128)(2,1)} custom-call(bf16[16,128]{1,0:T(8,128)(2,1)S(1)} %collective-permute-done.10.far_ref, bf16[16,128]{1,0:T(8,128)(2,1)S(1)} %collective-permute-done.11.near_ref, bf16[2,16,128]{2,1,0:T(8,128)(2,1)S(1)} %get-tuple-element.62.low_ref, bf16[144,128]{1,0:T(8,128)(2,1)S(1)} %get-tuple-element.63.hidden_ref), custom_call_target="tpu_custom_call" | custom-call | flops 2097152 | bytes 131072 | tf_op jit(solution)/shard_map/atom_out/pallas_call | solution.py:820
  (2 shorter events, 0.0 us)
Async XLA Ops:
  0.6 9.2 %copy-start = (bf16[128,16]{0,1:T(8,128)(2,1)S(1)}, bf16[128,16]{0,1:T(8,128)(2,1)}, u32[]{:S(2)}) copy-start(bf16[128,16]{0,1:T(8,128)(2,1)} %param.27) | copy-start | bytes 12292
  1.6 12.3 %collective-permute-start = (bf16[464,128]{1,0:T(8,128)(2,1)S(1)}, bf16[464,128]{1,0:T(8,128)(2,1)S(1)}, u32[]{:S(2)}, u32[]{:S(2)}) collective-permute-start(bf16[464,128]{1,0:T(8,128)(2,1)S(1)} %get-tuple-element.36), channel_id=1, source_target_pairs={{0,1},{1,0},{2,3},{3,2},{4,5},{5,4},{6,7},{7,6},{8,9},{9,8},{10,11... | collective-permute-start | bytes 356360 | tf_op jit(solution)/shard_map/ppermute | solution.py:647
  1.7 12.2 %collective-permute-start.1 = (bf16[464,128]{1,0:T(8,128)(2,1)S(1)}, bf16[464,128]{1,0:T(8,128)(2,1)S(1)}, u32[]{:S(2)}, u32[]{:S(2)}) collective-permute-start(bf16[464,128]{1,0:T(8,128)(2,1)S(1)} %get-tuple-element.37), channel_id=1, source_target_pairs={{1,2},{3,4},{5,6},{7,8},{9,10},{11,12},{13,14},{15,16},{17,18},{19... | collective-permute-start | bytes 356360 | tf_op jit(solution)/shard_map/ppermute | solution.py:648
  16.7 5.2 %collective-permute-start.2 = (bf16[16,896]{1,0:T(8,128)(2,1)S(1)}, bf16[16,896]{1,0:T(8,128)(2,1)S(1)}, u32[]{:S(2)}, u32[]{:S(2)}) collective-permute-start(bf16[16,896]{1,0:T(8,128)(2,1)S(1)} %get-tuple-element.45.own_ref), channel_id=1, source_target_pairs={{0,1},{1,0},{2,3},{3,2},{4,5},{5,4},{6,7},{7,6},{8,9},{9,8},{10,11... | collective-permute-start | bytes 86024 | tf_op jit(solution)/shard_map/ppermute | solution.py:713
  16.8 15.4 %all-to-all-start = ((bf16[16,16,768]{2,1,0:T(8,128)(2,1)}), bf16[16,16,768]{2,1,0:T(8,128)(2,1)S(1)}, u32[]{:S(2)}, u32[]{:S(2)}) async-start(bf16[16,16,768]{2,1,0:T(8,128)(2,1)} %get-tuple-element.44), calls=%async_computation | async-start | bytes 786432 | tf_op jit(solution)/shard_map/all_to_all | solution.py:714
  21.9 9.6 %collective-permute-start.5 = (bf16[2,16,896]{2,1,0:T(8,128)(2,1)S(1)}, bf16[2,16,896]{2,1,0:T(8,128)(2,1)S(1)}, u32[]{:S(2)}, u32[]{:S(2)}) collective-permute-start(bf16[2,16,896]{2,1,0:T(8,128)(2,1)S(1)} %stack.1.own_ref), channel_id=1, source_target_pairs={{0,4},{1,5},{2,6},{3,7},{4,0},{5,1},{6,2},{7,3},{8,12},{9,13},{10,... | collective-permute-start | bytes 172040 | tf_op jit(solution)/shard_map/ppermute | solution.py:724
  23.5 8.1 %collective-permute-start.4 = (bf16[2,16,896]{2,1,0:T(8,128)(2,1)S(1)}, bf16[2,16,896]{2,1,0:T(8,128)(2,1)S(1)}, u32[]{:S(2)}, u32[]{:S(2)}) collective-permute-start(bf16[2,16,896]{2,1,0:T(8,128)(2,1)S(1)} %stack.1.own_ref), channel_id=1, source_target_pairs={{0,6},{1,7},{2,0},{3,1},{4,2},{5,3},{6,4},{7,5},{8,14},{9,15},{10,... | collective-permute-start | bytes 172040 | tf_op jit(solution)/shard_map/ppermute | solution.py:724
  26.8 5.4 %collective-permute-start.3 = (bf16[2,16,896]{2,1,0:T(8,128)(2,1)S(1)}, bf16[2,16,896]{2,1,0:T(8,128)(2,1)S(1)}, u32[]{:S(2)}, u32[]{:S(2)}) collective-permute-start(bf16[2,16,896]{2,1,0:T(8,128)(2,1)S(1)} %stack.1.own_ref), channel_id=1, source_target_pairs={{0,2},{1,3},{2,4},{3,5},{4,6},{5,7},{6,0},{7,1},{8,10},{9,11},{10,... | collective-permute-start | bytes 172040 | tf_op jit(solution)/shard_map/ppermute | solution.py:724
  37.7 1.4 %collective-permute-start.6 = (bf16[4,16,1024]{2,1,0:T(8,128)(2,1)S(1)}, bf16[4,16,1024]{2,1,0:T(8,128)(2,1)S(1)}, u32[]{:S(2)}, u32[]{:S(2)}) collective-permute-start(bf16[4,16,1024]{2,1,0:T(8,128)(2,1)S(1)} %get-tuple-element.51), channel_id=1, source_target_pairs={{0,1},{1,0},{2,3},{3,2},{4,5},{5,4},{6,7},{7,6},{8,9},{9,8},{10,11... | collective-permute-start | bytes 393224 | tf_op jit(solution)/shard_map/ppermute | solution.py:766
  39.5 5.8 %collective-permute-start.7 = (bf16[16,1792]{1,0:T(8,128)(2,1)S(1)}, bf16[16,1792]{1,0:T(8,128)(2,1)S(1)}, u32[]{:S(2)}, u32[]{:S(2)}) collective-permute-start(bf16[16,1792]{1,0:T(8,128)(2,1)S(1)} %get-tuple-element.54), channel_id=1, source_target_pairs={{0,4},{1,5},{2,6},{3,7},{4,0},{5,1},{6,2},{7,3},{8,12},{9,13},{10,... | collective-permute-start | bytes 172040 | tf_op jit(solution)/shard_map/ppermute | solution.py:778
  41.2 5.4 %collective-permute-start.8 = (bf16[16,1792]{1,0:T(8,128)(2,1)S(1)}, bf16[16,1792]{1,0:T(8,128)(2,1)S(1)}, u32[]{:S(2)}, u32[]{:S(2)}) collective-permute-start(bf16[16,1792]{1,0:T(8,128)(2,1)S(1)} %get-tuple-element.55), channel_id=1, source_target_pairs={{0,2},{1,3},{2,4},{3,5},{4,6},{5,7},{6,0},{7,1},{8,10},{9,11},{10,... | collective-permute-start | bytes 172040 | tf_op jit(solution)/shard_map/ppermute | solution.py:778
  43.0 4.2 %collective-permute-start.9 = (bf16[16,1792]{1,0:T(8,128)(2,1)S(1)}, bf16[16,1792]{1,0:T(8,128)(2,1)S(1)}, u32[]{:S(2)}, u32[]{:S(2)}) collective-permute-start(bf16[16,1792]{1,0:T(8,128)(2,1)S(1)} %get-tuple-element.56), channel_id=1, source_target_pairs={{0,6},{1,7},{2,0},{3,1},{4,2},{5,3},{6,4},{7,5},{8,14},{9,15},{10,... | collective-permute-start | bytes 172040 | tf_op jit(solution)/shard_map/ppermute | solution.py:778
  48.0 9.2 %collective-permute-start.10 = (bf16[16,128]{1,0:T(8,128)(2,1)S(1)}, bf16[16,128]{1,0:T(8,128)(2,1)S(1)}, u32[]{:S(2)}, u32[]{:S(2)}) collective-permute-start(bf16[16,128]{1,0:T(8,128)(2,1)S(1)} %get-tuple-element.60), channel_id=1, source_target_pairs={{1,2},{3,4},{5,6},{7,8},{9,10},{11,12},{13,14},{15,16},{17,18},{19... | collective-permute-start | bytes 12296 | tf_op jit(solution)/shard_map/ppermute | solution.py:806
  52.8 4.4 %collective-permute-start.11 = (bf16[16,128]{1,0:T(8,128)(2,1)S(1)}, bf16[16,128]{1,0:T(8,128)(2,1)S(1)}, u32[]{:S(2)}, u32[]{:S(2)}) collective-permute-start(bf16[16,128]{1,0:T(8,128)(2,1)S(1)} %get-tuple-element.61), channel_id=1, source_target_pairs={{0,1},{1,0},{2,3},{3,2},{4,5},{5,4},{6,7},{7,6},{8,9},{9,8},{10,11... | collective-permute-start | bytes 12296 | tf_op jit(solution)/shard_map/ppermute | solution.py:805

commit v6 on v5

--- a/solution.py
+++ b/solution.py
@@ -168,8 +168,8 @@
 
 def atom_kernel(
     side_ref,
+    far_ref,
     near_ref,
-    far_ref,
     atoms_ref,
     bias_ref,
     cot_ref,
@@ -705,8 +705,8 @@
         cost_estimate=pl.CostEstimate(flops=1 << 28, bytes_accessed=2 << 20, transcendentals=1 << 17),
     )(
         inside(side),
+        far,
         near,
-        far,
         *[inside(value) for value in atom_inputs],
         outside(w_token_qkv),
     )

time: 58.7 us -> 58 us (0.988)
  starting transfers between devices: 29.1 us -> 28.3 us
    ppermute x2, starting transfers between devices: 12.9 us -> 12.2 us  [shards(): far = lax.ppermute(far, ('row', 'col'), chip_pairs)]
  transfers between devices with their start and end apart: 13 -> 13, of which waited for: 6 -> 6; matrix products, arithmetic and copies ran while one was open for 0% -> 0% of each run, Pallas kernels for 20% -> 21%
where the time goes in v6:
time: 58 us; the launch traced here: 57.2 us
  starting transfers between devices  28.3 us (49%)
  Pallas kernels  23.1 us (40%)
  waiting for transfers between devices  4.94 us (9%)
  between operations  0.8 us (1%)
    ppermute x2, starting transfers between devices, shards(): far = lax.ppermute(far, ('row', 'col'), chip_pairs)  12.2 us
    pallas_call x2, Pallas kernels, pair_bias(): pl.pallas_call(functools.partial(pair_bias_kernel, first), in_specs=[HBM,...  7.95 us
    pallas_call x1, Pallas kernels, shards(): pl.pallas_call(token_kernel, in_specs=[VMEM] * 5 + [HBM] * 2 + [VMEM] + [...  5.52 us
    ppermute x3, starting transfers between devices, shards(): shifted = [lax.ppermute(own, 'col', chip_shift(s)) for s in GATHER_SHIFTS]  5.13 us
    all_to_all x1, starting transfers between devices, shards(): keys = lax.all_to_all(to_row, 'row', 0, 0).reshape(256, 768)  5.05 us
    ppermute x3, starting transfers between devices, shards(): lax.ppermute(part, 'col', chip_shift(s))  4.95 us
    pallas_call x1, Pallas kernels, shards(): pl.pallas_call(pair_grad_kernel, in_specs=[VMEM] * 5, out_specs=HBM, out_...  3.85 us
    pallas_call x1, Pallas kernels, shards(): pl.pallas_call(atom_kernel, in_specs=[VMEM] * 9 + [HBM], out_specs=[VMEM]...  2.82 us
  transfers between devices with their start and end apart: 13, of which 6 were waited for; matrix products, arithmetic and copies ran while one was open for 0% of the time, Pallas kernels for 21%

profile of v6, /device:TPU:8, one launch (start us, length us, event | category | flops | bytes accessed | tf_op | source)
XLA Modules:
  0.0 57.2 jit_solution(18194340382408175676)
XLA Ops:
  0.6 0.0 copy-start
  0.6 1.0 %pack.1 = (bf16[464,128]{1,0:T(8,128)(2,1)S(1)}, bf16[464,128]{1,0:T(8,128)(2,1)S(1)}, f32[48,128]{1,0:T(8,128)S(1)}) custom-call(s32[4]{0:T(128)} %shift_ref.1, s32[16]{0:T(128)} %count_ref.1, s32[16]{0:T(128)} %mask_ref.1, bf16[128,128]{1,0:T(8,128)(2,1)} %refs_0_.1, bf16[4,128,128]{2,1,0:T(8,128)(2,1)} %refs_1_.1, bf16[128,128]{1,0:T(8,128)(2,1)} %refs_2_.1, ...), custom_call_target="tpu_custom_call" | custom-call | bytes 1048576 | tf_op jit(solution)/shard_map/pack/pallas_call | solution.py:630
  1.6 7.5 %collective-permute-start = (bf16[464,128]{1,0:T(8,128)(2,1)S(1)}, bf16[464,128]{1,0:T(8,128)(2,1)S(1)}, u32[]{:S(2)}, u32[]{:S(2)}) collective-permute-start(bf16[464,128]{1,0:T(8,128)(2,1)S(1)} %get-tuple-element.36), channel_id=1, source_target_pairs={{1,2},{3,4},{5,6},{7,8},{9,10},{11,12},{13,14},{15,16},{17,18},{19... | collective-permute-start | bytes 356360 | tf_op jit(solution)/shard_map/ppermute | solution.py:648
  9.1 0.1 collective-permute-start.1
  9.2 0.0 copy-done
  9.2 4.0 %pair_bias_early.1 = (f32[8,16,8,256]{3,2,1,0:T(8,128)}, bf16[128,128]{1,0:T(8,128)(2,1)S(1)}, bf16[4,128,128]{2,1,0:T(8,128)(2,1)S(1)}, bf16[128,128]{1,0:T(8,1...) custom-call(bf16[128,256,128]{2,1,0:T(8,128)(2,1)} %bitcast.11, ...), custom_call_target="tpu_custom_call" | custom-call | flops 536870912 | bytes 4194304 | tf_op jit(solution)/shard_map/pair_bias_early/pallas_call | solution.py:653
  13.2 0.0 collective-permute-done.far_ref
  13.2 0.0 collective-permute-done.1.near_ref
  13.3 2.8 %atom_stage.1 = (bf16[144,128]{1,0:T(8,128)(2,1)S(1)}, f32[16,768]{1,0:T(8,128)}, bf16[16,16,768]{2,1,0:T(8,128)(2,1)}, bf16[16,896]{1,0:T(8,128)(2,1)S(1)}, bf16[768,1536]{1,0:T(8,128)(2,1)S(1)}) custom-call(f32[48,128]{1,0:T(8,128)S(1)} %get-tuple-element.35.side_ref, bf16[464,128]{1,0:T(8,128)(2,1)S(1)} %collective-permute-done.far_ref, ...), custom_call_target="tpu_custom_call" | custom-call | flops 268435456 | bytes 2097152 | tf_op jit(solution)/shard_map/atom_stage/pallas_call | solution.py:687
  16.1 0.6 collective-permute-start.2
  16.6 5.0 %all-to-all-start = ((bf16[16,16,768]{2,1,0:T(8,128)(2,1)}), bf16[16,16,768]{2,1,0:T(8,128)(2,1)S(1)}, u32[]{:S(2)}, u32[]{:S(2)}) async-start(bf16[16,16,768]{2,1,0:T(8,128)(2,1)} %get-tuple-element.44), calls=%async_computation | async-start | bytes 786432 | tf_op jit(solution)/shard_map/all_to_all | solution.py:714
  21.7 0.0 collective-permute-done.2.partner_ref
  21.7 1.7 %collective-permute-start.5 = (bf16[2,16,896]{2,1,0:T(8,128)(2,1)S(1)}, bf16[2,16,896]{2,1,0:T(8,128)(2,1)S(1)}, u32[]{:S(2)}, u32[]{:S(2)}) collective-permute-start(bf16[2,16,896]{2,1,0:T(8,128)(2,1)S(1)} %stack.1.own_ref), channel_id=1, source_target_pairs={{0,4},{1,5},{2,6},{3,7},{4,0},{5,1},{6,2},{7,3},{8,12},{9,13},{10,... | collective-permute-start | bytes 172040 | tf_op jit(solution)/shard_map/ppermute | solution.py:724
  23.5 2.6 %collective-permute-start.4 = (bf16[2,16,896]{2,1,0:T(8,128)(2,1)S(1)}, bf16[2,16,896]{2,1,0:T(8,128)(2,1)S(1)}, u32[]{:S(2)}, u32[]{:S(2)}) collective-permute-start(bf16[2,16,896]{2,1,0:T(8,128)(2,1)S(1)} %stack.1.own_ref), channel_id=1, source_target_pairs={{0,6},{1,7},{2,0},{3,1},{4,2},{5,3},{6,4},{7,5},{8,14},{9,15},{10,... | collective-permute-start | bytes 172040 | tf_op jit(solution)/shard_map/ppermute | solution.py:724
  26.1 0.8 %collective-permute-start.3 = (bf16[2,16,896]{2,1,0:T(8,128)(2,1)S(1)}, bf16[2,16,896]{2,1,0:T(8,128)(2,1)S(1)}, u32[]{:S(2)}, u32[]{:S(2)}) collective-permute-start(bf16[2,16,896]{2,1,0:T(8,128)(2,1)S(1)} %stack.1.own_ref), channel_id=1, source_target_pairs={{0,2},{1,3},{2,4},{3,5},{4,6},{5,7},{6,0},{7,1},{8,10},{9,11},{10,... | collective-permute-start | bytes 172040 | tf_op jit(solution)/shard_map/ppermute | solution.py:724
  26.8 3.9 %pair_bias_late.1.late_ref = f32[8,16,8,256]{3,2,1,0:T(8,128)} custom-call(bf16[128,256,128]{2,1,0:T(8,128)(2,1)} %bitcast.12, bf16[128,128]{1,0:T(8,128)(2,1)S(1)} %broadcast_bitcast_fusion.head_ref), custom_call_target="tpu_custom_call" | custom-call | flops 536870912 | bytes 4194304 | tf_op jit(solution)/shard_map/pair_bias_late/pallas_call | solution.py:653
  30.8 0.0 collective-permute-done.5.third_ref
  30.8 0.0 collective-permute-done.4.second_ref
  30.8 0.6 %collective-permute-done.3.first_ref = bf16[2,16,896]{2,1,0:T(8,128)(2,1)S(1)} collective-permute-done((bf16[2,16,896]{2,1,0:T(8,128)(2,1)S(1)}, bf16[2,16,896]{2,1,0:T(8,128)(2,1)S(1)}, u32[]{:S(2)}, u32[]{:S(2)}) %collective-permute-start.3) | collective-permute-done | bytes 57376 | tf_op jit(solution)/shard_map/ppermute | solution.py:724
  31.5 0.0 all-to-all-done
  31.5 5.5 %token_stage.1 = (f32[16,16,8,256]{3,2,1,0:T(8,128)S(1)}, f32[16,16,8,256]{3,2,1,0:T(8,128)S(1)}, f32[128,128]{1,0:T(8,128)S(1)}, f32[4,16,768]{2,1,0:T(8,128)S(...) custom-call(bf16[256,768]{1,0:T(8,128)(2,1)S(1)} %bitcast.10, ...), custom_call_target="tpu_custom_call" | custom-call | flops 2147483648 | bytes 12582912 | tf_op jit(solution)/shard_map/token_stage/pallas_call | solution.py:730
  37.0 0.1 collective-permute-start.6
  37.1 1.3 %collective-permute-done.6.given_ref = bf16[4,16,1024]{2,1,0:T(8,128)(2,1)S(1)} collective-permute-done((bf16[4,16,1024]{2,1,0:T(8,128)(2,1)S(1)}, bf16[4,16,1024]{2,1,0:T(8,128)(2,1)S(1)}, u32[]{:S(2)}, u32[]{:S(2)}) %collective-permute-start.6) | collective-permute-done | bytes 131104 | tf_op jit(solution)/shard_map/ppermute | solution.py:766
  38.4 0.4 fold.1
  38.8 1.7 %collective-permute-start.7 = (bf16[16,1792]{1,0:T(8,128)(2,1)S(1)}, bf16[16,1792]{1,0:T(8,128)(2,1)S(1)}, u32[]{:S(2)}, u32[]{:S(2)}) collective-permute-start(bf16[16,1792]{1,0:T(8,128)(2,1)S(1)} %get-tuple-element.54), channel_id=1, source_target_pairs={{0,4},{1,5},{2,6},{3,7},{4,0},{5,1},{6,2},{7,3},{8,12},{9,13},{10,... | collective-permute-start | bytes 172040 | tf_op jit(solution)/shard_map/ppermute | solution.py:778
  40.5 1.8 %collective-permute-start.8 = (bf16[16,1792]{1,0:T(8,128)(2,1)S(1)}, bf16[16,1792]{1,0:T(8,128)(2,1)S(1)}, u32[]{:S(2)}, u32[]{:S(2)}) collective-permute-start(bf16[16,1792]{1,0:T(8,128)(2,1)S(1)} %get-tuple-element.55), channel_id=1, source_target_pairs={{0,2},{1,3},{2,4},{3,5},{4,6},{5,7},{6,0},{7,1},{8,10},{9,11},{10,... | collective-permute-start | bytes 172040 | tf_op jit(solution)/shard_map/ppermute | solution.py:778
  42.3 1.5 %collective-permute-start.9 = (bf16[16,1792]{1,0:T(8,128)(2,1)S(1)}, bf16[16,1792]{1,0:T(8,128)(2,1)S(1)}, u32[]{:S(2)}, u32[]{:S(2)}) collective-permute-start(bf16[16,1792]{1,0:T(8,128)(2,1)S(1)} %get-tuple-element.56), channel_id=1, source_target_pairs={{0,6},{1,7},{2,0},{3,1},{4,2},{5,3},{6,4},{7,5},{8,14},{9,15},{10,... | collective-permute-start | bytes 172040 | tf_op jit(solution)/shard_map/ppermute | solution.py:778
  43.7 0.9 %collective-permute-done.7.first_ref = bf16[16,1792]{1,0:T(8,128)(2,1)S(1)} collective-permute-done((bf16[16,1792]{1,0:T(8,128)(2,1)S(1)}, bf16[16,1792]{1,0:T(8,128)(2,1)S(1)}, u32[]{:S(2)}, u32[]{:S(2)}) %collective-permute-start.7) | collective-permute-done | bytes 57376 | tf_op jit(solution)/shard_map/ppermute | solution.py:778
  44.6 1.3 %collective-permute-done.8.second_ref = bf16[16,1792]{1,0:T(8,128)(2,1)S(1)} collective-permute-done((bf16[16,1792]{1,0:T(8,128)(2,1)S(1)}, bf16[16,1792]{1,0:T(8,128)(2,1)S(1)}, u32[]{:S(2)}, u32[]{:S(2)}) %collective-permute-start.8) | collective-permute-done | bytes 57376 | tf_op jit(solution)/shard_map/ppermute | solution.py:778
  45.9 0.5 collective-permute-done.9.third_ref
  46.4 0.8 %merge.1 = (f32[128,128]{1,0:T(8,128)S(1)}, f32[128,128]{1,0:T(8,128)S(1)}, bf16[2,16,128]{2,1,0:T(8,128)(2,1)S(1)}, bf16[16,128]{1,0:T(8,128)(2,1)S(1)}, bf16[16,128]{1,0:T(8,128)(2,1)S(1)}) custom-call(f32[128,128]{1,0:T(8,128)S(1)} %get-tuple-element.49.stats_ref, f32[16,768]{1,0:T(8,128)S(1)} %get-tuple-element.52.own_ref, ...), custom_call_target="tpu_custom_call" | custom-call | flops 67108864 | bytes 2097152 | tf_op jit(solution)/shard_map/merge/pallas_call | solution.py:781
  47.3 4.8 %collective-permute-start.10 = (bf16[16,128]{1,0:T(8,128)(2,1)S(1)}, bf16[16,128]{1,0:T(8,128)(2,1)S(1)}, u32[]{:S(2)}, u32[]{:S(2)}) collective-permute-start(bf16[16,128]{1,0:T(8,128)(2,1)S(1)} %get-tuple-element.60), channel_id=1, source_target_pairs={{1,2},{3,4},{5,6},{7,8},{9,10},{11,12},{13,14},{15,16},{17,18},{19... | collective-permute-start | bytes 12296 | tf_op jit(solution)/shard_map/ppermute | solution.py:806
  52.0 0.3 collective-permute-start.11
  52.3 3.8 %pair_grad.1 = bf16[128,256,128]{2,1,0:T(8,128)(2,1)} custom-call(f32[16,16,8,256]{3,2,1,0:T(8,128)S(1)} %get-tuple-element.64.prob_ref, f32[16,16,8,256]{3,2,1,0:T(8,128)S(1)} %get-tuple-element.65.grad_ref, f32[128,128]{1,0:T(8,128)S(1)} %get-tuple-element.66.scale_ref, f32[128,128]{1,0:T(8,128)S(1)} %get-tuple-element.67.diag_ref, ...), custom_call_target="tpu_custom_call" | custom-call | flops 1073741824 | bytes 14680064 | tf_op jit(solution)/shard_map/pair_grad/pallas_call | solution.py:808
  56.2 0.3 collective-permute-done.10.far_ref
  56.4 0.0 collective-permute-done.11.near_ref
  56.4 0.8 %atom_out.1 = bf16[128,128]{1,0:T(8,128)(2,1)} custom-call(bf16[16,128]{1,0:T(8,128)(2,1)S(1)} %collective-permute-done.10.far_ref, bf16[16,128]{1,0:T(8,128)(2,1)S(1)} %collective-permute-done.11.near_ref, bf16[2,16,128]{2,1,0:T(8,128)(2,1)S(1)} %get-tuple-element.62.low_ref, bf16[144,128]{1,0:T(8,128)(2,1)S(1)} %get-tuple-element.63.hidden_ref), custom_call_target="tpu_custom_call" | custom-call | flops 2097152 | bytes 131072 | tf_op jit(solution)/shard_map/atom_out/pallas_call | solution.py:820
  (2 shorter events, 0.0 us)
Async XLA Ops:
  0.6 8.6 %copy-start = (bf16[128,16]{0,1:T(8,128)(2,1)S(1)}, bf16[128,16]{0,1:T(8,128)(2,1)}, u32[]{:S(2)}) copy-start(bf16[128,16]{0,1:T(8,128)(2,1)} %param.27) | copy-start | bytes 12292
  1.6 11.6 %collective-permute-start = (bf16[464,128]{1,0:T(8,128)(2,1)S(1)}, bf16[464,128]{1,0:T(8,128)(2,1)S(1)}, u32[]{:S(2)}, u32[]{:S(2)}) collective-permute-start(bf16[464,128]{1,0:T(8,128)(2,1)S(1)} %get-tuple-element.36), channel_id=1, source_target_pairs={{1,2},{3,4},{5,6},{7,8},{9,10},{11,12},{13,14},{15,16},{17,18},{19... | collective-permute-start | bytes 356360 | tf_op jit(solution)/shard_map/ppermute | solution.py:648
  9.1 4.2 %collective-permute-start.1 = (bf16[464,128]{1,0:T(8,128)(2,1)S(1)}, bf16[464,128]{1,0:T(8,128)(2,1)S(1)}, u32[]{:S(2)}, u32[]{:S(2)}) collective-permute-start(bf16[464,128]{1,0:T(8,128)(2,1)S(1)} %get-tuple-element.37), channel_id=1, source_target_pairs={{0,1},{1,0},{2,3},{3,2},{4,5},{5,4},{6,7},{7,6},{8,9},{9,8},{10,11... | collective-permute-start | bytes 356360 | tf_op jit(solution)/shard_map/ppermute | solution.py:647
  16.1 5.6 %collective-permute-start.2 = (bf16[16,896]{1,0:T(8,128)(2,1)S(1)}, bf16[16,896]{1,0:T(8,128)(2,1)S(1)}, u32[]{:S(2)}, u32[]{:S(2)}) collective-permute-start(bf16[16,896]{1,0:T(8,128)(2,1)S(1)} %get-tuple-element.45.own_ref), channel_id=1, source_target_pairs={{0,1},{1,0},{2,3},{3,2},{4,5},{5,4},{6,7},{7,6},{8,9},{9,8},{10,11... | collective-permute-start | bytes 86024 | tf_op jit(solution)/shard_map/ppermute | solution.py:713
  16.6 14.8 %all-to-all-start = ((bf16[16,16,768]{2,1,0:T(8,128)(2,1)}), bf16[16,16,768]{2,1,0:T(8,128)(2,1)S(1)}, u32[]{:S(2)}, u32[]{:S(2)}) async-start(bf16[16,16,768]{2,1,0:T(8,128)(2,1)} %get-tuple-element.44), calls=%async_computation | async-start | bytes 786432 | tf_op jit(solution)/shard_map/all_to_all | solution.py:714
  21.7 9.1 %collective-permute-start.5 = (bf16[2,16,896]{2,1,0:T(8,128)(2,1)S(1)}, bf16[2,16,896]{2,1,0:T(8,128)(2,1)S(1)}, u32[]{:S(2)}, u32[]{:S(2)}) collective-permute-start(bf16[2,16,896]{2,1,0:T(8,128)(2,1)S(1)} %stack.1.own_ref), channel_id=1, source_target_pairs={{0,4},{1,5},{2,6},{3,7},{4,0},{5,1},{6,2},{7,3},{8,12},{9,13},{10,... | collective-permute-start | bytes 172040 | tf_op jit(solution)/shard_map/ppermute | solution.py:724
  23.5 7.4 %collective-permute-start.4 = (bf16[2,16,896]{2,1,0:T(8,128)(2,1)S(1)}, bf16[2,16,896]{2,1,0:T(8,128)(2,1)S(1)}, u32[]{:S(2)}, u32[]{:S(2)}) collective-permute-start(bf16[2,16,896]{2,1,0:T(8,128)(2,1)S(1)} %stack.1.own_ref), channel_id=1, source_target_pairs={{0,6},{1,7},{2,0},{3,1},{4,2},{5,3},{6,4},{7,5},{8,14},{9,15},{10,... | collective-permute-start | bytes 172040 | tf_op jit(solution)/shard_map/ppermute | solution.py:724
  26.1 5.4 %collective-permute-start.3 = (bf16[2,16,896]{2,1,0:T(8,128)(2,1)S(1)}, bf16[2,16,896]{2,1,0:T(8,128)(2,1)S(1)}, u32[]{:S(2)}, u32[]{:S(2)}) collective-permute-start(bf16[2,16,896]{2,1,0:T(8,128)(2,1)S(1)} %stack.1.own_ref), channel_id=1, source_target_pairs={{0,2},{1,3},{2,4},{3,5},{4,6},{5,7},{6,0},{7,1},{8,10},{9,11},{10,... | collective-permute-start | bytes 172040 | tf_op jit(solution)/shard_map/ppermute | solution.py:724
  37.0 1.4 %collective-permute-start.6 = (bf16[4,16,1024]{2,1,0:T(8,128)(2,1)S(1)}, bf16[4,16,1024]{2,1,0:T(8,128)(2,1)S(1)}, u32[]{:S(2)}, u32[]{:S(2)}) collective-permute-start(bf16[4,16,1024]{2,1,0:T(8,128)(2,1)S(1)} %get-tuple-element.51), channel_id=1, source_target_pairs={{0,1},{1,0},{2,3},{3,2},{4,5},{5,4},{6,7},{7,6},{8,9},{9,8},{10,11... | collective-permute-start | bytes 393224 | tf_op jit(solution)/shard_map/ppermute | solution.py:766
  38.8 5.8 %collective-permute-start.7 = (bf16[16,1792]{1,0:T(8,128)(2,1)S(1)}, bf16[16,1792]{1,0:T(8,128)(2,1)S(1)}, u32[]{:S(2)}, u32[]{:S(2)}) collective-permute-start(bf16[16,1792]{1,0:T(8,128)(2,1)S(1)} %get-tuple-element.54), channel_id=1, source_target_pairs={{0,4},{1,5},{2,6},{3,7},{4,0},{5,1},{6,2},{7,3},{8,12},{9,13},{10,... | collective-permute-start | bytes 172040 | tf_op jit(solution)/shard_map/ppermute | solution.py:778
  40.5 5.4 %collective-permute-start.8 = (bf16[16,1792]{1,0:T(8,128)(2,1)S(1)}, bf16[16,1792]{1,0:T(8,128)(2,1)S(1)}, u32[]{:S(2)}, u32[]{:S(2)}) collective-permute-start(bf16[16,1792]{1,0:T(8,128)(2,1)S(1)} %get-tuple-element.55), channel_id=1, source_target_pairs={{0,2},{1,3},{2,4},{3,5},{4,6},{5,7},{6,0},{7,1},{8,10},{9,11},{10,... | collective-permute-start | bytes 172040 | tf_op jit(solution)/shard_map/ppermute | solution.py:778
  42.3 4.2 %collective-permute-start.9 = (bf16[16,1792]{1,0:T(8,128)(2,1)S(1)}, bf16[16,1792]{1,0:T(8,128)(2,1)S(1)}, u32[]{:S(2)}, u32[]{:S(2)}) collective-permute-start(bf16[16,1792]{1,0:T(8,128)(2,1)S(1)} %get-tuple-element.56), channel_id=1, source_target_pairs={{0,6},{1,7},{2,0},{3,1},{4,2},{5,3},{6,4},{7,5},{8,14},{9,15},{10,... | collective-permute-start | bytes 172040 | tf_op jit(solution)/shard_map/ppermute | solution.py:778
  47.3 9.2 %collective-permute-start.10 = (bf16[16,128]{1,0:T(8,128)(2,1)S(1)}, bf16[16,128]{1,0:T(8,128)(2,1)S(1)}, u32[]{:S(2)}, u32[]{:S(2)}) collective-permute-start(bf16[16,128]{1,0:T(8,128)(2,1)S(1)} %get-tuple-element.60), channel_id=1, source_target_pairs={{1,2},{3,4},{5,6},{7,8},{9,10},{11,12},{13,14},{15,16},{17,18},{19... | collective-permute-start | bytes 12296 | tf_op jit(solution)/shard_map/ppermute | solution.py:806
  52.0 4.4 %collective-permute-start.11 = (bf16[16,128]{1,0:T(8,128)(2,1)S(1)}, bf16[16,128]{1,0:T(8,128)(2,1)S(1)}, u32[]{:S(2)}, u32[]{:S(2)}) collective-permute-start(bf16[16,128]{1,0:T(8,128)(2,1)S(1)} %get-tuple-element.61), channel_id=1, source_target_pairs={{0,1},{1,0},{2,3},{3,2},{4,5},{5,4},{6,7},{7,6},{8,9},{9,8},{10,11... | collective-permute-start | bytes 12296 | tf_op jit(solution)/shard_map/ppermute | solution.py:805
